TPU v7x, 32 devices: a whole 2x2x4 slice. The times are simulated.
32 devices in a mesh: grp: 2 (over x), comp: 8 (over z, y), lon: 2 (over core).
Axes of the slice: x: 2, y: 2, z: 4, core: 2. Of those that a mesh axis runs over, the one named last changes fastest.
Arguments:
- spectrum: float32 [2304, 48, 256], P(('grp', 'comp'), None, 'lon'), parts along dimension 0, may hold values from 0.05 to 2
- water_depth: float32 [48, 256], P(None, 'lon'), may hold values from 5 to 5000
- sea_mask: int32 [48, 256], P(None, 'lon'), may hold values 0 or 1
- wind_field: float32 [2, 96, 256], P(None, 'grp', 'lon'), parts along dimension 1, may hold values from -8 to 8
- slot_comp: int32 [1152], replicated, may hold values from 0 to 1151, as said below
- substeps: int32 [32], replicated, may hold values from 1 to 4
- coupling: bfloat16 [5, 36, 36], replicated, may hold values from -0.4375 to 0.4375
Outputs:
- spectrum_new: float32 [2304, 48, 256], P(('grp', 'comp'), None, 'lon'), parts along dimension 0
There are 2 independent parts, one for each index of `grp`. A program takes and returns all parts, laid end to end along the dimension named above; an argument that names none is the same for every part. Nothing has to cross between parts.
Inputs may be any that keep to these rules, and one draw needn't show every extreme that they name: A permutation: slot s holds component slot_comp[s], components numbered k = f * 36 + d; slots are ordered by frequency up to a shift: slot_comp[s] // 36 differs from 32 s / 1152 by at most 3.
All inputs are finite; a program needn't handle non-finite values. No bound on the sum of `sea_mask` on one device may be relied on, other than what follows from the above.
Results may differ from a plain program's by a relative error of at most 0.015.
Values may be sent and summed in bfloat16 or wider, within the bound.
A program may use at most 128 MiB of HBM per device.

v0:
```python
import math

import jax
import jax.numpy as jnp
from jax import lax
from jax.sharding import PartitionSpec as P

NDIR = 36
NFREQ = 32


def extended_2(block, sides, width):
    for axis, dim in sides:
        count = lax.axis_size(axis)
        forward = [(i, i + 1) for i in range(count - 1)]
        forward.append((count - 1, 0))
        backward = [(target, source) for source, target in forward]
        low = lax.ppermute(
            lax.slice_in_dim(block, block.shape[dim] - width, None, axis=dim), axis, forward
        )
        high = lax.ppermute(lax.slice_in_dim(block, 0, width, axis=dim), axis, backward)
        block = jnp.concatenate([low, block, high], axis=dim)
    return block


def take_range(values, low_edge, high_edge, dimension):
    return lax.slice_in_dim(values, low_edge, high_edge, axis=dimension)


def advect(quantity, velocity, ocean_rows, dimension):
    extent = quantity.shape[dimension]
    face_speed = 0.5 * (
        take_range(velocity, 1, extent - 2, dimension)
        + take_range(velocity, 2, extent - 1, dimension)
    )
    face_speed = (
        face_speed
        * take_range(ocean_rows, 1, extent - 2, dimension)
        * take_range(ocean_rows, 2, extent - 1, dimension)
    )
    behind = take_range(quantity, 0, extent - 3, dimension)
    before = take_range(quantity, 1, extent - 2, dimension)
    after = take_range(quantity, 2, extent - 1, dimension)
    beyond = take_range(quantity, 3, extent, dimension)
    forward = face_speed >= 0.0
    upwind = jnp.where(forward, before, after)
    downwind = jnp.where(forward, after, before)
    farther = jnp.where(forward, behind, beyond)
    courant = jnp.abs(face_speed)
    face_value = (
        0.5 * (upwind + downwind)
        - 0.5 * courant * (downwind - upwind)
        - (1.0 - courant * courant) / 6.0 * (downwind - 2.0 * upwind + farther)
    )
    fluxes = face_speed * face_value
    return take_range(quantity, 2, extent - 2, dimension) - (
        take_range(fluxes, 1, extent - 3, dimension) - take_range(fluxes, 0, extent - 4, dimension)
    )


def pad_rows(values):
    return jnp.pad(values, ((0, 0), (2, 2), (0, 0)))


def banded(coupling, values):
    accumulated = None
    for offset_index in range(5):
        offset = offset_index - 2
        product = jnp.einsum(
            "ij,fjc->fic", coupling[offset_index], values, preferred_element_type=jnp.float32
        )
        padded = jnp.pad(product, ((2, 2), (0, 0), (0, 0)))
        shifted = padded[2 + offset : 2 + offset + NFREQ]
        accumulated = shifted if accumulated is None else accumulated + shifted
    return accumulated


def sources(natural, weather, coupling):
    frequency = 0.0418 * jnp.power(1.1, jnp.arange(NFREQ, dtype=jnp.int32).astype(jnp.float32))
    freq_scale = jnp.sqrt(frequency / 0.2)
    heading = 2.0 * math.pi * (jnp.arange(NDIR, dtype=jnp.int32).astype(jnp.float32) + 0.5) / NDIR
    projected = (
        jnp.cos(heading)[:, None] * weather[0][None, :]
        + jnp.sin(heading)[:, None] * weather[1][None, :]
    )
    growth_rate = 0.3 * jnp.maximum(0.0, freq_scale[:, None, None] * projected[None] - 1.0)
    energy = natural.astype(jnp.float32)
    square = (energy * energy).astype(jnp.bfloat16)
    linear_part = banded(coupling, natural)
    square_part = banded(coupling, square)
    growth = growth_rate * energy
    transfer = 0.5 * (energy * square_part - energy * energy * linear_part)
    return (0.5 * (growth + transfer)).astype(jnp.bfloat16)


def on_device(spectrum, water_depth, sea_mask, wind_field, slot_comp, substeps, coupling):
    slot_count = spectrum.shape[0]
    lat_rows = spectrum.shape[1]
    strip_width = spectrum.shape[2]
    slots_all = slot_comp.shape[0]
    comp_devices = lax.axis_size("comp")
    comp_place = lax.axis_index("comp")
    own_comps = lax.dynamic_slice_in_dim(slot_comp, comp_place * slot_count, slot_count)
    freq_index = own_comps // NDIR
    dir_index = own_comps % NDIR
    ocean = sea_mask.astype(jnp.float32)
    energy = spectrum * ocean[None]
    margin = 2
    terrain = extended_2(jnp.stack([water_depth, ocean]), (("lon", 2),), margin)
    depth_wide = terrain[0]
    ocean_rows = terrain[1][None]
    frequency = 0.0418 * jnp.power(1.1, freq_index.astype(jnp.float32))
    wavenumber = (2.0 * math.pi * frequency) ** 2 / 9.81
    group_speed = (
        0.8 * jnp.sqrt(jnp.tanh(wavenumber[:, None, None] * depth_wide[None])) * ocean_rows
    )
    heading = 2.0 * math.pi * (dir_index.astype(jnp.float32) + 0.5) / NDIR
    east_speed = group_speed * jnp.cos(heading)[:, None, None]
    north_speed = group_speed * jnp.sin(heading)[:, None, None]
    step_count = jnp.take(substeps, freq_index)
    for substep in range(4):
        extended = extended_2(energy, (("lon", 2),), 2)
        advanced = advect(extended, east_speed, ocean_rows, 2)
        advanced = advect(
            pad_rows(advanced),
            pad_rows(north_speed[:, :, 2:-2]),
            pad_rows(ocean_rows[:, :, 2:-2]),
            1,
        )
        active = (step_count > substep)[:, None, None]
        energy = jnp.where(active, advanced, energy)
    cell_share = lat_rows * strip_width // comp_devices
    flattened = energy.reshape(slot_count, lat_rows * strip_width)
    weather = lax.dynamic_slice_in_dim(
        wind_field.reshape(2, lat_rows * strip_width), comp_place * cell_share, cell_share, axis=1
    )
    inverse = (
        jnp.zeros((slots_all,), jnp.int32).at[slot_comp].set(jnp.arange(slots_all, dtype=jnp.int32))
    )
    gathered = lax.all_to_all(flattened, "comp", split_axis=1, concat_axis=0, tiled=True)
    natural = jnp.take(gathered, inverse, axis=0)
    change = sources(
        natural.astype(jnp.bfloat16).reshape(NFREQ, NDIR, cell_share), weather, coupling
    )
    updated = natural + change.reshape(slots_all, cell_share).astype(jnp.float32)
    home_rows = jnp.take(updated, slot_comp, axis=0)
    result = lax.all_to_all(home_rows, "comp", split_axis=0, concat_axis=1, tiled=True)
    return result.reshape(slot_count, lat_rows, strip_width)


def solution(mesh):
    in_specs = (
        P(("grp", "comp"), None, "lon"),
        P(None, "lon"),
        P(None, "lon"),
        P(None, "grp", "lon"),
        P(),
        P(),
        P(),
    )
    out_specs = P(("grp", "comp"), None, "lon")
    return jax.shard_map(
        on_device, mesh=mesh, in_specs=in_specs, out_specs=out_specs, check_vma=False
    )
```

profile of v0, /device:TPU:0, one launch (start us, length us, event | category | flops | bytes accessed | tf_op | source)
XLA Modules:
  0.0 458.3 jit_solution(14508766065114598997)
XLA Ops:
  2.3 6.7 %copy.33 = f32[144,48,128]{0,1,2:T(8,128)} copy(f32[144,48,128]{2,1,0:T(8,128)} %param.9) | data formatting | bytes 7077888 | tf_op args[0]
  9.0 3.4 broadcast_multiply_fusion.1
  12.4 2.6 copy-done.8
  18.1 4.6 %sqrt_multiply_fusion = (f32[144,48,132]{0,1,2:T(8,128)S(1)}, f32[144,48,132]{0,1,2:T(8,128)}) fusion(f32[48,132]{0,1:T(8,128)S(1)} %copy.35, f32[48,132]{0,1:T(8,128)S(1)} %copy.34, f32[144]{0:T(256)S(1)} %multiply_multiply_fusion, f32[144]{0:T(256)S(1)} %cos.10), kind=kLoop, calls=%fused_computation.48 | loop fusion | flops 2737152 | bytes 7350912 | tf_op jit(solution)/shard_map/mul | solution.py:115
  22.7 3.3 slice_multiply_fusion
  26.3 16.6 %fusion.50 = (f32[144,48,129]{0,1,2:T(8,128)}, f32[144,48,129]{0,1,2:T(8,128)S(1)}) fusion(f32[144,48,2]{0,1,2:T(8,128)S(1)} %collective-permute-done.3, f32[144,48,128]{0,1,2:T(8,128)} %copy-done.8, f32[144,48,2]{0,1,2:T(8,128)S(1)} %collective-permute-done.2, f32[48,129]{0,1:T(8,128)S(1)} %copy.37, f32[48,129]{0,1:T(8,128)S(1)} %copy.36, ...), kind=kLoop, calls=%fused_computation.99 | loop fusion | flops 24074496 | bytes 17965440 | tf_op jit(solution)/shard_map/mul | solution.py:55
  42.9 9.6 %fusion.64 = f32[144,48,128]{0,1,2:T(8,128)} fusion(f32[144,48,129]{0,1,2:T(8,128)} %get-tuple-element.18, f32[144,48,128]{0,1,2:T(8,128)S(1)} %bitcast.94, f32[48,128]{0,1:T(8,128)S(1)} %copy.32), kind=kLoop, calls=%fused_computation.127 | loop fusion | flops 2654208 | bytes 14180352 | tf_op jit(solution)/shard_map/sub | solution.py:56
  52.5 22.6 %fusion.7 = (f32[144,49,128]{0,1,2:T(8,128)}, f32[144,49,128]{0,1,2:T(8,128)}) fusion(f32[144,48,128]{0,1,2:T(8,128)} %fusion.64, f32[49,128]{0,1:T(8,128)S(1)} %copy.39, f32[49,128]{0,1:T(8,128)S(1)} %copy.38, f32[144,48,128]{0,1,2:T(8,128)} %slice_multiply_fusion), kind=kLoop, calls=%fused_computation.29 | loop fusion | flops 20772864 | bytes 14353408 | tf_op jit(solution)/shard_map/mul | solution.py:55
  75.1 7.7 %fusion.63 = f32[144,48,128]{0,1,2:T(8,128)S(1)} fusion(f32[144,48,128]{0,1,2:T(8,128)} %fusion.64, f32[144,49,128]{0,1,2:T(8,128)} %get-tuple-element.14, pred[144]{0:T(512)(128)(4,1)S(1)} %get-tuple-element.42, f32[144,48,128]{0,1,2:T(8,128)S(1)} %bitcast.96, f32[48,128]{0,1:T(8,128)S(1)} %copy.32), kind=kLoop, calls=%fused_computation.124 | loop fusion | flops 3538944 | bytes 17719440 | tf_op jit(solution)/shard_map/jit(_where)/select_n | solution.py:131
  84.7 6.1 %fusion.45 = f32[144,48,129]{0,1,2:T(8,128)} fusion(f32[144,48,129]{0,1,2:T(8,128)S(1)} %get-tuple-element.19, f32[144,48,2]{0,1,2:T(8,128)S(1)} %collective-permute-done.5, f32[144,48,128]{0,1,2:T(8,128)S(1)} %fusion.63, f32[144,48,2]{0,1,2:T(8,128)S(1)} %collective-permute-done.4), kind=kLoop, calls=%fused_computation.92 | loop fusion | flops 21399552 | bytes 10782720 | tf_op jit(solution)/shard_map/mul | solution.py:55
  90.8 8.9 %fusion.61 = f32[144,48,128]{0,1,2:T(8,128)} fusion(f32[144,48,128]{0,1,2:T(8,128)S(1)} %fusion.63, f32[144,48,129]{0,1,2:T(8,128)} %fusion.45), kind=kLoop, calls=%fused_computation.121 | loop fusion | flops 1769472 | bytes 14155776 | tf_op jit(solution)/shard_map/sub | solution.py:56
  99.7 19.4 %fusion.12 = f32[144,49,128]{0,1,2:T(8,128)} fusion(f32[144,49,128]{0,1,2:T(8,128)} %get-tuple-element.15, f32[144,48,128]{0,1,2:T(8,128)} %fusion.61), kind=kLoop, calls=%fused_computation.34 | loop fusion | flops 18063360 | bytes 10764288 | tf_op jit(solution)/shard_map/mul | solution.py:55
  119.1 7.8 %fusion.60 = f32[144,48,128]{0,1,2:T(8,128)S(1)} fusion(f32[144,48,128]{0,1,2:T(8,128)S(1)} %fusion.63, f32[144,48,128]{0,1,2:T(8,128)} %fusion.61, f32[144,49,128]{0,1,2:T(8,128)} %fusion.12, pred[144]{0:T(512)(128)(4,1)S(1)} %get-tuple-element.41), kind=kLoop, calls=%fused_computation.119 | loop fusion | flops 2654208 | bytes 17694864 | tf_op jit(solution)/shard_map/jit(_where)/select_n | solution.py:131
  129.7 6.2 %fusion.40 = f32[144,48,129]{0,1,2:T(8,128)} fusion(f32[144,48,129]{0,1,2:T(8,128)S(1)} %bitcast.90, f32[144,48,2]{0,1,2:T(8,128)S(1)} %collective-permute-done.7, f32[144,48,128]{0,1,2:T(8,128)S(1)} %fusion.60, f32[144,48,2]{0,1,2:T(8,128)S(1)} %collective-permute-done.6), kind=kLoop, calls=%fused_computation.85 | loop fusion | flops 21399552 | bytes 10782720 | tf_op jit(solution)/shard_map/mul | solution.py:55
  135.9 8.7 %fusion.58 = f32[144,48,128]{0,1,2:T(8,128)S(1)} fusion(f32[144,48,128]{0,1,2:T(8,128)} %copy-done.2, f32[144,48,129]{0,1,2:T(8,128)} %fusion.40), kind=kLoop, calls=%fused_computation.116 | loop fusion | flops 1769472 | bytes 14155776 | tf_op jit(solution)/shard_map/sub | solution.py:56
  144.6 13.1 %fusion.17 = f32[144,49,128]{0,1,2:T(8,128)} fusion(f32[144,49,128]{0,1,2:T(8,128)} %get-tuple-element.15, f32[144,48,128]{0,1,2:T(8,128)S(1)} %fusion.58), kind=kLoop, calls=%fused_computation.39 | loop fusion | flops 18063360 | bytes 10764288 | tf_op jit(solution)/shard_map/mul | solution.py:55
  157.7 8.0 %fusion.57 = f32[144,48,128]{0,1,2:T(8,128)S(1)} fusion(f32[144,48,128]{0,1,2:T(8,128)S(1)} %copy-done.3, f32[144,48,128]{0,1,2:T(8,128)} %copy-done.7, f32[144,49,128]{0,1,2:T(8,128)} %fusion.17, pred[144]{0:T(512)(128)(4,1)S(1)} %get-tuple-element.40), kind=kLoop, calls=%fused_computation.114 | loop fusion | flops 2654208 | bytes 17694864 | tf_op jit(solution)/shard_map/jit(_where)/select_n | solution.py:131
  167.3 6.3 %fusion.35 = f32[144,48,129]{0,1,2:T(8,128)} fusion(f32[144,48,129]{0,1,2:T(8,128)S(1)} %bitcast.92, f32[144,48,2]{0,1,2:T(8,128)S(1)} %collective-permute-done.9, f32[144,48,128]{0,1,2:T(8,128)S(1)} %fusion.57, f32[144,48,2]{0,1,2:T(8,128)S(1)} %collective-permute-done.8), kind=kLoop, calls=%fused_computation.78 | loop fusion | flops 21399552 | bytes 10782720 | tf_op jit(solution)/shard_map/mul | solution.py:55
  173.6 8.8 %fusion.55 = f32[144,48,128]{0,1,2:T(8,128)} fusion(f32[144,48,128]{0,1,2:T(8,128)S(1)} %fusion.57, f32[144,48,129]{0,1,2:T(8,128)} %fusion.35), kind=kLoop, calls=%fused_computation.111 | loop fusion | flops 1769472 | bytes 14155776 | tf_op jit(solution)/shard_map/sub | solution.py:56
  182.4 16.2 %fusion.22 = f32[144,49,128]{0,1,2:T(8,128)S(1)} fusion(f32[144,49,128]{0,1,2:T(8,128)} %get-tuple-element.15, f32[144,48,128]{0,1,2:T(8,128)} %fusion.55), kind=kLoop, calls=%fused_computation.44 | loop fusion | flops 18063360 | bytes 10764288 | tf_op jit(solution)/shard_map/mul | solution.py:55
  198.6 4.4 fusion.54
  203.0 5.0 %copy.40 = f32[144,48,128]{2,1,0:T(8,128)S(1)} copy(f32[144,48,128]{0,1,2:T(8,128)} %fusion.54) | data formatting | bytes 7077888 | tf_op jit(solution)/shard_map/jit(_where)/select_n | solution.py:131
  208.0 2.5 all_to_all.26
  210.5 4.9 %copy.41 = f32[144,8,768]{2,0,1:T(8,128)} copy(f32[144,8,768]{2,1,0:T(8,128)} %all_to_all.26) | data formatting | bytes 7077888 | tf_op jit(solution)/shard_map/all_to_all | solution.py:140
  215.4 7.2 %all-to-all-start = ((f32[144,8,768]{2,0,1:T(8,128)}), f32[144,8,768]{2,0,1:T(8,128)S(1)}, u32[]{:S(2)}, u32[]{:S(2)}) async-start(f32[144,8,768]{2,0,1:T(8,128)} %copy.41), calls=%async_computation | async-start | bytes 7077888 | tf_op jit(solution)/shard_map/all_to_all | solution.py:140
  225.2 6.6 %scatter_custom_fusion = s32[1152]{0:T(1024)S(1)} fusion(s32[1152]{0:T(1024)} %compare_select_fusion.2, s32[1152]{0:T(1024)} %iota.17, s32[]{:T(128)} %constant.39.clone.1), kind=kCustom, calls=%fused_computation.216 | custom fusion | bytes 5120 | tf_op jit(solution)/shard_map/scatter | solution.py:138
  236.7 65.4 %all-to-all-done = f32[144,8,768]{2,0,1:T(8,128)S(1)} async-done(((f32[144,8,768]{2,0,1:T(8,128)}), f32[144,8,768]{2,0,1:T(8,128)S(1)}, u32[]{:S(2)}, u32[]{:S(2)}) %all-to-all-start) | async-done | bytes 3538976 | tf_op jit(solution)/shard_map/all_to_all | solution.py:140
  302.0 5.1 %gather_fusion.1 = f32[1152,768]{1,0:T(8,128)} fusion(f32[1152,768]{1,0:T(8,128)S(1)} %bitcast.88, s32[2048]{0:T(1024)} %pad_clamp_fusion.1), kind=kCustom, calls=%fused_computation.clone | custom fusion | bytes 7082496 | tf_op jit(solution)/shard_map/jit(_take)/gather | solution.py:141
  307.2 4.3 multiply_convert_fusion
  311.4 2.4 reshape.143
  313.9 2.7 convolution_bitcast_fusion
  316.5 2.6 convolution_bitcast_fusion.1
  319.1 2.5 convolution_bitcast_fusion.2
  321.7 2.6 convolution_bitcast_fusion.3
  324.3 3.6 convert_element_type.94
  327.9 4.2 convolution_bitcast_fusion.4
  332.1 2.5 convolution_bitcast_fusion.5
  334.6 2.5 convolution_bitcast_fusion.6
  337.2 2.7 convolution_bitcast_fusion.7
  339.8 2.6 fusion.92
  342.8 12.3 %fusion.79 = f32[32,36,768]{2,1,0:T(8,128)} fusion(f32[32,36,768]{2,1,0:T(8,128)S(1)} %copy-done.9, f32[32,36,768]{2,1,0:T(8,128)S(1)} %copy-done.10, bf16[32,36,768]{2,1,0:T(8,128)(2,1)S(1)} %reshape.143, f32[32,36,768]{2,1,0:T(8,128)} %convolution_bitcast_fusion.2, f32[32,36,768]{2,1,0:T(8,128)} %convolution_bitcast_fusion.3, ...), kind=kOutput, calls=%fused_computation.166 | convolution fusion | flops 84049920 | bytes 40241664 | tf_op jit(solution)/shard_map/ij,fjc->fic/dot_general | solution.py:69
  355.1 4.8 %reshape.145 = f32[1152,768]{1,0:T(8,128)} reshape(f32[32,36,768]{2,1,0:T(8,128)} %fusion.79) | data formatting | bytes 7077888 | tf_op jit(solution)/shard_map/convert_element_type | solution.py:145
  359.9 3.5 select_add_fusion
  363.4 4.8 %gather_fusion.2 = f32[1152,768]{1,0:T(8,128)} fusion(f32[1152,768]{1,0:T(8,128)S(1)} %select_add_fusion, s32[2048]{0:T(1024)S(1)} %copy-done.15), kind=kCustom, calls=%fused_computation.1.clone | custom fusion | bytes 7082496 | tf_op jit(solution)/shard_map/jit(_take)/gather | solution.py:146
  368.2 2.3 broadcast_select_fusion
  370.5 83.1 %all_to_all.35 = f32[8,144,768]{2,1,0:T(8,128)S(1)} all-to-all(f32[8,144,768]{2,1,0:T(8,128)S(1)} %bitcast.98), channel_id=1, replica_groups=mesh['grp'=2,'comp'=8,'lon'=2] {'comp'}, dimensions={0} | all-to-all | bytes 7077888 | tf_op jit(solution)/shard_map/all_to_all | solution.py:147
  453.6 2.1 copy.42
  455.7 2.2 reshape.144
  (110 shorter events, 19.5 us)
Async XLA Ops:
  0.0 15.7 %copy-start = (s32[32]{0:T(128)S(1)}, s32[32]{0:T(128)}, u32[]{:S(2)}) copy-start(s32[32]{0:T(128)} %param.14) | copy-start | bytes 388
  1.6 16.1 %collective-permute-start = (f32[2,48,2]{2,1,0:T(8,128)S(1)}, f32[2,48,2]{2,1,0:T(8,128)S(1)}, u32[]{:S(2)}, u32[]{:S(2)}) collective-permute-start(f32[2,48,2]{2,1,0:T(8,128)S(1)} %get-tuple-element.34), channel_id=1, source_target_pairs={{0,1},{1,0},{2,3},{3,2},{4,5},{5,4},{6,7},{7,6},{8,9},{9,8},{10,11... | collective-permute-start | bytes 2312 | tf_op jit(solution)/shard_map/ppermute | solution.py:18
  2.1 15.6 %collective-permute-start.1 = (f32[2,48,2]{2,1,0:T(8,128)S(1)}, f32[2,48,2]{2,1,0:T(8,128)S(1)}, u32[]{:S(2)}, u32[]{:S(2)}) collective-permute-start(f32[2,48,2]{2,1,0:T(8,128)S(1)} %get-tuple-element.35), channel_id=1, source_target_pairs={{1,0},{0,1},{3,2},{2,3},{5,4},{4,5},{7,6},{6,7},{9,8},{8,9},{11,10... | collective-permute-start | bytes 2312 | tf_op jit(solution)/shard_map/ppermute | solution.py:21
  9.0 6.6 %copy-start.14 = (s32[1152]{0:T(1024)S(1)}, s32[1152]{0:T(1024)}, u32[]{:S(2)}) copy-start(s32[1152]{0:T(1024)} %param.13) | copy-start | bytes 13828
  9.0 8.7 %copy-start.12 = (f32[48,128]{1,0:T(8,128)S(1)}, f32[48,128]{1,0:T(8,128)}, u32[]{:S(2)}) copy-start(f32[48,128]{1,0:T(8,128)} %param.10) | copy-start | bytes 73732
  12.4 2.6 copy-start.8
  15.0 11.3 %collective-permute-start.2 = (f32[144,48,2]{0,1,2:T(8,128)S(1)}, f32[144,48,2]{0,1,2:T(8,128)S(1)}, u32[]{:S(2)}, u32[]{:S(2)}) collective-permute-start(f32[144,48,2]{0,1,2:T(8,128)S(1)} %get-tuple-element.26), channel_id=1, source_target_pairs={{0,1},{1,0},{2,3},{3,2},{4,5},{5,4},{6,7},{7,6},{8,9},{9,8},{10,11... | collective-permute-start | bytes 165896 | tf_op jit(solution)/shard_map/ppermute | solution.py:18
  15.5 10.8 %collective-permute-start.3 = (f32[144,48,2]{0,1,2:T(8,128)S(1)}, f32[144,48,2]{0,1,2:T(8,128)S(1)}, u32[]{:S(2)}, u32[]{:S(2)}) collective-permute-start(f32[144,48,2]{0,1,2:T(8,128)S(1)} %get-tuple-element.27), channel_id=1, source_target_pairs={{1,0},{0,1},{3,2},{2,3},{5,4},{4,5},{7,6},{6,7},{9,8},{8,9},{11,10... | collective-permute-start | bytes 165896 | tf_op jit(solution)/shard_map/ppermute | solution.py:21
  22.7 20.2 %slice-start.4 = ((s8[6291456]{0:T(1024)(128)(4,1)}), s8[2097152]{0:T(1024)(128)(4,1)S(1)}, s32[]{:S(2)}) async-start(s8[6291456]{0:T(1024)(128)(4,1)} %bitcast.93), calls=%async_computation.6 | async-start | bytes 4194304
  26.3 16.6 %slice-start.5 = ((s8[6291456]{0:T(1024)(128)(4,1)}), s8[4194304]{0:T(1024)(128)(4,1)S(1)}, s32[]{:S(2)}) async-start(s8[6291456]{0:T(1024)(128)(4,1)} %bitcast.93), calls=%async_computation.7 | async-start | bytes 8388608
  42.9 41.8 %copy-start.4 = (f32[144,48,129]{0,1,2:T(8,128)}, f32[144,48,129]{0,1,2:T(8,128)S(1)}, u32[]{:S(2)}) copy-start(f32[144,48,129]{0,1,2:T(8,128)S(1)} %get-tuple-element.19) | copy-start | bytes 10699780
  42.9 32.2 %slice-start.6 = ((s8[6291456]{0:T(1024)(128)(4,1)}), s8[4194304]{0:T(1024)(128)(4,1)S(1)}, s32[]{:S(2)}) async-start(s8[6291456]{0:T(1024)(128)(4,1)} %bitcast.95), calls=%async_computation.8 | async-start | bytes 8388608
  52.5 22.6 %slice-start.7 = ((s8[6291456]{0:T(1024)(128)(4,1)}), s8[2097152]{0:T(1024)(128)(4,1)S(1)}, s32[]{:S(2)}) async-start(s8[6291456]{0:T(1024)(128)(4,1)} %bitcast.95), calls=%async_computation.9 | async-start | bytes 4194304
  82.9 1.4 collective-permute-start.4
  83.3 1.3 collective-permute-start.5
  99.7 29.9 %slice-start = ((s8[6340608]{0:T(1024)(128)(4,1)}), s8[4194304]{0:T(1024)(128)(4,1)S(1)}, s32[]{:S(2)}) async-start(s8[6340608]{0:T(1024)(128)(4,1)} %bitcast.89), calls=%async_computation.2 | async-start | bytes 8388608
  119.1 10.5 %slice-start.1 = ((s8[6340608]{0:T(1024)(128)(4,1)}), s8[2146304]{0:T(1024)(128)(4,1)S(1)}, s32[]{:S(2)}) async-start(s8[6340608]{0:T(1024)(128)(4,1)} %bitcast.89), calls=%async_computation.3 | async-start | bytes 4292608
  126.9 2.7 copy-start.2
  127.0 1.4 collective-permute-start.6
  127.2 1.3 collective-permute-start.7
  144.5 13.1 %copy-start.7 = (f32[144,48,128]{0,1,2:T(8,128)}, f32[144,48,128]{0,1,2:T(8,128)S(1)}, u32[]{:S(2)}) copy-start(f32[144,48,128]{0,1,2:T(8,128)S(1)} %fusion.58) | copy-start | bytes 10616836
  144.5 13.1 %copy-start.3 = (f32[144,48,128]{0,1,2:T(8,128)S(1)}, f32[144,48,128]{0,1,2:T(8,128)}, u32[]{:S(2)}) copy-start(f32[144,48,128]{0,1,2:T(8,128)} %copy-done.2) | copy-start | bytes 10616836
  144.5 22.7 %slice-start.2 = ((s8[6340608]{0:T(1024)(128)(4,1)}), s8[4194304]{0:T(1024)(128)(4,1)S(1)}, s32[]{:S(2)}) async-start(s8[6340608]{0:T(1024)(128)(4,1)} %bitcast.91), calls=%async_computation.4 | async-start | bytes 8388608
  157.7 9.6 %slice-start.3 = ((s8[6340608]{0:T(1024)(128)(4,1)}), s8[2146304]{0:T(1024)(128)(4,1)S(1)}, s32[]{:S(2)}) async-start(s8[6340608]{0:T(1024)(128)(4,1)} %bitcast.91), calls=%async_computation.5 | async-start | bytes 4292608
  165.7 1.4 collective-permute-start.8
  165.9 1.3 collective-permute-start.9
  182.4 16.2 %copy-start.6 = (f32[144,48,128]{0,1,2:T(8,128)S(1)}, f32[144,48,128]{0,1,2:T(8,128)}, u32[]{:S(2)}) copy-start(f32[144,48,128]{0,1,2:T(8,128)} %fusion.55) | copy-start | bytes 10616836
  215.4 86.6 %all-to-all-start = ((f32[144,8,768]{2,0,1:T(8,128)}), f32[144,8,768]{2,0,1:T(8,128)S(1)}, u32[]{:S(2)}, u32[]{:S(2)}) async-start(f32[144,8,768]{2,0,1:T(8,128)} %copy.41), calls=%async_computation | async-start | bytes 7077888 | tf_op jit(solution)/shard_map/all_to_all | solution.py:140
  307.2 6.7 %copy-start.13 = (bf16[5,36,36]{2,1,0:T(8,128)(2,1)S(1)}, bf16[5,36,36]{2,1,0:T(8,128)(2,1)}, u32[]{:S(2)}) copy-start(bf16[5,36,36]{2,1,0:T(8,128)(2,1)} %param.15) | copy-start | bytes 38884
  327.9 4.2 copy-start.5
  337.1 5.2 %copy-start.9 = (f32[32,36,768]{2,1,0:T(8,128)S(1)}, f32[32,36,768]{2,1,0:T(8,128)}, u32[]{:S(2)}) copy-start(f32[32,36,768]{2,1,0:T(8,128)} %convolution_bitcast_fusion) | copy-start | bytes 10616836
  337.1 5.7 %copy-start.10 = (f32[32,36,768]{2,1,0:T(8,128)S(1)}, f32[32,36,768]{2,1,0:T(8,128)}, u32[]{:S(2)}) copy-start(f32[32,36,768]{2,1,0:T(8,128)} %convolution_bitcast_fusion.1) | copy-start | bytes 10616836
  337.1 5.7 %copy-start.11 = (f32[36,768]{1,0:T(8,128)S(1)}, f32[36,768]{1,0:T(8,128)}, u32[]{:S(2)}) copy-start(f32[36,768]{1,0:T(8,128)} %multiply_add_fusion) | copy-start | bytes 331780
  337.1 5.7 %copy-start.16 = (f32[32]{0:T(128)S(1)}, f32[32]{0:T(128)}, u32[]{:S(2)}) copy-start(f32[32]{0:T(128)} %multiply_sqrt_fusion) | copy-start | bytes 388
  359.9 3.5 copy-start.15
  453.6 4.3 copy-start.1
where the time goes:
time: 467 us; the launch traced here: 458 us
  other arithmetic  198 us (42%)
  blocking collectives  83.1 us (18%)
  waiting for transfers between devices  68.5 us (15%)
  local copies, waits for them, and re-layouts  60.2 us (13%)
  matrix products  37.2 us (8%)
  starting transfers between devices  10 us (2%)
    mul x8, other arithmetic, advect(): fluxes = face_speed * face_value  107 us
    all_to_all x1, blocking collectives, on_device(): lax.all_to_all(home_rows, 'comp', split_axis=0, concat_axis=1, tiled=True)  83.1 us
    all_to_all x1, waiting for transfers between devices, on_device(): lax.all_to_all(flattened, 'comp', split_axis=1, concat_axis=0, tiled=True)  65.4 us
    dot_general x10, matrix products, banded(): jnp.einsum('ij,fjc->fic', coupling[offset_index], values, preferred_eleme...  37.2 us
    sub x4, other arithmetic, advect(): take_range(quantity, 2, extent - 2, dimension)  35.9 us
    select_n x4, other arithmetic, on_device(): energy = jnp.where(active, advanced, energy)  28 us
    unnamed x52, local copies, waits for them, and re-layouts  12.4 us
  transfers between devices with their start and end apart: 11, of which 7 were waited for; matrix products, arithmetic and copies ran while one was open for 8% of the time, Pallas kernels for 0%

commit v1 on v0

v1 whole, which is shorter than its diff:
```python
import functools
import math

import jax
import jax.numpy as jnp
from jax import lax
from jax.experimental import pallas as pl
from jax.experimental.pallas import tpu as pltpu
from jax.sharding import PartitionSpec as P

NDIR = 36
NFREQ = 32
ROUND = 16
ROWS = 2
CHUNKS = 2
REACH = 8
NOWHERE = -100000
VMEM = 48 * 1024 * 1024


def round_up(value, step):
    return (value + step - 1) // step * step


def advect_kernel(
    place, steps, mine, other, depth, ocean, face_x, face_y, params, out_mine, out_other,
    q, r, ax, bx, cx, ay, by, cy
):
    lat = depth.shape[0]
    width = depth.shape[2]
    half = width // 2
    wave = params[0][:, :1][None]
    east = params[1][:, :1][None]
    north = params[2][:, :1][None]
    count = params[3][:, :1][None]
    zeros = jnp.zeros((2, ROUND, width), jnp.float32)
    r[0:2] = zeros
    r[lat + 2 : lat + 4] = zeros
    q[:, :, 0:half] = jnp.swapaxes(mine[...], 0, 1)
    q[:, :, half:width] = jnp.swapaxes(other[...].astype(jnp.float32), 0, 1)

    def prepare(i, carry):
        rows = pl.ds(i * ROWS, ROWS)
        sea = ocean[rows]
        r[pl.ds(i * ROWS + 2, ROWS)] = 0.8 * jnp.sqrt(jnp.tanh(wave * depth[rows])) * sea
        q[rows] = q[rows] * sea
        return carry

    lax.fori_loop(0, lat // ROWS, prepare, 0)

    def weights(c):
        first = 0.5 * c * (1.0 + c)
        return first, 0.5 * c * (1.0 - c), first * (1.0 - c) * (1.0 / 3.0)

    def coefficients(i, carry):
        rows = pl.ds(i * ROWS, ROWS)
        speed = r[pl.ds(i * ROWS + 2, ROWS)]
        above = r[pl.ds(i * ROWS + 3, ROWS)]
        ahead = pltpu.roll(speed, width - 1, 2)
        ax[rows], bx[rows], cx[rows] = weights((speed + ahead) * east * face_x[rows])
        ay[rows], by[rows], cy[rows] = weights((speed + above) * north * face_y[rows])
        return carry

    lax.fori_loop(0, lat // ROWS, coefficients, 0)

    def substep(t, carry):
        def along_x(i, inner):
            rows = pl.ds(i * ROWS, ROWS)
            here = q[rows]
            ahead = pltpu.roll(here, width - 1, 2)
            bend = pltpu.roll(here, 1, 2) + ahead - 2.0 * here
            bend_ahead = pltpu.roll(bend, width - 1, 2)
            third = cx[rows]
            flux = (
                ax[rows] * here
                + bx[rows] * ahead
                - third * jnp.where(third >= 0.0, bend, bend_ahead)
            )
            r[pl.ds(i * ROWS + 2, ROWS)] = here - (flux - pltpu.roll(flux, 1, 2))
            return inner

        lax.fori_loop(0, lat // ROWS, along_x, 0)
        active = count > t.astype(jnp.float32)

        def along_y(i, last):
            rows = pl.ds(i * ROWS, ROWS)
            around = r[pl.ds(i * ROWS + 1, ROWS + 3)]
            bend = around[:-2] + around[2:] - 2.0 * around[1:-1]
            here = around[1:-2]
            third = cy[rows]
            flux = (
                ay[rows] * here
                + by[rows] * around[2:-1]
                - third * jnp.where(third >= 0.0, bend[:-1], bend[1:])
            )
            below = jnp.concatenate([last, flux[:-1]], axis=0)
            q[rows] = jnp.where(active, here - (flux - below), q[rows])
            return flux[-1:]

        lax.fori_loop(0, lat // ROWS, along_y, jnp.zeros((1, ROUND, width), jnp.float32))
        return carry

    lax.fori_loop(0, steps[pl.program_id(0)], substep, 0)
    out_mine[...] = q[:, :, 0:half].astype(jnp.bfloat16)
    out_other[...] = q[:, :, half:width].astype(jnp.bfloat16)


def advance(place, steps, mine, other, depth, ocean, face_x, face_y, params):
    handled, lat, half = other.shape
    whole = pl.BlockSpec((lat, 1, 2 * half), lambda i, place, steps: (0, 0, 0))
    field = pltpu.VMEM((lat, ROUND, 2 * half), jnp.float32)
    out = pl.BlockSpec((lat, ROUND, half), lambda i, place, steps: (0, i, 0))
    shape = jax.ShapeDtypeStruct((lat, handled, half), jnp.bfloat16)
    return pl.pallas_call(
        advect_kernel,
        grid_spec=pltpu.PrefetchScalarGridSpec(
            num_scalar_prefetch=2,
            grid=(handled // ROUND,),
            in_specs=[
                pl.BlockSpec((ROUND, lat, half), lambda i, place, steps: (i + place[0], 0, 0)),
                pl.BlockSpec((ROUND, lat, half), lambda i, place, steps: (i, 0, 0)),
                whole,
                whole,
                whole,
                whole,
                pl.BlockSpec((4, ROUND, half), lambda i, place, steps: (0, i, 0)),
            ],
            out_specs=[out, out],
            scratch_shapes=[
                field,
                pltpu.VMEM((lat + 4, ROUND, 2 * half), jnp.float32),
            ]
            + [field] * 6,
        ),
        out_shape=[shape, shape],
        compiler_params=pltpu.CompilerParams(vmem_limit_bytes=VMEM),
        cost_estimate=pl.CostEstimate(
            flops=120 * handled * lat * half * 2,
            bytes_accessed=10 * handled * lat * half * 2,
            transcendentals=0,
        ),
        name="advance",
    )(place, steps, mine, other, depth, ocean, face_x, face_y, params)


def source_kernel(pieces, matrix, scales, wind, *refs):
    inputs, outputs = refs[:pieces], refs[pieces:]
    slots = inputs[0].shape[1]

    def pair(ref):
        return jnp.concatenate([ref[0], ref[1]], axis=1)

    def twice(ref):
        return jnp.concatenate([ref, ref], axis=1)

    near = jnp.concatenate([pair(ref) for ref in inputs], axis=0)
    wide = near.astype(jnp.float32)
    square = (wide * wide).astype(jnp.bfloat16)
    wind_east = jnp.concatenate([wind[0, 0], wind[0, 1]], axis=1)
    wind_north = jnp.concatenate([wind[1, 0], wind[1, 1]], axis=1)
    half = inputs[0].shape[2]
    for part in range(2):
        rows = slice(part * slots, part * slots + slots)
        linear_part = jnp.dot(matrix[rows, :], near, preferred_element_type=jnp.float32)
        square_part = jnp.dot(matrix[rows, :], square, preferred_element_type=jnp.float32)
        energy = wide[rows]
        push = twice(scales[0, rows]) * wind_east + twice(scales[1, rows]) * wind_north
        rate = 0.3 * jnp.maximum(0.0, push - 1.0)
        transfer = 0.5 * (energy * square_part - energy * energy * linear_part)
        change = (0.5 * (rate * energy + transfer)).astype(jnp.bfloat16)
        outputs[part][0] = change[:, :half]
        outputs[part][1] = change[:, half:]


def sources(matrix, scales, wind, inputs):
    rows, slots, half = inputs[0].shape
    block = pl.BlockSpec((2, slots, half), lambda i: (i, 0, 0))
    shape = jax.ShapeDtypeStruct((rows, slots, half), jnp.bfloat16)
    return pl.pallas_call(
        functools.partial(source_kernel, len(inputs)),
        grid=(rows // 2,),
        in_specs=[
            pl.BlockSpec(matrix.shape, lambda i: (0, 0)),
            pl.BlockSpec(scales.shape, lambda i: (0, 0, 0)),
            pl.BlockSpec((2, 2, 1, half), lambda i: (0, i, 0, 0)),
        ]
        + [block] * len(inputs),
        out_specs=[block, block],
        out_shape=[shape, shape],
        compiler_params=pltpu.CompilerParams(vmem_limit_bytes=VMEM),
        cost_estimate=pl.CostEstimate(
            flops=4 * matrix.size * rows * half,
            bytes_accessed=2 * (len(inputs) + 2) * rows * slots * half,
            transcendentals=0,
        ),
        name="sources",
    )(matrix, scales, wind, *inputs)


def finish_kernel(chunks, place, natural, *refs):
    changes, out = refs[: 2 * chunks], refs[2 * chunks]
    part_rows = natural.shape[0] // 2
    chunk_rows = part_rows // chunks
    for which in range(2):
        part = place[1] if which == 0 else 1 - place[1]
        start = pl.multiple_of(part * part_rows, 8)
        change = jnp.concatenate(
            [changes[which * chunks + chunk][...] for chunk in range(chunks)], axis=0
        ).astype(jnp.float32)
        total = natural[pl.ds(start, part_rows)].astype(jnp.float32) + change
        out[:, pl.ds(start, part_rows), :] = jnp.swapaxes(total, 0, 1)


def finish(place, natural, changes):
    lat, slots, half = natural.shape
    blocks = slots // ROUND
    return pl.pallas_call(
        functools.partial(finish_kernel, len(changes) // 2),
        grid_spec=pltpu.PrefetchScalarGridSpec(
            num_scalar_prefetch=1,
            grid=(blocks,),
            in_specs=[pl.BlockSpec((lat, ROUND, half), lambda i, place: (0, i, 0))]
            + [
                pl.BlockSpec((change.shape[0], ROUND, half), lambda i, place: (0, i, 0))
                for change in changes
            ],
            out_specs=pl.BlockSpec(
                (ROUND, lat, half), lambda i, place: (lax.rem(i + place[0], blocks), 0, 0)
            ),
        ),
        out_shape=jax.ShapeDtypeStruct((slots, lat, half), jnp.float32),
        compiler_params=pltpu.CompilerParams(vmem_limit_bytes=VMEM),
        name="finish",
    )(place, natural, *changes)


def frequency_of(index):
    return 0.0418 * jnp.power(1.1, index.astype(jnp.float32))


def heading_of(index):
    return 2.0 * math.pi * (index.astype(jnp.float32) + 0.5) / NDIR


def over_lanes(values, lanes):
    return jnp.broadcast_to(values[:, None], (values.shape[0], lanes))


def on_device(spectrum, water_depth, sea_mask, wind_field, slot_comp, substeps, coupling):
    slots, lat, half = spectrum.shape
    comp_count = lax.axis_size("comp")
    groups = comp_count // 2
    padded = round_up(slots, ROUND)
    handled = round_up(padded // 2, ROUND)
    rest = padded - handled
    comp_place = lax.axis_index("comp")
    lon_place = lax.axis_index("lon")
    member = comp_place % 2
    group = comp_place // 2
    places = 2 * NFREQ // comp_count
    reach = (REACH + places - 1) // places
    swap = [(0, 1), (1, 0)]
    pairs = [(i, i ^ 1) for i in range(comp_count)]

    comps = jnp.pad(
        slot_comp.reshape(comp_count, slots),
        ((0, 0), (0, padded - slots)),
        constant_values=NOWHERE,
    )
    own_start = lon_place * rest
    order = (jnp.arange(padded, dtype=jnp.int32) + own_start) % padded
    ordered = jnp.take(comps, order, axis=1)
    spread = jnp.pad(ordered, ((2 * reach, 2 * reach), (0, 0)), constant_values=NOWHERE)
    near = []
    offsets = [0]
    for distance in range(1, reach + 1):
        offsets += [-distance, distance]
    for offset in offsets:
        for who in range(2):
            index = (group + offset + reach) * 2 + (member if who == 0 else 1 - member)
            near.append(lax.dynamic_index_in_dim(spread, index, 0, keepdims=False))
    near = jnp.concatenate(near)
    home = near[: 2 * padded]

    padded_spectrum = jnp.pad(spectrum, ((0, padded - slots), (0, 0), (0, 0)))
    sent = lax.dynamic_slice_in_dim(padded_spectrum, rest - own_start, handled, axis=0)
    other = lax.ppermute(sent.astype(jnp.bfloat16), "lon", swap)
    terrain = jnp.stack([water_depth, sea_mask.astype(jnp.float32)])
    terrain = jnp.concatenate([terrain, lax.ppermute(terrain, "lon", swap)], axis=2)
    depth, ocean = terrain[0], terrain[1]
    face_x = 0.5 * ocean * jnp.roll(ocean, -1, axis=1)
    face_y = 0.5 * ocean * jnp.pad(ocean[1:], ((0, 1), (0, 0)))

    held = near[:handled]
    real = held >= 0
    held = jnp.where(real, held, 0)
    held_freq = held // NDIR
    wavenumber = (2.0 * math.pi * frequency_of(held_freq)) ** 2 / 9.81
    heading = heading_of(held % NDIR)
    count = jnp.where(real, jnp.take(substeps, held_freq), 0)
    params = jnp.stack(
        [
            over_lanes(values, half)
            for values in (
                wavenumber,
                jnp.cos(heading),
                jnp.sin(heading),
                count.astype(jnp.float32),
            )
        ]
    )
    most = jnp.max(count.reshape(handled // ROUND, ROUND), axis=1)
    block_place = (own_start // ROUND).astype(jnp.int32)
    mine, foreign = advance(
        block_place[None],
        most,
        padded_spectrum,
        other,
        depth[:, None],
        ocean[:, None],
        face_x[:, None],
        face_y[:, None],
        params,
    )
    returned = lax.ppermute(
        lax.dynamic_slice_in_dim(foreign, lon_place * (handled - rest), rest, axis=1), "lon", swap
    )
    natural = jnp.concatenate([mine, returned], axis=1)

    home_safe = jnp.where(home >= 0, home, 0)
    home_heading = heading_of(home_safe % NDIR)
    home_scale = jnp.sqrt(frequency_of(home_safe // NDIR) / 0.2)
    scales = jnp.stack(
        [
            over_lanes(home_scale * jnp.cos(home_heading), half),
            over_lanes(home_scale * jnp.sin(home_heading), half),
        ]
    )
    directions = jnp.arange(NDIR, dtype=jnp.int32)
    home_dir = (home[:, None] % NDIR == directions[None]).astype(jnp.bfloat16)
    near_dir = (near[:, None] % NDIR == directions[None]).astype(jnp.bfloat16)
    gap = near[None] // NDIR - home[:, None] // NDIR
    matrix = None
    for index in range(5):
        rows = jnp.dot(home_dir, coupling[index], preferred_element_type=jnp.bfloat16)
        term = jnp.dot(rows, near_dir.T, preferred_element_type=jnp.bfloat16)
        term = jnp.where(gap == index - 2, term, jnp.zeros_like(term))
        matrix = term if matrix is None else matrix + term

    part_rows = lat // 2
    chunk_rows = part_rows // CHUNKS
    changes = [[], []]
    for chunk in range(CHUNKS):
        start = member * part_rows + chunk * chunk_rows
        far_start = (1 - member) * part_rows + chunk * chunk_rows
        own = lax.dynamic_slice_in_dim(natural, start, chunk_rows, axis=0)
        far = lax.dynamic_slice_in_dim(natural, far_start, chunk_rows, axis=0)
        paired = lax.ppermute(far, "comp", pairs)
        inputs = [own, paired]
        for distance in range(1, reach + 1):
            step = 2 * distance
            up = [(i, i + step) for i in range(comp_count - step)]
            down = [(i + step, i) for i in range(comp_count - step)]
            for route in (up, down):
                for block in (own, paired):
                    inputs.append(lax.ppermute(block, "comp", route))
        wind = lax.dynamic_slice_in_dim(wind_field, start, chunk_rows, axis=1)[:, :, None]
        kept, sent_back = sources(matrix, scales, wind, inputs)
        changes[0].append(kept)
        changes[1].append(lax.ppermute(sent_back, "comp", pairs))

    out_place = jnp.stack([block_place, member.astype(jnp.int32)])
    return finish(out_place, natural, changes[0] + changes[1])[:slots]


def solution(mesh):
    in_specs = (
        P(("grp", "comp"), None, "lon"),
        P(None, "lon"),
        P(None, "lon"),
        P(None, "grp", "lon"),
        P(),
        P(),
        P(),
    )
    out_specs = P(("grp", "comp"), None, "lon")
    return jax.shard_map(
        on_device, mesh=mesh, in_specs=in_specs, out_specs=out_specs, check_vma=False
    )
```

time: 467 us -> 261 us (0.56); the launches traced: 458 us -> 261 us
  other arithmetic: 198 us -> 0.8 us
  Pallas kernels: 0 us -> 189 us
  blocking collectives: 83.1 us -> 0 us
  local copies, waits for them, and re-layouts: 60.2 us -> 9.12 us
  waiting for transfers between devices: 68.5 us -> 18 us
  matrix products: 37.2 us -> 9.66 us
  starting transfers between devices: 10 us -> 33 us
    pallas_call x0 -> x4, Pallas kernels: none -> 189 us  [the longest x1 174 us: advance(): pl.pallas_call(advect_kernel, grid_spec=pltpu.PrefetchScalarGridSpec(num_...]
    mul x14 -> x3, other arithmetic: 118 us -> 0.22 us  [the longest x1 0.13 us: on_device(): home_scale * jnp.cos(home_heading)]
    all_to_all x1 -> x0, blocking collectives: 83.1 us -> none  [on_device(): lax.all_to_all(home_rows, 'comp', split_axis=0, concat_axis=1, tiled=True)]
    all_to_all x1 -> x0, waiting for transfers between devices: 65.4 us -> none  [on_device(): lax.all_to_all(flattened, 'comp', split_axis=1, concat_axis=0, tiled=True)]
    sub x4 -> x0, other arithmetic: 35.9 us -> none  [advect(): take_range(quantity, 2, extent - 2, dimension)]
    select_n x8 -> x5, other arithmetic: 31 us -> 0.22 us  [the longest x2 0.1 us: on_device(): ordered = jnp.take(comps, order, axis=1)]
    ppermute x10 -> x15, starting transfers between devices: 2.84 us -> 33 us  [the longest x8 25.4 us: on_device(): inputs.append(lax.ppermute(block, 'comp', route))]
    dot_general x10 -> x5, matrix products: 37.2 us -> 9.66 us  [on_device(): term = jnp.dot(rows, near_dir.T, preferred_element_type=jnp.bfloat16)]
  transfers between devices with their start and end apart: 11 -> 15, of which waited for: 7 -> 4; matrix products, arithmetic and copies ran while one was open for 8% -> 6% of each run, Pallas kernels for 0% -> 4%
where the time goes in v1:
time: 261 us
  Pallas kernels  189 us (72%)
  starting transfers between devices  33 us (13%)
  waiting for transfers between devices  18 us (7%)
  matrix products  9.66 us (4%)
  local copies, waits for them, and re-layouts  9.12 us (3%)
    pallas_call x1, Pallas kernels, advance(): pl.pallas_call(advect_kernel, grid_spec=pltpu.PrefetchScalarGridSpec(num_...  174 us
    ppermute x8, starting transfers between devices, on_device(): inputs.append(lax.ppermute(block, 'comp', route))  25.4 us
    pallas_call x2, Pallas kernels, sources(): pl.pallas_call(functools.partial(source_kernel, len(inputs)), grid=(rows...  10.4 us
    dot_general x5, matrix products, on_device(): term = jnp.dot(rows, near_dir.T, preferred_element_type=jnp.bfloat16)  9.66 us
    ppermute x2, waiting for transfers between devices, on_device(): changes[1].append(lax.ppermute(sent_back, 'comp', pairs))  9.09 us
    ppermute x8, waiting for transfers between devices, on_device(): inputs.append(lax.ppermute(block, 'comp', route))  7.07 us
  transfers between devices with their start and end apart: 15, of which 4 were waited for; matrix products, arithmetic and copies ran while one was open for 6% of the time, Pallas kernels for 4%

profile of v1, /device:TPU:0, one launch (start us, length us, event | category | flops | bytes accessed | tf_op | source)
XLA Modules:
  0.0 260.5 jit_solution(18320028792044839707)
XLA Ops:
  0.0 1.7 dynamic-slice_convert_fusion
  1.7 0.5 collective-permute-start
  2.3 0.1 collective-permute-start.1
  2.5 0.1 reshape.405
  2.6 0.1 copy.12
  2.7 0.7 gather_fusion
  3.4 0.1 select_bitcast_fusion
  3.5 0.2 fusion.29
  3.8 1.2 gather_fusion.1
  5.1 0.1 gather.12
  5.4 0.1 stack_broadcast_in_dim.13
  5.5 0.1 fusion.50.steps
  5.8 0.1 maximum_multiply_fusion
  6.2 173.9 %advance.1 = (bf16[48,80,128]{2,1,0:T(8,128)(2,1)S(1)}, bf16[48,80,128]{2,1,0:T(8,128)(2,1)S(1)}) custom-call(s32[1]{0:T(128)} %bitcast.place, s32[5]{0:T(128)S(1)} %fusion.50.steps, f32[144,48,128]{2,1,0:T(8,128)} %mine.1, bf16[80,48,128]{2,1,0:T(8,128)(2,1)S(1)} %collective-permute-done.other, f32[48,1,256]{2,1,0:T(1,128)S(1)} %copy.14.depth, ...), custom_call_target="tpu_custom_call" | custom-call | flops 117964800 | bytes 9830400 | tf_op jit(solution)/shard_map/advance/pallas_call | solution.py:114
  180.1 0.1 constant_dynamic-slice_fusion.6
  180.2 0.5 collective-permute-start.2
  180.7 0.5 dynamic-slice_reduce_fusion
  181.2 0.1 concatenate.77
  181.3 0.1 add_select_fusion.5
  181.5 2.0 convolution_select_fusion.3
  183.5 1.2 constant_dynamic-update-slice_fusion.natural
  184.8 1.0 constant_dynamic-slice_fusion
  185.8 2.6 %collective-permute-start.8 = (bf16[12,144,128]{2,1,0:T(8,128)(2,1)}, bf16[12,144,128]{2,1,0:T(8,128)(2,1)}, u32[]{:S(2)}, u32[]{:S(2)}) collective-permute-start(bf16[12,144,128]{2,1,0:T(8,128)(2,1)} %get-tuple-element.27), channel_id=1, source_target_pairs={{0,2},{2,0},{4,6},{6,4},{8,10},{10,8},{12,14},{14,12},{1,3},{3,1},... | collective-permute-start | bytes 1327112 | tf_op jit(solution)/shard_map/ppermute | solution.py:358
  188.5 1.3 convolution_select_fusion.2
  189.7 1.3 convolution_select_fusion.1
  191.0 1.3 collective-permute-start.11
  192.3 5.3 %collective-permute-start.9 = (bf16[12,144,128]{2,1,0:T(8,128)(2,1)S(1)}, bf16[12,144,128]{2,1,0:T(8,128)(2,1)}, u32[]{:S(2)}, u32[]{:S(2)}) collective-permute-start(bf16[12,144,128]{2,1,0:T(8,128)(2,1)S(1)} %get-tuple-element.28.refs_0_), channel_id=1, source_target_pairs={{0,4},{2,6},{4,8},{6,10},{8,12},{10,14},{1,5},{3,7},{5,9},{7,11},{... | collective-permute-start | bytes 1327112 | tf_op jit(solution)/shard_map/ppermute | solution.py:366
  197.7 1.9 collective-permute-done.8.refs_1_
  199.5 4.3 %collective-permute-start.10 = (bf16[12,144,128]{2,1,0:T(8,128)(2,1)}, bf16[12,144,128]{2,1,0:T(8,128)(2,1)}, u32[]{:S(2)}, u32[]{:S(2)}) collective-permute-start(bf16[12,144,128]{2,1,0:T(8,128)(2,1)} %collective-permute-done.8.refs_1_), channel_id=1, source_target_pairs={{0,4},{2,6},{4,8},{6,10},{8,12},{10,14},{1,5},{3,7},{5,9},{7,11},{... | collective-permute-start | bytes 1327112 | tf_op jit(solution)/shard_map/ppermute | solution.py:366
  203.8 0.1 cosine_multiply_fusion
  203.9 2.8 %fusion.2 = bf16[288,864]{1,0:T(8,128)(2,1)} fusion(bf16[288,864]{1,0:T(8,128)(2,1)} %convolution_select_fusion.1, bf16[288,864]{1,0:T(8,128)(2,1)} %convolution_select_fusion.2, bf16[288,864]{1,0:T(8,128)(2,1)} %convolution_select_fusion.3, s32[288]{0:T(512)S(1)} %copy-done.13, s32[864]{0:T(1024)S(1)} %copy-done.9, s32[864]{0:T(1024)S(1)} %get-tuple-element.36, ...), kind=kOutput, calls=%fused_computation.15 | convolution fusion | flops 21441024 | bytes 2013184 | tf_op jit(solution)/shard_map/dot_general | solution.py:346
  206.7 1.3 collective-permute-start.12
  208.0 0.1 stack_broadcast_in_dim.16
  208.1 0.1 stack_broadcast_in_dim.17
  208.3 5.3 %collective-permute-start.4 = (bf16[12,144,128]{2,1,0:T(8,128)(2,1)S(1)}, bf16[12,144,128]{2,1,0:T(8,128)(2,1)}, u32[]{:S(2)}, u32[]{:S(2)}) collective-permute-start(bf16[12,144,128]{2,1,0:T(8,128)(2,1)S(1)} %get-tuple-element.30.refs_0_), channel_id=1, source_target_pairs={{0,4},{2,6},{4,8},{6,10},{8,12},{10,14},{1,5},{3,7},{5,9},{7,11},{... | collective-permute-start | bytes 1327112 | tf_op jit(solution)/shard_map/ppermute | solution.py:366
  213.6 1.3 collective-permute-start.6
  214.9 5.3 %collective-permute-start.5 = (bf16[12,144,128]{2,1,0:T(8,128)(2,1)S(1)}, bf16[12,144,128]{2,1,0:T(8,128)(2,1)}, u32[]{:S(2)}, u32[]{:S(2)}) collective-permute-start(bf16[12,144,128]{2,1,0:T(8,128)(2,1)S(1)} %collective-permute-done.3.refs_1_), channel_id=1, source_target_pairs={{0,4},{2,6},{4,8},{6,10},{8,12},{10,14},{1,5},{3,7},{5,9},{7,11},{... | collective-permute-start | bytes 1327112 | tf_op jit(solution)/shard_map/ppermute | solution.py:366
  220.2 1.3 collective-permute-start.7
  221.6 2.3 fusion.3.matrix
  223.9 1.0 copy-done.1
  224.9 5.2 %sources.3 = (bf16[12,144,128]{2,1,0:T(8,128)(2,1)S(1)}, bf16[12,144,128]{2,1,0:T(8,128)(2,1)S(1)}) custom-call(bf16[288,864]{1,0:T(8,128)(2,1)S(1)} %copy-done.1, f32[2,288,128]{2,1,0:T(8,128)S(1)} %pad_maximum_fusion.scales, f32[2,12,1,128]{3,2,1,0:T(1,128)S(1)} %broadcast_in_dim.52.wind, bf16[12,144,128]{2,1,0:T(8,128)(2,1)S(1)} %get-tuple-element.28.refs_0_, ...), custom_call_target="tpu_custom_call" | custom-call | flops 1528823808 | bytes 3538944 | tf_op jit(solution)/shard_map/sources/pallas_call | solution.py:179
  230.2 2.3 collective-permute-start.14
  232.5 2.3 collective-permute-done.5.refs_3_
  234.8 4.8 %collective-permute-done.7.refs_5_ = bf16[12,144,128]{2,1,0:T(8,128)(2,1)} collective-permute-done((bf16[12,144,128]{2,1,0:T(8,128)(2,1)S(1)}, bf16[12,144,128]{2,1,0:T(8,128)(2,1)}, u32[]{:S(2)}, u32[]{:S(2)}) %collective-permute-start.7) | collective-permute-done | bytes 442400 | tf_op jit(solution)/shard_map/ppermute | solution.py:366
  239.5 5.1 %sources.2 = (bf16[12,144,128]{2,1,0:T(8,128)(2,1)S(1)}, bf16[12,144,128]{2,1,0:T(8,128)(2,1)S(1)}) custom-call(bf16[288,864]{1,0:T(8,128)(2,1)S(1)} %copy-done.1, f32[2,288,128]{2,1,0:T(8,128)S(1)} %pad_maximum_fusion.scales, f32[2,12,1,128]{3,2,1,0:T(1,128)S(1)} %broadcast_in_dim.51.wind, bf16[12,144,128]{2,1,0:T(8,128)(2,1)S(1)} %get-tuple-element.30.refs_0_, ...), custom_call_target="tpu_custom_call" | custom-call | flops 1528823808 | bytes 3538944 | tf_op jit(solution)/shard_map/sources/pallas_call | solution.py:179
  244.7 1.6 collective-permute-start.13
  246.3 9.1 %collective-permute-done.13.refs_2_ = bf16[12,144,128]{2,1,0:T(8,128)(2,1)S(1)} collective-permute-done((bf16[12,144,128]{2,1,0:T(8,128)(2,1)S(1)}, bf16[12,144,128]{2,1,0:T(8,128)(2,1)S(1)}, u32[]{:S(2)}, u32[]{:S(2)}) %collective-permute-start.13) | collective-permute-done | bytes 442400 | tf_op jit(solution)/shard_map/ppermute | solution.py:370
  255.4 5.1 %finish.1 = f32[144,48,128]{2,1,0:T(8,128)} custom-call(s32[2]{0:T(128)S(1)} %pad_add_fusion.1.place, bf16[48,144,128]{2,1,0:T(8,128)(2,1)S(1)} %constant_dynamic-update-slice_fusion.natural, bf16[12,144,128]{2,1,0:T(8,128)(2,1)S(1)} %get-tuple-element.13.refs_0_, bf16[12,144,128]{2,1,0:T(8,128)(2,1)S(1)} %get-tuple-element.14.refs_1_, ...), custom_call_target="tpu_custom_call" | custom-call | tf_op jit(solution)/shard_map/finish/pallas_call | solution.py:217
  (73 shorter events, 1.1 us)
Async XLA Ops:
  0.0 3.8 %copy-start = (s32[32]{0:T(128)S(1)}, s32[32]{0:T(128)}, u32[]{:S(2)}) copy-start(s32[32]{0:T(128)} %param.12) | copy-start | bytes 388
  0.0 2.3 copy-start.5
  0.0 2.3 copy-start.4
  0.0 2.5 copy-start.7
  1.7 4.4 %collective-permute-start = (bf16[80,48,128]{2,1,0:T(8,128)(2,1)S(1)}, bf16[80,48,128]{2,1,0:T(8,128)(2,1)S(1)}, u32[]{:S(2)}, u32[]{:S(2)}) collective-permute-start(bf16[80,48,128]{2,1,0:T(8,128)(2,1)S(1)} %dynamic-slice_convert_fusion), channel_id=1, source_target_pairs={{0,1},{1,0},{2,3},{3,2},{4,5},{5,4},{6,7},{7,6},{8,9},{9,8},{10,11... | collective-permute-start | bytes 2949128 | tf_op jit(solution)/shard_map/ppermute | solution.py:287
  2.3 3.4 %collective-permute-start.1 = (f32[2,48,128]{2,1,0:T(8,128)S(1)}, f32[2,48,128]{2,1,0:T(8,128)S(1)}, u32[]{:S(2)}, u32[]{:S(2)}) collective-permute-start(f32[2,48,128]{2,1,0:T(8,128)S(1)} %pad_maximum_fusion.3), channel_id=1, source_target_pairs={{0,1},{1,0},{2,3},{3,2},{4,5},{5,4},{6,7},{7,6},{8,9},{9,8},{10,11... | collective-permute-start | bytes 147464 | tf_op jit(solution)/shard_map/ppermute | solution.py:289
  3.4 2.0 copy-start.2
  6.1 174.6 %copy-start.3 = (s32[8,144]{0,1:T(8,128)S(1)}, s32[8,144]{0,1:T(8,128)}, u32[]{:S(2)}) copy-start(s32[8,144]{0,1:T(8,128)} %copy-done.2) | copy-start | bytes 13828
  180.2 3.3 %collective-permute-start.2 = (bf16[48,64,128]{2,1,0:T(8,128)(2,1)S(1)}, bf16[48,64,128]{2,1,0:T(8,128)(2,1)}, u32[]{:S(2)}, u32[]{:S(2)}) collective-permute-start(bf16[48,64,128]{2,1,0:T(8,128)(2,1)S(1)} %constant_dynamic-slice_fusion.6), channel_id=1, source_target_pairs={{0,1},{1,0},{2,3},{3,2},{4,5},{5,4},{6,7},{7,6},{8,9},{9,8},{10,11... | collective-permute-start | bytes 2359304 | tf_op jit(solution)/shard_map/ppermute | solution.py:325
  181.4 2.0 copy-start.10
  181.4 2.0 copy-start.12
  181.4 2.0 copy-start.8
  184.8 3.7 %copy-start.9 = (s32[864]{0:T(1024)S(1)}, s32[864]{0:T(1024)}, u32[]{:S(2)}) copy-start(s32[864]{0:T(1024)} %copy-done.8) | copy-start | bytes 10372
  184.8 3.7 %copy-start.11 = (s32[288]{0:T(512)S(1)}, s32[288]{0:T(512)}, u32[]{:S(2)}) copy-start(s32[288]{0:T(512)} %copy-done.10) | copy-start | bytes 3460
  184.8 3.7 %copy-start.13 = (s32[288]{0:T(512)S(1)}, s32[288]{0:T(512)}, u32[]{:S(2)}) copy-start(s32[288]{0:T(512)} %copy-done.12) | copy-start | bytes 3460
  184.8 3.7 %copy-start.14 = (bf16[5,36,36]{2,1,0:T(8,128)(2,1)S(1)}, bf16[5,36,36]{2,1,0:T(8,128)(2,1)}, u32[]{:S(2)}) copy-start(bf16[5,36,36]{2,1,0:T(8,128)(2,1)} %param.13) | copy-start | bytes 38884
  185.8 13.7 %collective-permute-start.8 = (bf16[12,144,128]{2,1,0:T(8,128)(2,1)}, bf16[12,144,128]{2,1,0:T(8,128)(2,1)}, u32[]{:S(2)}, u32[]{:S(2)}) collective-permute-start(bf16[12,144,128]{2,1,0:T(8,128)(2,1)} %get-tuple-element.27), channel_id=1, source_target_pairs={{0,2},{2,0},{4,6},{6,4},{8,10},{10,8},{12,14},{14,12},{1,3},{3,1},... | collective-permute-start | bytes 1327112 | tf_op jit(solution)/shard_map/ppermute | solution.py:358
  191.0 17.2 %collective-permute-start.11 = (bf16[12,144,128]{2,1,0:T(8,128)(2,1)S(1)}, bf16[12,144,128]{2,1,0:T(8,128)(2,1)}, u32[]{:S(2)}, u32[]{:S(2)}) collective-permute-start(bf16[12,144,128]{2,1,0:T(8,128)(2,1)S(1)} %get-tuple-element.28.refs_0_), channel_id=1, source_target_pairs={{4,0},{6,2},{8,4},{10,6},{12,8},{14,10},{5,1},{7,3},{9,5},{11,7},{... | collective-permute-start | bytes 1327112 | tf_op jit(solution)/shard_map/ppermute | solution.py:366
  192.3 21.3 %collective-permute-start.9 = (bf16[12,144,128]{2,1,0:T(8,128)(2,1)S(1)}, bf16[12,144,128]{2,1,0:T(8,128)(2,1)}, u32[]{:S(2)}, u32[]{:S(2)}) collective-permute-start(bf16[12,144,128]{2,1,0:T(8,128)(2,1)S(1)} %get-tuple-element.28.refs_0_), channel_id=1, source_target_pairs={{0,4},{2,6},{4,8},{6,10},{8,12},{10,14},{1,5},{3,7},{5,9},{7,11},{... | collective-permute-start | bytes 1327112 | tf_op jit(solution)/shard_map/ppermute | solution.py:366
  197.6 17.2 %collective-permute-start.3 = (bf16[12,144,128]{2,1,0:T(8,128)(2,1)}, bf16[12,144,128]{2,1,0:T(8,128)(2,1)S(1)}, u32[]{:S(2)}, u32[]{:S(2)}) collective-permute-start(bf16[12,144,128]{2,1,0:T(8,128)(2,1)} %get-tuple-element.29), channel_id=1, source_target_pairs={{0,2},{2,0},{4,6},{6,4},{8,10},{10,8},{12,14},{14,12},{1,3},{3,1},... | collective-permute-start | bytes 1327112 | tf_op jit(solution)/shard_map/ppermute | solution.py:358
  199.5 20.7 %collective-permute-start.10 = (bf16[12,144,128]{2,1,0:T(8,128)(2,1)}, bf16[12,144,128]{2,1,0:T(8,128)(2,1)}, u32[]{:S(2)}, u32[]{:S(2)}) collective-permute-start(bf16[12,144,128]{2,1,0:T(8,128)(2,1)} %collective-permute-done.8.refs_1_), channel_id=1, source_target_pairs={{0,4},{2,6},{4,8},{6,10},{8,12},{10,14},{1,5},{3,7},{5,9},{7,11},{... | collective-permute-start | bytes 1327112 | tf_op jit(solution)/shard_map/ppermute | solution.py:366
  203.9 17.6 %copy-start.6 = (f32[2,48,128]{2,1,0:T(8,128)S(1)}, f32[2,48,128]{2,1,0:T(8,128)}, u32[]{:S(2)}) copy-start(f32[2,48,128]{2,1,0:T(8,128)} %param.10) | copy-start | bytes 147460
  206.7 17.2 %collective-permute-start.12 = (bf16[12,144,128]{2,1,0:T(8,128)(2,1)}, bf16[12,144,128]{2,1,0:T(8,128)(2,1)}, u32[]{:S(2)}, u32[]{:S(2)}) collective-permute-start(bf16[12,144,128]{2,1,0:T(8,128)(2,1)} %collective-permute-done.8.refs_1_), channel_id=1, source_target_pairs={{4,0},{6,2},{8,4},{10,6},{12,8},{14,10},{5,1},{7,3},{9,5},{11,7},{... | collective-permute-start | bytes 1327112 | tf_op jit(solution)/shard_map/ppermute | solution.py:366
  208.3 24.2 %collective-permute-start.4 = (bf16[12,144,128]{2,1,0:T(8,128)(2,1)S(1)}, bf16[12,144,128]{2,1,0:T(8,128)(2,1)}, u32[]{:S(2)}, u32[]{:S(2)}) collective-permute-start(bf16[12,144,128]{2,1,0:T(8,128)(2,1)S(1)} %get-tuple-element.30.refs_0_), channel_id=1, source_target_pairs={{0,4},{2,6},{4,8},{6,10},{8,12},{10,14},{1,5},{3,7},{5,9},{7,11},{... | collective-permute-start | bytes 1327112 | tf_op jit(solution)/shard_map/ppermute | solution.py:366
  213.6 18.9 %collective-permute-start.6 = (bf16[12,144,128]{2,1,0:T(8,128)(2,1)S(1)}, bf16[12,144,128]{2,1,0:T(8,128)(2,1)}, u32[]{:S(2)}, u32[]{:S(2)}) collective-permute-start(bf16[12,144,128]{2,1,0:T(8,128)(2,1)S(1)} %get-tuple-element.30.refs_0_), channel_id=1, source_target_pairs={{4,0},{6,2},{8,4},{10,6},{12,8},{14,10},{5,1},{7,3},{9,5},{11,7},{... | collective-permute-start | bytes 1327112 | tf_op jit(solution)/shard_map/ppermute | solution.py:366
  214.9 19.9 %collective-permute-start.5 = (bf16[12,144,128]{2,1,0:T(8,128)(2,1)S(1)}, bf16[12,144,128]{2,1,0:T(8,128)(2,1)}, u32[]{:S(2)}, u32[]{:S(2)}) collective-permute-start(bf16[12,144,128]{2,1,0:T(8,128)(2,1)S(1)} %collective-permute-done.3.refs_1_), channel_id=1, source_target_pairs={{0,4},{2,6},{4,8},{6,10},{8,12},{10,14},{1,5},{3,7},{5,9},{7,11},{... | collective-permute-start | bytes 1327112 | tf_op jit(solution)/shard_map/ppermute | solution.py:366
  220.2 19.3 %collective-permute-start.7 = (bf16[12,144,128]{2,1,0:T(8,128)(2,1)S(1)}, bf16[12,144,128]{2,1,0:T(8,128)(2,1)}, u32[]{:S(2)}, u32[]{:S(2)}) collective-permute-start(bf16[12,144,128]{2,1,0:T(8,128)(2,1)S(1)} %collective-permute-done.3.refs_1_), channel_id=1, source_target_pairs={{4,0},{6,2},{8,4},{10,6},{12,8},{14,10},{5,1},{7,3},{9,5},{11,7},{... | collective-permute-start | bytes 1327112 | tf_op jit(solution)/shard_map/ppermute | solution.py:366
  223.9 1.0 copy-start.1
  230.2 16.2 %collective-permute-start.14 = (bf16[12,144,128]{2,1,0:T(8,128)(2,1)S(1)}, bf16[12,144,128]{2,1,0:T(8,128)(2,1)S(1)}, u32[]{:S(2)}, u32[]{:S(2)}) collective-permute-start(bf16[12,144,128]{2,1,0:T(8,128)(2,1)S(1)} %get-tuple-element.16), channel_id=1, source_target_pairs={{0,2},{2,0},{4,6},{6,4},{8,10},{10,8},{12,14},{14,12},{1,3},{3,1},... | collective-permute-start | bytes 1327112 | tf_op jit(solution)/shard_map/ppermute | solution.py:370
  244.7 10.8 %collective-permute-start.13 = (bf16[12,144,128]{2,1,0:T(8,128)(2,1)S(1)}, bf16[12,144,128]{2,1,0:T(8,128)(2,1)S(1)}, u32[]{:S(2)}, u32[]{:S(2)}) collective-permute-start(bf16[12,144,128]{2,1,0:T(8,128)(2,1)S(1)} %get-tuple-element.15), channel_id=1, source_target_pairs={{0,2},{2,0},{4,6},{6,4},{8,10},{10,8},{12,14},{14,12},{1,3},{3,1},... | collective-permute-start | bytes 1327112 | tf_op jit(solution)/shard_map/ppermute | solution.py:370

commit v2 on v1

--- a/solution.py
+++ b/solution.py
@@ -11,7 +11,8 @@
 NDIR = 36
 NFREQ = 32
 ROUND = 16
-ROWS = 2
+UNROLL = 16
+UNROLL_C = 4
 CHUNKS = 2
 REACH = 8
 NOWHERE = -100000
@@ -22,82 +23,100 @@
     return (value + step - 1) // step * step
 
 
+def depth_speed(scaled):
+    value = jnp.tanh(scaled)
+    return 0.8 * value * lax.rsqrt(value)
+
+
+def face_weights(c):
+    forward = c >= 0.0
+    first = 0.5 * c * (1.0 + c)
+    third = first * (1.0 - c) * (1.0 / 3.0)
+    behind = jnp.where(forward, third, 0.0)
+    beyond = third - behind
+    return (
+        -behind,
+        first + 2.0 * behind - beyond,
+        c - first + 2.0 * beyond - behind,
+        -beyond,
+    )
+
+
+def cell_weights(right, left):
+    return (
+        left[0],
+        left[1] - right[0],
+        1.0 - right[1] + left[2],
+        left[3] - right[2],
+        -right[3],
+    )
+
+
 def advect_kernel(
-    place, steps, mine, other, depth, ocean, face_x, face_y, params, out_mine, out_other,
-    q, r, ax, bx, cx, ay, by, cy
+    place, steps, mine, other, depth, ocean, face_x, face_left, face_y, params, out_mine, out_other,
+    q, r, *taps
 ):
     lat = depth.shape[0]
     width = depth.shape[2]
     half = width // 2
-    wave = params[0][:, :1][None]
-    east = params[1][:, :1][None]
-    north = params[2][:, :1][None]
-    count = params[3][:, :1][None]
-    zeros = jnp.zeros((2, ROUND, width), jnp.float32)
-    r[0:2] = zeros
-    r[lat + 2 : lat + 4] = zeros
+    shape = (1, ROUND, width)
+    wave = jnp.broadcast_to(params[0][:, :1][None], shape)
+    east = jnp.broadcast_to(params[1][:, :1][None], shape)
+    north = jnp.broadcast_to(params[2][:, :1][None], shape)
+    count = jnp.broadcast_to(params[3][:, :1][None], shape)
+    taps_x, taps_y = taps[:5], taps[5:]
+    r[0:2] = jnp.zeros((2, ROUND, width), jnp.float32)
+    r[lat + 2 : lat + 4] = jnp.zeros((2, ROUND, width), jnp.float32)
     q[:, :, 0:half] = jnp.swapaxes(mine[...], 0, 1)
     q[:, :, half:width] = jnp.swapaxes(other[...].astype(jnp.float32), 0, 1)
 
     def prepare(i, carry):
-        rows = pl.ds(i * ROWS, ROWS)
-        sea = ocean[rows]
-        r[pl.ds(i * ROWS + 2, ROWS)] = 0.8 * jnp.sqrt(jnp.tanh(wave * depth[rows])) * sea
-        q[rows] = q[rows] * sea
+        row = pl.ds(i, 1)
+        sea = ocean[row]
+        r[pl.ds(i + 2, 1)] = depth_speed(wave * depth[row]) * sea
+        q[row] = q[row] * sea
         return carry
 
-    lax.fori_loop(0, lat // ROWS, prepare, 0)
-
-    def weights(c):
-        first = 0.5 * c * (1.0 + c)
-        return first, 0.5 * c * (1.0 - c), first * (1.0 - c) * (1.0 / 3.0)
-
-    def coefficients(i, carry):
-        rows = pl.ds(i * ROWS, ROWS)
-        speed = r[pl.ds(i * ROWS + 2, ROWS)]
-        above = r[pl.ds(i * ROWS + 3, ROWS)]
-        ahead = pltpu.roll(speed, width - 1, 2)
-        ax[rows], bx[rows], cx[rows] = weights((speed + ahead) * east * face_x[rows])
-        ay[rows], by[rows], cy[rows] = weights((speed + above) * north * face_y[rows])
-        return carry
-
-    lax.fori_loop(0, lat // ROWS, coefficients, 0)
+    lax.fori_loop(0, lat, prepare, 0, unroll=UNROLL)
+
+    def coefficients(i, below):
+        row = pl.ds(i, 1)
+        speed = r[pl.ds(i + 2, 1)]
+        above = r[pl.ds(i + 3, 1)]
+        right = (speed + pltpu.roll(speed, width - 1, 2)) * east * face_x[row]
+        left = (speed + pltpu.roll(speed, 1, 2)) * east * face_left[row]
+        for tap, value in zip(taps_x, cell_weights(face_weights(right), face_weights(left))):
+            tap[row] = value
+        weights = face_weights((speed + above) * north * face_y[row])
+        for tap, value in zip(taps_y, cell_weights(weights, below)):
+            tap[row] = value
+        return weights
+
+    none = jnp.zeros(shape, jnp.float32)
+    lax.fori_loop(0, lat, coefficients, (none,) * 4, unroll=UNROLL_C)
 
     def substep(t, carry):
         def along_x(i, inner):
-            rows = pl.ds(i * ROWS, ROWS)
-            here = q[rows]
-            ahead = pltpu.roll(here, width - 1, 2)
-            bend = pltpu.roll(here, 1, 2) + ahead - 2.0 * here
-            bend_ahead = pltpu.roll(bend, width - 1, 2)
-            third = cx[rows]
-            flux = (
-                ax[rows] * here
-                + bx[rows] * ahead
-                - third * jnp.where(third >= 0.0, bend, bend_ahead)
-            )
-            r[pl.ds(i * ROWS + 2, ROWS)] = here - (flux - pltpu.roll(flux, 1, 2))
+            row = pl.ds(i, 1)
+            here = q[row]
+            total = taps_x[2][row] * here
+            for tap, shift in ((0, 2), (1, 1), (3, width - 1), (4, width - 2)):
+                total = total + taps_x[tap][row] * pltpu.roll(here, shift, 2)
+            r[pl.ds(i + 2, 1)] = total
             return inner
 
-        lax.fori_loop(0, lat // ROWS, along_x, 0)
+        lax.fori_loop(0, lat, along_x, 0, unroll=UNROLL)
         active = count > t.astype(jnp.float32)
 
-        def along_y(i, last):
-            rows = pl.ds(i * ROWS, ROWS)
-            around = r[pl.ds(i * ROWS + 1, ROWS + 3)]
-            bend = around[:-2] + around[2:] - 2.0 * around[1:-1]
-            here = around[1:-2]
-            third = cy[rows]
-            flux = (
-                ay[rows] * here
-                + by[rows] * around[2:-1]
-                - third * jnp.where(third >= 0.0, bend[:-1], bend[1:])
-            )
-            below = jnp.concatenate([last, flux[:-1]], axis=0)
-            q[rows] = jnp.where(active, here - (flux - below), q[rows])
-            return flux[-1:]
-
-        lax.fori_loop(0, lat // ROWS, along_y, jnp.zeros((1, ROUND, width), jnp.float32))
+        def along_y(i, inner):
+            row = pl.ds(i, 1)
+            total = taps_y[0][row] * r[row]
+            for tap in range(1, 5):
+                total = total + taps_y[tap][row] * r[pl.ds(i + tap, 1)]
+            q[row] = jnp.where(active, total, q[row])
+            return inner
+
+        lax.fori_loop(0, lat, along_y, 0, unroll=UNROLL)
         return carry
 
     lax.fori_loop(0, steps[pl.program_id(0)], substep, 0)
@@ -105,7 +124,7 @@
     out_other[...] = q[:, :, half:width].astype(jnp.bfloat16)
 
 
-def advance(place, steps, mine, other, depth, ocean, face_x, face_y, params):
+def advance(place, steps, mine, other, depth, ocean, face_x, face_left, face_y, params):
     handled, lat, half = other.shape
     whole = pl.BlockSpec((lat, 1, 2 * half), lambda i, place, steps: (0, 0, 0))
     field = pltpu.VMEM((lat, ROUND, 2 * half), jnp.float32)
@@ -123,6 +142,7 @@
                 whole,
                 whole,
                 whole,
+                whole,
                 pl.BlockSpec((4, ROUND, half), lambda i, place, steps: (0, i, 0)),
             ],
             out_specs=[out, out],
@@ -130,7 +150,7 @@
                 field,
                 pltpu.VMEM((lat + 4, ROUND, 2 * half), jnp.float32),
             ]
-            + [field] * 6,
+            + [field] * 10,
         ),
         out_shape=[shape, shape],
         compiler_params=pltpu.CompilerParams(vmem_limit_bytes=VMEM),
@@ -140,7 +160,7 @@
             transcendentals=0,
         ),
         name="advance",
-    )(place, steps, mine, other, depth, ocean, face_x, face_y, params)
+    )(place, steps, mine, other, depth, ocean, face_x, face_left, face_y, params)
 
 
 def source_kernel(pieces, matrix, scales, wind, *refs):
@@ -319,6 +339,7 @@
         depth[:, None],
         ocean[:, None],
         face_x[:, None],
+        jnp.roll(face_x, 1, axis=1)[:, None],
         face_y[:, None],
         params,
     )

time: 261 us -> 129 us (0.49)
  Pallas kernels: 189 us -> 56.3 us
    pallas_call x1, Pallas kernels: 174 us -> 40.8 us  [advance(): pl.pallas_call(advect_kernel, grid_spec=pltpu.PrefetchScalarGridSpec(num_...]
  transfers between devices with their start and end apart: 15 -> 15, of which waited for: 4 -> 4; matrix products, arithmetic and copies ran while one was open for 6% -> 13% of each run, Pallas kernels for 4% -> 8%
where the time goes in v2:
time: 129 us; the launch traced here: 128 us
  Pallas kernels  56.3 us (44%)
  starting transfers between devices  32.8 us (25%)
  waiting for transfers between devices  17.1 us (13%)
  matrix products  9.69 us (8%)
  local copies, waits for them, and re-layouts  9.23 us (7%)
  other arithmetic  2.45 us (2%)
    pallas_call x1, Pallas kernels, advance(): pl.pallas_call(advect_kernel, grid_spec=pltpu.PrefetchScalarGridSpec(num_...  40.8 us
    ppermute x8, starting transfers between devices, on_device(): inputs.append(lax.ppermute(block, 'comp', route))  25.1 us
    pallas_call x2, Pallas kernels, sources(): pl.pallas_call(functools.partial(source_kernel, len(inputs)), grid=(rows...  10.4 us
    dot_general x5, matrix products, on_device(): term = jnp.dot(rows, near_dir.T, preferred_element_type=jnp.bfloat16)  9.69 us
    ppermute x2, waiting for transfers between devices, on_device(): changes[1].append(lax.ppermute(sent_back, 'comp', pairs))  8.8 us
    ppermute x8, waiting for transfers between devices, on_device(): inputs.append(lax.ppermute(block, 'comp', route))  6.41 us
    pallas_call x1, Pallas kernels, finish(): pl.pallas_call(functools.partial(finish_kernel, len(changes) // 2), grid_...  5.09 us
    ppermute x2, starting transfers between devices, on_device(): changes[1].append(lax.ppermute(sent_back, 'comp', pairs))  4.03 us
  transfers between devices with their start and end apart: 15, of which 4 were waited for; matrix products, arithmetic and copies ran while one was open for 13% of the time, Pallas kernels for 8%

profile of v2, /device:TPU:0, one launch (start us, length us, event | category | flops | bytes accessed | tf_op | source)
XLA Modules:
  0.0 128.0 jit_solution(17084288630380875928)
XLA Ops:
  0.0 0.8 convert_bitcast_fusion
  0.8 0.7 pad_maximum_fusion.3
  1.5 0.5 collective-permute-start.1
  2.0 1.7 %dynamic-slice_convert_fusion = bf16[80,48,128]{2,1,0:T(8,128)(2,1)S(1)} fusion(f32[144,48,128]{2,1,0:T(8,128)} %mine.1, s32[]{:T(128)S(6)} %select_n.274), kind=kLoop, calls=%fused_computation.7 | loop fusion | bytes 1966084 | tf_op jit(solution)/shard_map/convert_element_type | solution.py:307
  3.6 0.1 collective-permute-start
  3.9 0.1 copy.13
  4.1 0.7 gather_fusion
  4.7 0.1 select_bitcast_fusion
  4.8 0.2 fusion.29
  5.2 1.2 gather_fusion.1
  6.8 0.1 stack_broadcast_in_dim.13
  6.9 0.1 fusion.50.steps
  7.5 0.1 maximum_multiply_fusion
  7.8 40.8 %advance.1 = (bf16[48,80,128]{2,1,0:T(8,128)(2,1)S(1)}, bf16[48,80,128]{2,1,0:T(8,128)(2,1)S(1)}) custom-call(s32[1]{0:T(128)} %bitcast.place, s32[5]{0:T(128)S(1)} %fusion.50.steps, f32[144,48,128]{2,1,0:T(8,128)} %mine.1, bf16[80,48,128]{2,1,0:T(8,128)(2,1)S(1)} %collective-permute-done.other, f32[48,1,256]{2,1,0:T(1,128)S(1)} %copy.15.depth, ...), custom_call_target="tpu_custom_call" | custom-call | flops 117964800 | bytes 9830400 | tf_op jit(solution)/shard_map/advance/pallas_call | solution.py:133
  48.6 0.1 constant_dynamic-slice_fusion.6
  48.7 0.5 collective-permute-start.2
  49.3 0.5 dynamic-slice_reduce_fusion
  49.8 0.1 concatenate.85
  49.9 0.1 add_select_fusion.5
  50.0 2.0 %convolution_select_fusion.3 = bf16[288,864]{1,0:T(8,128)(2,1)} fusion(s32[288]{0:T(512)S(1)} %get-tuple-element.47, s32[864]{0:T(1024)S(1)} %get-tuple-element.43, s32[864]{0:T(1024)S(1)} %get-tuple-element.42, s32[288]{0:T(512)S(1)} %get-tuple-element.46, bf16[5,36,36]{2,1,0:T(8,128)(2,1)} %param.13), kind=kOutput, calls=%fused_computation.11 | convolution fusion | flops 19450368 | bytes 517120 | tf_op jit(solution)/shard_map/dot_general | solution.py:367
  52.1 1.2 constant_dynamic-update-slice_fusion.natural
  53.4 1.1 constant_dynamic-slice_fusion
  54.4 2.6 %collective-permute-start.8 = (bf16[12,144,128]{2,1,0:T(8,128)(2,1)}, bf16[12,144,128]{2,1,0:T(8,128)(2,1)}, u32[]{:S(2)}, u32[]{:S(2)}) collective-permute-start(bf16[12,144,128]{2,1,0:T(8,128)(2,1)} %get-tuple-element.27), channel_id=1, source_target_pairs={{0,2},{2,0},{4,6},{6,4},{8,10},{10,8},{12,14},{14,12},{1,3},{3,1},... | collective-permute-start | bytes 1327112 | tf_op jit(solution)/shard_map/ppermute | solution.py:379
  57.0 1.3 %convolution_select_fusion.2 = bf16[288,864]{1,0:T(8,128)(2,1)} fusion(s32[288]{0:T(512)S(1)} %copy-done.12, s32[864]{0:T(1024)S(1)} %copy-done.8, s32[864]{0:T(1024)S(1)} %get-tuple-element.42, s32[288]{0:T(512)S(1)} %copy-done.10, bf16[5,36,36]{2,1,0:T(8,128)(2,1)S(1)} %copy-done.13), kind=kOutput, calls=%fused_computation.10 | convolution fusion | flops 19450368 | bytes 520192 | tf_op jit(solution)/shard_map/dot_general | solution.py:367
  58.3 1.3 convolution_select_fusion.1
  59.6 1.3 collective-permute-start.11
  60.9 5.3 %collective-permute-start.9 = (bf16[12,144,128]{2,1,0:T(8,128)(2,1)S(1)}, bf16[12,144,128]{2,1,0:T(8,128)(2,1)}, u32[]{:S(2)}, u32[]{:S(2)}) collective-permute-start(bf16[12,144,128]{2,1,0:T(8,128)(2,1)S(1)} %get-tuple-element.28.refs_0_), channel_id=1, source_target_pairs={{0,4},{2,6},{4,8},{6,10},{8,12},{10,14},{1,5},{3,7},{5,9},{7,11},{... | collective-permute-start | bytes 1327112 | tf_op jit(solution)/shard_map/ppermute | solution.py:387
  66.2 1.9 %collective-permute-done.8.refs_1_ = bf16[12,144,128]{2,1,0:T(8,128)(2,1)} collective-permute-done((bf16[12,144,128]{2,1,0:T(8,128)(2,1)}, bf16[12,144,128]{2,1,0:T(8,128)(2,1)}, u32[]{:S(2)}, u32[]{:S(2)}) %collective-permute-start.8) | collective-permute-done | bytes 442400 | tf_op jit(solution)/shard_map/ppermute | solution.py:379
  68.1 4.0 %collective-permute-start.10 = (bf16[12,144,128]{2,1,0:T(8,128)(2,1)}, bf16[12,144,128]{2,1,0:T(8,128)(2,1)}, u32[]{:S(2)}, u32[]{:S(2)}) collective-permute-start(bf16[12,144,128]{2,1,0:T(8,128)(2,1)} %collective-permute-done.8.refs_1_), channel_id=1, source_target_pairs={{0,4},{2,6},{4,8},{6,10},{8,12},{10,14},{1,5},{3,7},{5,9},{7,11},{... | collective-permute-start | bytes 1327112 | tf_op jit(solution)/shard_map/ppermute | solution.py:387
  72.1 0.1 cosine_multiply_fusion
  72.2 2.8 %fusion.2 = bf16[288,864]{1,0:T(8,128)(2,1)} fusion(bf16[288,864]{1,0:T(8,128)(2,1)} %convolution_select_fusion.1, bf16[288,864]{1,0:T(8,128)(2,1)} %convolution_select_fusion.2, bf16[288,864]{1,0:T(8,128)(2,1)} %convolution_select_fusion.3, s32[288]{0:T(512)S(1)} %copy-done.12, s32[864]{0:T(1024)S(1)} %copy-done.8, s32[864]{0:T(1024)S(1)} %get-tuple-element.42, ...), kind=kOutput, calls=%fused_computation.15 | convolution fusion | flops 21441024 | bytes 2013184 | tf_op jit(solution)/shard_map/dot_general | solution.py:367
  75.0 1.3 collective-permute-start.12
  76.3 0.1 stack_broadcast_in_dim.16
  76.4 0.1 stack_broadcast_in_dim.17
  76.6 5.3 %collective-permute-start.4 = (bf16[12,144,128]{2,1,0:T(8,128)(2,1)S(1)}, bf16[12,144,128]{2,1,0:T(8,128)(2,1)}, u32[]{:S(2)}, u32[]{:S(2)}) collective-permute-start(bf16[12,144,128]{2,1,0:T(8,128)(2,1)S(1)} %get-tuple-element.30.refs_0_), channel_id=1, source_target_pairs={{0,4},{2,6},{4,8},{6,10},{8,12},{10,14},{1,5},{3,7},{5,9},{7,11},{... | collective-permute-start | bytes 1327112 | tf_op jit(solution)/shard_map/ppermute | solution.py:387
  81.9 1.3 %collective-permute-start.6 = (bf16[12,144,128]{2,1,0:T(8,128)(2,1)S(1)}, bf16[12,144,128]{2,1,0:T(8,128)(2,1)}, u32[]{:S(2)}, u32[]{:S(2)}) collective-permute-start(bf16[12,144,128]{2,1,0:T(8,128)(2,1)S(1)} %get-tuple-element.30.refs_0_), channel_id=1, source_target_pairs={{4,0},{6,2},{8,4},{10,6},{12,8},{14,10},{5,1},{7,3},{9,5},{11,7},{... | collective-permute-start | bytes 1327112 | tf_op jit(solution)/shard_map/ppermute | solution.py:387
  83.2 5.3 %collective-permute-start.5 = (bf16[12,144,128]{2,1,0:T(8,128)(2,1)S(1)}, bf16[12,144,128]{2,1,0:T(8,128)(2,1)}, u32[]{:S(2)}, u32[]{:S(2)}) collective-permute-start(bf16[12,144,128]{2,1,0:T(8,128)(2,1)S(1)} %collective-permute-done.3.refs_1_), channel_id=1, source_target_pairs={{0,4},{2,6},{4,8},{6,10},{8,12},{10,14},{1,5},{3,7},{5,9},{7,11},{... | collective-permute-start | bytes 1327112 | tf_op jit(solution)/shard_map/ppermute | solution.py:387
  88.5 1.3 %collective-permute-start.7 = (bf16[12,144,128]{2,1,0:T(8,128)(2,1)S(1)}, bf16[12,144,128]{2,1,0:T(8,128)(2,1)}, u32[]{:S(2)}, u32[]{:S(2)}) collective-permute-start(bf16[12,144,128]{2,1,0:T(8,128)(2,1)S(1)} %collective-permute-done.3.refs_1_), channel_id=1, source_target_pairs={{4,0},{6,2},{8,4},{10,6},{12,8},{14,10},{5,1},{7,3},{9,5},{11,7},{... | collective-permute-start | bytes 1327112 | tf_op jit(solution)/shard_map/ppermute | solution.py:387
  89.8 2.3 %fusion.3.matrix = bf16[288,864]{1,0:T(8,128)(2,1)} fusion(bf16[288,864]{1,0:T(8,128)(2,1)} %fusion.2, s32[288]{0:T(512)S(1)} %copy-done.12, s32[864]{0:T(1024)S(1)} %copy-done.8, s32[864]{0:T(1024)S(1)} %get-tuple-element.42, s32[288]{0:T(512)S(1)} %copy-done.10, bf16[5,36,36]{2,1,0:T(8,128)(2,1)S(1)} %copy-done.13), kind=kOutput, calls=%fused_computation.16 | convolution fusion | flops 20445696 | bytes 1017856 | tf_op jit(solution)/shard_map/dot_general | solution.py:367
  92.2 1.0 copy-done.1
  93.2 5.2 %sources.3 = (bf16[12,144,128]{2,1,0:T(8,128)(2,1)S(1)}, bf16[12,144,128]{2,1,0:T(8,128)(2,1)S(1)}) custom-call(bf16[288,864]{1,0:T(8,128)(2,1)S(1)} %copy-done.1, f32[2,288,128]{2,1,0:T(8,128)S(1)} %pad_maximum_fusion.scales, f32[2,12,1,128]{3,2,1,0:T(1,128)S(1)} %broadcast_in_dim.56.wind, bf16[12,144,128]{2,1,0:T(8,128)(2,1)S(1)} %get-tuple-element.28.refs_0_, ...), custom_call_target="tpu_custom_call" | custom-call | flops 1528823808 | bytes 3538944 | tf_op jit(solution)/shard_map/sources/pallas_call | solution.py:199
  98.5 2.5 %collective-permute-start.14 = (bf16[12,144,128]{2,1,0:T(8,128)(2,1)S(1)}, bf16[12,144,128]{2,1,0:T(8,128)(2,1)S(1)}, u32[]{:S(2)}, u32[]{:S(2)}) collective-permute-start(bf16[12,144,128]{2,1,0:T(8,128)(2,1)S(1)} %get-tuple-element.16), channel_id=1, source_target_pairs={{0,2},{2,0},{4,6},{6,4},{8,10},{10,8},{12,14},{14,12},{1,3},{3,1},... | collective-permute-start | bytes 1327112 | tf_op jit(solution)/shard_map/ppermute | solution.py:391
  101.0 2.3 %collective-permute-done.5.refs_3_ = bf16[12,144,128]{2,1,0:T(8,128)(2,1)} collective-permute-done((bf16[12,144,128]{2,1,0:T(8,128)(2,1)S(1)}, bf16[12,144,128]{2,1,0:T(8,128)(2,1)}, u32[]{:S(2)}, u32[]{:S(2)}) %collective-permute-start.5) | collective-permute-done | bytes 442400 | tf_op jit(solution)/shard_map/ppermute | solution.py:387
  103.3 4.1 %collective-permute-done.7.refs_5_ = bf16[12,144,128]{2,1,0:T(8,128)(2,1)} collective-permute-done((bf16[12,144,128]{2,1,0:T(8,128)(2,1)S(1)}, bf16[12,144,128]{2,1,0:T(8,128)(2,1)}, u32[]{:S(2)}, u32[]{:S(2)}) %collective-permute-start.7) | collective-permute-done | bytes 442400 | tf_op jit(solution)/shard_map/ppermute | solution.py:387
  107.4 5.1 %sources.2 = (bf16[12,144,128]{2,1,0:T(8,128)(2,1)S(1)}, bf16[12,144,128]{2,1,0:T(8,128)(2,1)S(1)}) custom-call(bf16[288,864]{1,0:T(8,128)(2,1)S(1)} %copy-done.1, f32[2,288,128]{2,1,0:T(8,128)S(1)} %pad_maximum_fusion.scales, f32[2,12,1,128]{3,2,1,0:T(1,128)S(1)} %broadcast_in_dim.55.wind, bf16[12,144,128]{2,1,0:T(8,128)(2,1)S(1)} %get-tuple-element.30.refs_0_, ...), custom_call_target="tpu_custom_call" | custom-call | flops 1528823808 | bytes 3538944 | tf_op jit(solution)/shard_map/sources/pallas_call | solution.py:199
  112.5 1.5 %collective-permute-start.13 = (bf16[12,144,128]{2,1,0:T(8,128)(2,1)S(1)}, bf16[12,144,128]{2,1,0:T(8,128)(2,1)S(1)}, u32[]{:S(2)}, u32[]{:S(2)}) collective-permute-start(bf16[12,144,128]{2,1,0:T(8,128)(2,1)S(1)} %get-tuple-element.15), channel_id=1, source_target_pairs={{0,2},{2,0},{4,6},{6,4},{8,10},{10,8},{12,14},{14,12},{1,3},{3,1},... | collective-permute-start | bytes 1327112 | tf_op jit(solution)/shard_map/ppermute | solution.py:391
  114.1 8.8 %collective-permute-done.13.refs_2_ = bf16[12,144,128]{2,1,0:T(8,128)(2,1)S(1)} collective-permute-done((bf16[12,144,128]{2,1,0:T(8,128)(2,1)S(1)}, bf16[12,144,128]{2,1,0:T(8,128)(2,1)S(1)}, u32[]{:S(2)}, u32[]{:S(2)}) %collective-permute-start.13) | collective-permute-done | bytes 442400 | tf_op jit(solution)/shard_map/ppermute | solution.py:391
  122.9 5.1 %finish.1 = f32[144,48,128]{2,1,0:T(8,128)} custom-call(s32[2]{0:T(128)S(1)} %pad_add_fusion.1.place, bf16[48,144,128]{2,1,0:T(8,128)(2,1)S(1)} %constant_dynamic-update-slice_fusion.natural, bf16[12,144,128]{2,1,0:T(8,128)(2,1)S(1)} %get-tuple-element.13.refs_0_, bf16[12,144,128]{2,1,0:T(8,128)(2,1)S(1)} %get-tuple-element.14.refs_1_, ...), custom_call_target="tpu_custom_call" | custom-call | tf_op jit(solution)/shard_map/finish/pallas_call | solution.py:237
  (74 shorter events, 1.6 us)
Async XLA Ops:
  0.0 5.2 %copy-start = (s32[32]{0:T(128)S(1)}, s32[32]{0:T(128)}, u32[]{:S(2)}) copy-start(s32[32]{0:T(128)} %param.12) | copy-start | bytes 388
  0.0 3.9 %copy-start.6 = (s32[1152]{0:T(1024)S(1)}, s32[1152]{0:T(1024)}, u32[]{:S(2)}) copy-start(s32[1152]{0:T(1024)} %param.11) | copy-start | bytes 13828
  1.5 5.5 %copy-start.4 = (f32[48,128]{1,0:T(8,128)S(1)}, f32[48,128]{1,0:T(8,128)}, u32[]{:S(2)}) copy-start(f32[48,128]{1,0:T(8,128)} %param.8) | copy-start | bytes 73732
  1.5 5.5 %collective-permute-start.1 = (f32[2,48,128]{2,1,0:T(8,128)S(1)}, f32[2,48,128]{2,1,0:T(8,128)S(1)}, u32[]{:S(2)}, u32[]{:S(2)}) collective-permute-start(f32[2,48,128]{2,1,0:T(8,128)S(1)} %pad_maximum_fusion.3), channel_id=1, source_target_pairs={{0,1},{1,0},{2,3},{3,2},{4,5},{5,4},{6,7},{7,6},{8,9},{9,8},{10,11... | collective-permute-start | bytes 147464 | tf_op jit(solution)/shard_map/ppermute | solution.py:309
  3.6 4.1 %collective-permute-start = (bf16[80,48,128]{2,1,0:T(8,128)(2,1)S(1)}, bf16[80,48,128]{2,1,0:T(8,128)(2,1)S(1)}, u32[]{:S(2)}, u32[]{:S(2)}) collective-permute-start(bf16[80,48,128]{2,1,0:T(8,128)(2,1)S(1)} %dynamic-slice_convert_fusion), channel_id=1, source_target_pairs={{0,1},{1,0},{2,3},{3,2},{4,5},{5,4},{6,7},{7,6},{8,9},{9,8},{10,11... | collective-permute-start | bytes 2949128 | tf_op jit(solution)/shard_map/ppermute | solution.py:307
  4.8 2.0 %copy-start.2 = (s32[8,144]{0,1:T(8,128)}, s32[8,144]{0,1:T(8,128)S(1)}, u32[]{:S(2)}) copy-start(s32[8,144]{0,1:T(8,128)S(1)} %select_bitcast_fusion) | copy-start | bytes 13828
  7.8 41.4 %copy-start.3 = (s32[8,144]{0,1:T(8,128)S(1)}, s32[8,144]{0,1:T(8,128)}, u32[]{:S(2)}) copy-start(s32[8,144]{0,1:T(8,128)} %copy-done.2) | copy-start | bytes 13828
  48.7 3.3 %collective-permute-start.2 = (bf16[48,64,128]{2,1,0:T(8,128)(2,1)S(1)}, bf16[48,64,128]{2,1,0:T(8,128)(2,1)}, u32[]{:S(2)}, u32[]{:S(2)}) collective-permute-start(bf16[48,64,128]{2,1,0:T(8,128)(2,1)S(1)} %constant_dynamic-slice_fusion.6), channel_id=1, source_target_pairs={{0,1},{1,0},{2,3},{3,2},{4,5},{5,4},{6,7},{7,6},{8,9},{9,8},{10,11... | collective-permute-start | bytes 2359304 | tf_op jit(solution)/shard_map/ppermute | solution.py:346
  50.0 2.0 %copy-start.9 = (s32[288]{0:T(512)}, s32[288]{0:T(512)S(1)}, u32[]{:S(2)}) copy-start(s32[288]{0:T(512)S(1)} %get-tuple-element.46) | copy-start | bytes 3460
  50.0 2.0 %copy-start.11 = (s32[288]{0:T(512)}, s32[288]{0:T(512)S(1)}, u32[]{:S(2)}) copy-start(s32[288]{0:T(512)S(1)} %get-tuple-element.47) | copy-start | bytes 3460
  50.0 2.0 %copy-start.7 = (s32[864]{0:T(1024)}, s32[864]{0:T(1024)S(1)}, u32[]{:S(2)}) copy-start(s32[864]{0:T(1024)S(1)} %get-tuple-element.43) | copy-start | bytes 10372
  53.3 3.7 %copy-start.8 = (s32[864]{0:T(1024)S(1)}, s32[864]{0:T(1024)}, u32[]{:S(2)}) copy-start(s32[864]{0:T(1024)} %copy-done.7) | copy-start | bytes 10372
  53.3 3.7 %copy-start.10 = (s32[288]{0:T(512)S(1)}, s32[288]{0:T(512)}, u32[]{:S(2)}) copy-start(s32[288]{0:T(512)} %copy-done.9) | copy-start | bytes 3460
  53.3 3.7 %copy-start.12 = (s32[288]{0:T(512)S(1)}, s32[288]{0:T(512)}, u32[]{:S(2)}) copy-start(s32[288]{0:T(512)} %copy-done.11) | copy-start | bytes 3460
  53.3 3.7 %copy-start.13 = (bf16[5,36,36]{2,1,0:T(8,128)(2,1)S(1)}, bf16[5,36,36]{2,1,0:T(8,128)(2,1)}, u32[]{:S(2)}) copy-start(bf16[5,36,36]{2,1,0:T(8,128)(2,1)} %param.13) | copy-start | bytes 38884
  54.4 13.7 %collective-permute-start.8 = (bf16[12,144,128]{2,1,0:T(8,128)(2,1)}, bf16[12,144,128]{2,1,0:T(8,128)(2,1)}, u32[]{:S(2)}, u32[]{:S(2)}) collective-permute-start(bf16[12,144,128]{2,1,0:T(8,128)(2,1)} %get-tuple-element.27), channel_id=1, source_target_pairs={{0,2},{2,0},{4,6},{6,4},{8,10},{10,8},{12,14},{14,12},{1,3},{3,1},... | collective-permute-start | bytes 1327112 | tf_op jit(solution)/shard_map/ppermute | solution.py:379
  59.6 17.0 %collective-permute-start.11 = (bf16[12,144,128]{2,1,0:T(8,128)(2,1)S(1)}, bf16[12,144,128]{2,1,0:T(8,128)(2,1)}, u32[]{:S(2)}, u32[]{:S(2)}) collective-permute-start(bf16[12,144,128]{2,1,0:T(8,128)(2,1)S(1)} %get-tuple-element.28.refs_0_), channel_id=1, source_target_pairs={{4,0},{6,2},{8,4},{10,6},{12,8},{14,10},{5,1},{7,3},{9,5},{11,7},{... | collective-permute-start | bytes 1327112 | tf_op jit(solution)/shard_map/ppermute | solution.py:387
  60.9 21.0 %collective-permute-start.9 = (bf16[12,144,128]{2,1,0:T(8,128)(2,1)S(1)}, bf16[12,144,128]{2,1,0:T(8,128)(2,1)}, u32[]{:S(2)}, u32[]{:S(2)}) collective-permute-start(bf16[12,144,128]{2,1,0:T(8,128)(2,1)S(1)} %get-tuple-element.28.refs_0_), channel_id=1, source_target_pairs={{0,4},{2,6},{4,8},{6,10},{8,12},{10,14},{1,5},{3,7},{5,9},{7,11},{... | collective-permute-start | bytes 1327112 | tf_op jit(solution)/shard_map/ppermute | solution.py:387
  66.2 17.0 %collective-permute-start.3 = (bf16[12,144,128]{2,1,0:T(8,128)(2,1)}, bf16[12,144,128]{2,1,0:T(8,128)(2,1)S(1)}, u32[]{:S(2)}, u32[]{:S(2)}) collective-permute-start(bf16[12,144,128]{2,1,0:T(8,128)(2,1)} %get-tuple-element.29), channel_id=1, source_target_pairs={{0,2},{2,0},{4,6},{6,4},{8,10},{10,8},{12,14},{14,12},{1,3},{3,1},... | collective-permute-start | bytes 1327112 | tf_op jit(solution)/shard_map/ppermute | solution.py:379
  68.1 20.4 %collective-permute-start.10 = (bf16[12,144,128]{2,1,0:T(8,128)(2,1)}, bf16[12,144,128]{2,1,0:T(8,128)(2,1)}, u32[]{:S(2)}, u32[]{:S(2)}) collective-permute-start(bf16[12,144,128]{2,1,0:T(8,128)(2,1)} %collective-permute-done.8.refs_1_), channel_id=1, source_target_pairs={{0,4},{2,6},{4,8},{6,10},{8,12},{10,14},{1,5},{3,7},{5,9},{7,11},{... | collective-permute-start | bytes 1327112 | tf_op jit(solution)/shard_map/ppermute | solution.py:387
  72.2 17.6 %copy-start.5 = (f32[2,48,128]{2,1,0:T(8,128)S(1)}, f32[2,48,128]{2,1,0:T(8,128)}, u32[]{:S(2)}) copy-start(f32[2,48,128]{2,1,0:T(8,128)} %param.10) | copy-start | bytes 147460
  75.0 17.2 %collective-permute-start.12 = (bf16[12,144,128]{2,1,0:T(8,128)(2,1)}, bf16[12,144,128]{2,1,0:T(8,128)(2,1)}, u32[]{:S(2)}, u32[]{:S(2)}) collective-permute-start(bf16[12,144,128]{2,1,0:T(8,128)(2,1)} %collective-permute-done.8.refs_1_), channel_id=1, source_target_pairs={{4,0},{6,2},{8,4},{10,6},{12,8},{14,10},{5,1},{7,3},{9,5},{11,7},{... | collective-permute-start | bytes 1327112 | tf_op jit(solution)/shard_map/ppermute | solution.py:387
  76.6 24.5 %collective-permute-start.4 = (bf16[12,144,128]{2,1,0:T(8,128)(2,1)S(1)}, bf16[12,144,128]{2,1,0:T(8,128)(2,1)}, u32[]{:S(2)}, u32[]{:S(2)}) collective-permute-start(bf16[12,144,128]{2,1,0:T(8,128)(2,1)S(1)} %get-tuple-element.30.refs_0_), channel_id=1, source_target_pairs={{0,4},{2,6},{4,8},{6,10},{8,12},{10,14},{1,5},{3,7},{5,9},{7,11},{... | collective-permute-start | bytes 1327112 | tf_op jit(solution)/shard_map/ppermute | solution.py:387
  81.9 19.1 %collective-permute-start.6 = (bf16[12,144,128]{2,1,0:T(8,128)(2,1)S(1)}, bf16[12,144,128]{2,1,0:T(8,128)(2,1)}, u32[]{:S(2)}, u32[]{:S(2)}) collective-permute-start(bf16[12,144,128]{2,1,0:T(8,128)(2,1)S(1)} %get-tuple-element.30.refs_0_), channel_id=1, source_target_pairs={{4,0},{6,2},{8,4},{10,6},{12,8},{14,10},{5,1},{7,3},{9,5},{11,7},{... | collective-permute-start | bytes 1327112 | tf_op jit(solution)/shard_map/ppermute | solution.py:387
  83.2 20.2 %collective-permute-start.5 = (bf16[12,144,128]{2,1,0:T(8,128)(2,1)S(1)}, bf16[12,144,128]{2,1,0:T(8,128)(2,1)}, u32[]{:S(2)}, u32[]{:S(2)}) collective-permute-start(bf16[12,144,128]{2,1,0:T(8,128)(2,1)S(1)} %collective-permute-done.3.refs_1_), channel_id=1, source_target_pairs={{0,4},{2,6},{4,8},{6,10},{8,12},{10,14},{1,5},{3,7},{5,9},{7,11},{... | collective-permute-start | bytes 1327112 | tf_op jit(solution)/shard_map/ppermute | solution.py:387
  88.5 18.9 %collective-permute-start.7 = (bf16[12,144,128]{2,1,0:T(8,128)(2,1)S(1)}, bf16[12,144,128]{2,1,0:T(8,128)(2,1)}, u32[]{:S(2)}, u32[]{:S(2)}) collective-permute-start(bf16[12,144,128]{2,1,0:T(8,128)(2,1)S(1)} %collective-permute-done.3.refs_1_), channel_id=1, source_target_pairs={{4,0},{6,2},{8,4},{10,6},{12,8},{14,10},{5,1},{7,3},{9,5},{11,7},{... | collective-permute-start | bytes 1327112 | tf_op jit(solution)/shard_map/ppermute | solution.py:387
  92.2 1.0 copy-start.1
  98.5 15.6 %collective-permute-start.14 = (bf16[12,144,128]{2,1,0:T(8,128)(2,1)S(1)}, bf16[12,144,128]{2,1,0:T(8,128)(2,1)S(1)}, u32[]{:S(2)}, u32[]{:S(2)}) collective-permute-start(bf16[12,144,128]{2,1,0:T(8,128)(2,1)S(1)} %get-tuple-element.16), channel_id=1, source_target_pairs={{0,2},{2,0},{4,6},{6,4},{8,10},{10,8},{12,14},{14,12},{1,3},{3,1},... | collective-permute-start | bytes 1327112 | tf_op jit(solution)/shard_map/ppermute | solution.py:391
  112.5 10.4 %collective-permute-start.13 = (bf16[12,144,128]{2,1,0:T(8,128)(2,1)S(1)}, bf16[12,144,128]{2,1,0:T(8,128)(2,1)S(1)}, u32[]{:S(2)}, u32[]{:S(2)}) collective-permute-start(bf16[12,144,128]{2,1,0:T(8,128)(2,1)S(1)} %get-tuple-element.15), channel_id=1, source_target_pairs={{0,2},{2,0},{4,6},{6,4},{8,10},{10,8},{12,14},{14,12},{1,3},{3,1},... | collective-permute-start | bytes 1327112 | tf_op jit(solution)/shard_map/ppermute | solution.py:391

commit v3 on v2

v3 whole, which is shorter than its diff:
```python
import functools
import math

import jax
import jax.numpy as jnp
from jax import lax
from jax.experimental import pallas as pl
from jax.experimental.pallas import tpu as pltpu
from jax.sharding import PartitionSpec as P

NDIR = 36
NFREQ = 32
ROUND = 16
UNROLL = 16
UNROLL_C = 4
CHUNKS = 3
REACH = 8
NOWHERE = -100000
VMEM = 48 * 1024 * 1024


def round_up(value, step):
    return (value + step - 1) // step * step


def depth_speed(scaled):
    value = jnp.tanh(scaled)
    return 0.8 * value * lax.rsqrt(value)


def face_weights(c):
    forward = c >= 0.0
    first = 0.5 * c * (1.0 + c)
    third = first * (1.0 - c) * (1.0 / 3.0)
    behind = jnp.where(forward, third, 0.0)
    beyond = third - behind
    return (
        -behind,
        first + 2.0 * behind - beyond,
        c - first + 2.0 * beyond - behind,
        -beyond,
    )


def cell_weights(right, left):
    return (
        left[0],
        left[1] - right[0],
        1.0 - right[1] + left[2],
        left[3] - right[2],
        -right[3],
    )


def advect_kernel(
    table, steps, mine, other, depth, ocean, face_x, face_left, face_y, params,
    keep, over_lon, over_pair, over_both, q, r, *taps
):
    lat = depth.shape[0]
    width = depth.shape[2]
    half = width // 2
    shape = (1, ROUND, width)
    wave = jnp.broadcast_to(params[0][:, :1][None], shape)
    east = jnp.broadcast_to(params[1][:, :1][None], shape)
    north = jnp.broadcast_to(params[2][:, :1][None], shape)
    count = jnp.broadcast_to(params[3][:, :1][None], shape)
    taps_x, taps_y = taps[:5], taps[5:]
    r[0:2] = jnp.zeros((2, ROUND, width), jnp.float32)
    r[lat + 2 : lat + 4] = jnp.zeros((2, ROUND, width), jnp.float32)
    q[:, :, 0:half] = jnp.swapaxes(mine[...], 0, 1)
    q[:, :, half:width] = jnp.swapaxes(other[...].astype(jnp.float32), 0, 1)

    def prepare(i, carry):
        row = pl.ds(i, 1)
        sea = ocean[row]
        r[pl.ds(i + 2, 1)] = depth_speed(wave * depth[row]) * sea
        q[row] = q[row] * sea
        return carry

    lax.fori_loop(0, lat, prepare, 0, unroll=UNROLL)

    def coefficients(i, below):
        row = pl.ds(i, 1)
        speed = r[pl.ds(i + 2, 1)]
        above = r[pl.ds(i + 3, 1)]
        right = (speed + pltpu.roll(speed, width - 1, 2)) * east * face_x[row]
        left = (speed + pltpu.roll(speed, 1, 2)) * east * face_left[row]
        for tap, value in zip(taps_x, cell_weights(face_weights(right), face_weights(left))):
            tap[row] = value
        weights = face_weights((speed + above) * north * face_y[row])
        for tap, value in zip(taps_y, cell_weights(weights, below)):
            tap[row] = value
        return weights

    none = jnp.zeros(shape, jnp.float32)
    lax.fori_loop(0, lat, coefficients, (none,) * 4, unroll=UNROLL_C)

    def substep(t, carry):
        def along_x(i, inner):
            row = pl.ds(i, 1)
            here = q[row]
            total = taps_x[2][row] * here
            for tap, shift in ((0, 2), (1, 1), (3, width - 1), (4, width - 2)):
                total = total + taps_x[tap][row] * pltpu.roll(here, shift, 2)
            r[pl.ds(i + 2, 1)] = total
            return inner

        lax.fori_loop(0, lat, along_x, 0, unroll=UNROLL)
        active = count > t.astype(jnp.float32)

        def along_y(i, inner):
            row = pl.ds(i, 1)
            total = taps_y[0][row] * r[row]
            for tap in range(1, 5):
                total = total + taps_y[tap][row] * r[pl.ds(i + tap, 1)]
            q[row] = jnp.where(active, total, q[row])
            return inner

        lax.fori_loop(0, lat, along_y, 0, unroll=UNROLL)
        return carry

    lax.fori_loop(0, steps[0], substep, 0)
    part_rows = lat // 2
    here = pl.ds(table[1] * part_rows, part_rows)
    there = pl.ds((1 - table[1]) * part_rows, part_rows)
    keep[...] = q[here, :, 0:half].astype(jnp.bfloat16)
    over_lon[...] = q[here, :, half:width].astype(jnp.bfloat16)
    over_pair[...] = q[there, :, 0:half].astype(jnp.bfloat16)
    over_both[...] = q[there, :, half:width].astype(jnp.bfloat16)


def advance(table, steps, mine, other, block, fields, params):
    _, lat, half = other.shape
    whole = pl.BlockSpec((lat, 1, 2 * half), lambda i, table, steps: (0, 0, 0))
    field = pltpu.VMEM((lat, ROUND, 2 * half), jnp.float32)
    out = pl.BlockSpec((lat // 2, ROUND, half), lambda i, table, steps: (0, 0, 0))
    shape = jax.ShapeDtypeStruct((lat // 2, ROUND, half), jnp.bfloat16)
    return pl.pallas_call(
        advect_kernel,
        grid_spec=pltpu.PrefetchScalarGridSpec(
            num_scalar_prefetch=2,
            grid=(1,),
            in_specs=[
                pl.BlockSpec((ROUND, lat, half), lambda i, table, steps: (table[0], 0, 0)),
                pl.BlockSpec((ROUND, lat, half), lambda i, table, steps: (block, 0, 0)),
            ]
            + [whole] * len(fields)
            + [pl.BlockSpec(params.shape, lambda i, table, steps: (0, 0, 0))],
            out_specs=[out] * 4,
            scratch_shapes=[
                field,
                pltpu.VMEM((lat + 4, ROUND, 2 * half), jnp.float32),
            ]
            + [field] * 10,
        ),
        out_shape=[shape] * 4,
        compiler_params=pltpu.CompilerParams(vmem_limit_bytes=VMEM),
        cost_estimate=pl.CostEstimate(
            flops=60000 * ROUND * lat * half // 8,
            bytes_accessed=10 * ROUND * lat * half,
            transcendentals=0,
        ),
        name="advance",
    )(table, steps, mine, other, *fields, params)


def source_kernel(spans, matrix, scales, wind, *refs):
    inputs, outputs = refs[: len(spans)], refs[len(spans) :]
    half = inputs[0].shape[2]
    slots = outputs[0].shape[1]

    def pair(ref):
        return jnp.concatenate([ref[0], ref[1]], axis=1)

    def twice(value):
        return jnp.concatenate([value, value], axis=1)

    near = jnp.concatenate([pair(ref) for ref in inputs], axis=0)
    wide = near.astype(jnp.float32)
    square = (wide * wide).astype(jnp.bfloat16)
    wind_east = jnp.concatenate([wind[0, 0], wind[0, 1]], axis=1)
    wind_north = jnp.concatenate([wind[1, 0], wind[1, 1]], axis=1)
    for part in (1, 0):
        rows = slice(part * slots, part * slots + slots)
        linear_part = jnp.dot(matrix[rows, :], near, preferred_element_type=jnp.float32)
        square_part = jnp.dot(matrix[rows, :], square, preferred_element_type=jnp.float32)
        energy = []
        start = 0
        for size, is_home in spans:
            if is_home:
                first = start + part * (size // 2)
                energy.append(wide[first : first + size // 2])
            start += size
        energy = jnp.concatenate(energy, axis=0)
        push = twice(scales[0, rows]) * wind_east + twice(scales[1, rows]) * wind_north
        rate = 0.3 * jnp.maximum(0.0, push - 1.0)
        transfer = 0.5 * (energy * square_part - energy * energy * linear_part)
        change = (0.5 * (rate * energy + transfer)).astype(jnp.bfloat16)
        total = (energy + change.astype(jnp.float32)).astype(jnp.bfloat16)
        outputs[part][0] = total[:, :half]
        outputs[part][1] = total[:, half:]


def sources(matrix, scales, wind, inputs, homes, first, rows):
    half = inputs[0].shape[2]
    slots = matrix.shape[0] // 2
    base = first // 2
    spans = tuple((block.shape[1], home) for block, home in zip(inputs, homes))
    out = pl.BlockSpec((2, slots, half), lambda i: (i, 0, 0))
    shape = jax.ShapeDtypeStruct((rows, slots, half), jnp.bfloat16)
    return pl.pallas_call(
        functools.partial(source_kernel, spans),
        grid=(rows // 2,),
        in_specs=[
            pl.BlockSpec(matrix.shape, lambda i: (0, 0)),
            pl.BlockSpec(scales.shape, lambda i: (0, 0, 0)),
            pl.BlockSpec((2, 2, 1, half), lambda i: (0, i + base, 0, 0)),
        ]
        + [pl.BlockSpec((2, size, half), lambda i: (i + base, 0, 0)) for size, _ in spans],
        out_specs=[out, out],
        out_shape=[shape, shape],
        compiler_params=pltpu.CompilerParams(vmem_limit_bytes=VMEM),
        cost_estimate=pl.CostEstimate(
            flops=16 * matrix.size * rows * half,
            bytes_accessed=2 * (matrix.shape[1] + 2 * slots) * rows * half,
            transcendentals=0,
        ),
        name="sources",
    )(matrix, scales, wind, *inputs)


def finish_kernel(chunks, table, *refs):
    values, out = refs[: 2 * chunks], refs[2 * chunks]
    part_rows = out.shape[1] // 2
    member = table[table.shape[0] - 1]
    for which in range(2):
        part = member if which == 0 else 1 - member
        start = pl.multiple_of(part * part_rows, 8)
        total = jnp.concatenate(
            [values[which * chunks + chunk][...] for chunk in range(chunks)], axis=0
        ).astype(jnp.float32)
        out[:, pl.ds(start, part_rows), :] = jnp.swapaxes(total, 0, 1)


def finish(table, values, lat):
    _, slots, half = values[0].shape
    return pl.pallas_call(
        functools.partial(finish_kernel, len(values) // 2),
        grid_spec=pltpu.PrefetchScalarGridSpec(
            num_scalar_prefetch=1,
            grid=(slots // ROUND,),
            in_specs=[
                pl.BlockSpec((value.shape[0], ROUND, half), lambda i, table: (0, i, 0))
                for value in values
            ],
            out_specs=pl.BlockSpec((ROUND, lat, half), lambda i, table: (table[i], 0, 0)),
        ),
        out_shape=jax.ShapeDtypeStruct((slots, lat, half), jnp.float32),
        compiler_params=pltpu.CompilerParams(vmem_limit_bytes=VMEM),
        name="finish",
    )(table, *values)


def frequency_of(index):
    return 0.0418 * jnp.power(1.1, index.astype(jnp.float32))


def heading_of(index):
    return 2.0 * math.pi * (index.astype(jnp.float32) + 0.5) / NDIR


def over_lanes(values, lanes):
    return jnp.broadcast_to(values[:, None], (values.shape[0], lanes))


def on_device(spectrum, water_depth, sea_mask, wind_field, slot_comp, substeps, coupling):
    slots, lat, half = spectrum.shape
    comp_count = lax.axis_size("comp")
    groups = comp_count // 2
    padded = round_up(slots, ROUND)
    handled = round_up(padded // 2, ROUND)
    rest = padded - handled
    comp_place = lax.axis_index("comp")
    lon_place = lax.axis_index("lon")
    member = comp_place % 2
    group = comp_place // 2
    places = 2 * NFREQ // comp_count
    reach = (REACH + places - 1) // places
    swap = [(0, 1), (1, 0)]
    pairs = [(i, i ^ 1) for i in range(comp_count)]

    blocks, handled_blocks, rest_blocks = padded // ROUND, handled // ROUND, rest // ROUND
    comps = jnp.pad(
        slot_comp.reshape(comp_count, slots),
        ((0, 0), (0, padded - slots)),
        constant_values=NOWHERE,
    ).reshape(comp_count, blocks, ROUND)
    spread = jnp.pad(comps, ((2 * reach, 2 * reach), (0, 0), (0, 0)), constant_values=NOWHERE)
    block_of = [[], []]
    for turn in range(handled_blocks):
        block_of[0].append(turn)
        block_of[1].append(turn + handled_blocks if turn < rest_blocks else turn)
    held_blocks = jnp.where(lon_place == 0, jnp.array(block_of[0]), jnp.array(block_of[1]))
    order = []
    for turn in range(handled_blocks):
        order.append((block_of[0][turn], block_of[1][turn]))
        if turn < rest_blocks:
            order.append((block_of[1][turn], block_of[0][turn]))
    pairs_of = jnp.array(order)
    held_order = jnp.where(lon_place == 0, pairs_of[:, 0], pairs_of[:, 1])
    sizes = [2 if turn < rest_blocks else 1 for turn in range(handled_blocks)]
    offsets = [0]
    for distance in range(1, reach + 1):
        offsets += [-distance, distance]

    def held_by(offset, who):
        index = (group + offset + reach) * 2 + (member if who == 0 else 1 - member)
        return jnp.take(lax.dynamic_index_in_dim(spread, index, 0, keepdims=False), held_order, axis=0)

    held_of = {(offset, who): held_by(offset, who) for offset in offsets for who in range(2)}
    near = []
    start = 0
    for size in sizes:
        for offset in offsets:
            for who in range(2):
                near.append(held_of[offset, who][start : start + size].reshape(-1))
        start += size
    near = jnp.concatenate(near)
    home = jnp.concatenate([held_of[0, who].reshape(-1) for who in range(2)])

    padded_spectrum = jnp.pad(spectrum, ((0, padded - slots), (0, 0), (0, 0)))

    def to_send(low, high):
        zero_takes = padded_spectrum[block_of[0][low] * ROUND :][: (high - low) * ROUND]
        one_takes = jnp.concatenate(
            [
                padded_spectrum[block * ROUND : (block + 1) * ROUND]
                for block in block_of[1][low:high]
            ]
        )
        chosen = jnp.where(lon_place == 0, one_takes, zero_takes)
        return lax.ppermute(chosen.astype(jnp.bfloat16), "lon", swap)

    terrain = jnp.stack([water_depth, sea_mask.astype(jnp.float32)])
    terrain = jnp.concatenate([terrain, lax.ppermute(terrain, "lon", swap)], axis=2)
    first_other = to_send(0, 1)
    rest_other = to_send(1, handled_blocks) if handled_blocks > 1 else None
    depth, ocean = terrain[0], terrain[1]
    face_x = 0.5 * ocean * jnp.roll(ocean, -1, axis=1)
    face_left = jnp.roll(face_x, 1, axis=1)
    face_y = 0.5 * ocean * jnp.pad(ocean[1:], ((0, 1), (0, 0)))
    fields = [value[:, None] for value in (depth, ocean, face_x, face_left, face_y)]

    own_comps = lax.dynamic_index_in_dim(comps, comp_place, 0, keepdims=False)
    held = jnp.take(own_comps, held_blocks, axis=0)
    real = held >= 0
    held = jnp.where(real, held, 0)
    held_freq = held // NDIR
    wavenumber = (2.0 * math.pi * frequency_of(held_freq)) ** 2 / 9.81
    heading = heading_of(held % NDIR)
    count = jnp.where(real, jnp.take(substeps, held_freq), 0)
    params = jnp.stack(
        [wavenumber, jnp.cos(heading), jnp.sin(heading), count.astype(jnp.float32)], axis=1
    )
    params = jnp.broadcast_to(params[..., None], params.shape + (half,))
    most = jnp.max(count, axis=1)
    both = [(i, j, i ^ 1, 1 - j) for i in range(comp_count) for j in range(2)]
    both = [(i * 2 + j, k * 2 + l) for i, j, k, l in both]

    part_rows = lat // 2
    inputs, homes = [], []
    for turn in range(handled_blocks):
        table = jnp.stack([held_blocks[turn], member]).astype(jnp.int32)
        keep, over_lon, over_pair, over_both = advance(
            table,
            most[turn : turn + 1],
            padded_spectrum,
            first_other if turn == 0 else rest_other,
            max(turn - 1, 0),
            fields,
            params[turn],
        )
        if turn < rest_blocks:
            parts = [
                keep,
                lax.ppermute(over_lon, "lon", swap),
                lax.ppermute(over_pair, "comp", pairs),
                lax.ppermute(over_both, ("comp", "lon"), both),
            ]
        else:
            parts = [keep, lax.ppermute(over_pair, "comp", pairs)]
        block = jnp.concatenate(parts, axis=1)
        inputs.append(block)
        homes.append(True)
        for distance in range(1, reach + 1):
            step = 2 * distance
            up = [(i, i + step) for i in range(comp_count - step)]
            down = [(i + step, i) for i in range(comp_count - step)]
            for route in (up, down):
                inputs.append(lax.ppermute(block, "comp", route))
                homes.append(False)

    home_safe = jnp.where(home >= 0, home, 0)
    home_heading = heading_of(home_safe % NDIR)
    home_scale = jnp.sqrt(frequency_of(home_safe // NDIR) / 0.2)
    scales = jnp.stack(
        [
            over_lanes(home_scale * jnp.cos(home_heading), half),
            over_lanes(home_scale * jnp.sin(home_heading), half),
        ]
    )
    directions = jnp.arange(NDIR, dtype=jnp.int32)
    home_dir = (home[:, None] % NDIR == directions[None]).astype(jnp.bfloat16)
    near_dir = (near[:, None] % NDIR == directions[None]).astype(jnp.bfloat16)
    gap = near[None] // NDIR - home[:, None] // NDIR
    matrix = None
    for index in range(5):
        rows = jnp.dot(home_dir, coupling[index], preferred_element_type=jnp.bfloat16)
        term = jnp.dot(rows, near_dir.T, preferred_element_type=jnp.bfloat16)
        term = jnp.where(gap == index - 2, term, jnp.zeros_like(term))
        matrix = term if matrix is None else matrix + term

    wind = lax.dynamic_slice_in_dim(wind_field, member * part_rows, part_rows, axis=1)[:, :, None]
    chunk_rows = part_rows // CHUNKS
    values = [[], []]
    for chunk in range(CHUNKS):
        kept, sent_back = sources(
            matrix, scales, wind, inputs, homes, chunk * chunk_rows, chunk_rows
        )
        values[0].append(kept)
        values[1].append(lax.ppermute(sent_back, "comp", pairs))
    out_table = jnp.concatenate([held_order, member[None]]).astype(jnp.int32)
    return finish(out_table, values[0] + values[1], lat)[:slots]


def solution(mesh):
    in_specs = (
        P(("grp", "comp"), None, "lon"),
        P(None, "lon"),
        P(None, "lon"),
        P(None, "grp", "lon"),
        P(),
        P(),
        P(),
    )
    out_specs = P(("grp", "comp"), None, "lon")
    return jax.shard_map(
        on_device, mesh=mesh, in_specs=in_specs, out_specs=out_specs, check_vma=False
    )
```

time: 129 us -> 178 us (1.38)
  waiting for transfers between devices: 17.1 us -> 40.5 us
  local copies, waits for them, and re-layouts: 9.23 us -> 16.8 us
  starting transfers between devices: 32.8 us -> 40.3 us
  other arithmetic: 2.45 us -> 9.94 us
  Pallas kernels: 56.3 us -> 61.1 us
  matrix products: 9.69 us -> 7.09 us
    ppermute x6 -> x18, waiting for transfers between devices: 10.7 us -> 31 us  [the longest x3 10.6 us: on_device(): values[1].append(lax.ppermute(sent_back, 'comp', pairs))]
    ppermute x6 -> x18, starting transfers between devices: 7.27 us -> 11.9 us  [the longest x4 6.08 us: on_device(): lax.ppermute(over_pair, 'comp', pairs)]
    pallas_call x1 -> x5, Pallas kernels: 40.8 us -> 45.4 us  [advance(): pl.pallas_call(advect_kernel, grid_spec=pltpu.PrefetchScalarGridSpec(num_...]
    unnamed x29 -> x41, local copies, waits for them, and re-layouts: 1.17 us -> 5.4 us
    another operation x2 -> x4, other arithmetic: 0.1 us -> 3.47 us  [the longest x3 3.46 us: on_device(): table = jnp.stack([held_blocks[turn], member]).astype(jnp.int32)]
    gather x1 -> x7, local copies, waits for them, and re-layouts: 0.66 us -> 3.89 us  [the longest x6 3.34 us: held_by(): jnp.take(lax.dynamic_index_in_dim(spread, index, 0, keepdims=False), held...]
    ppermute x8 -> x10, waiting for transfers between devices: 6.41 us -> 9.49 us  [on_device(): inputs.append(lax.ppermute(block, 'comp', route))]
    ppermute x8 -> x10, starting transfers between devices: 25.1 us -> 27.9 us  [on_device(): inputs.append(lax.ppermute(block, 'comp', route))]
  transfers between devices with their start and end apart: 15 -> 29, of which waited for: 4 -> 13; matrix products, arithmetic and copies ran while one was open for 13% -> 15% of each run, Pallas kernels for 8% -> 30%
where the time goes in v3:
time: 178 us; the launch traced here: 176 us
  Pallas kernels  61.1 us (34%)
  waiting for transfers between devices  40.5 us (23%)
  starting transfers between devices  40.3 us (23%)
  local copies, waits for them, and re-layouts  16.8 us (9%)
  other arithmetic  9.94 us (6%)
  matrix products  7.09 us (4%)
    pallas_call x5, Pallas kernels, advance(): pl.pallas_call(advect_kernel, grid_spec=pltpu.PrefetchScalarGridSpec(num_...  45.4 us
    ppermute x10, starting transfers between devices, on_device(): inputs.append(lax.ppermute(block, 'comp', route))  27.9 us
    pallas_call x3, Pallas kernels, sources(): pl.pallas_call(functools.partial(source_kernel, spans), grid=(rows // 2,)...  10.8 us
    ppermute x3, waiting for transfers between devices, on_device(): values[1].append(lax.ppermute(sent_back, 'comp', pairs))  10.6 us
    ppermute x4, waiting for transfers between devices, on_device(): lax.ppermute(over_both, ('comp', 'lon'), both)  9.93 us
    ppermute x10, waiting for transfers between devices, on_device(): inputs.append(lax.ppermute(block, 'comp', route))  9.49 us
    dot_general x5, matrix products, on_device(): term = jnp.dot(rows, near_dir.T, preferred_element_type=jnp.bfloat16)  7.09 us
    ppermute x4, waiting for transfers between devices, on_device(): lax.ppermute(over_pair, 'comp', pairs)  6.89 us
  transfers between devices with their start and end apart: 29, of which 13 were waited for; matrix products, arithmetic and copies ran while one was open for 15% of the time, Pallas kernels for 30%

profile of v3, /device:TPU:0, one launch (start us, length us, event | category | flops | bytes accessed | tf_op | source)
XLA Modules:
  0.0 176.5 jit_solution(9747419782285903446)
XLA Ops:
  2.0 1.3 fusion.73
  3.4 1.3 slice.263
  4.8 2.5 %fusion = bf16[64,48,128]{2,1,0:T(8,128)(2,1)} fusion(bf16[16,48,128]{2,1,0:T(8,128)(2,1)S(1)} %get-tuple-element.58, bf16[48,48,128]{2,1,0:T(8,128)(2,1)S(1)} %slice.263, f32[144,48,128]{2,1,0:T(8,128)} %mine.9, pred[]{:T(512)S(6)} %eq.72), kind=kLoop, calls=%fused_computation.14 | loop fusion | flops 786432 | bytes 2359297 | tf_op jit(solution)/shard_map/convert_element_type | solution.py:342
  12.4 1.2 gather_fusion.1
  17.2 1.3 convolution_select_fusion.3
  20.0 1.4 pad_add_fusion.5
  21.4 1.3 pad_add_fusion.3
  22.7 2.5 %fusion.3 = bf16[288,864]{1,0:T(8,128)(2,1)} fusion(bf16[288,864]{1,0:T(8,128)(2,1)S(1)} %convolution_select_fusion.1, bf16[288,864]{1,0:T(8,128)(2,1)S(1)} %convolution_select_fusion.2, bf16[288,864]{1,0:T(8,128)(2,1)} %convolution_select_fusion.3, s32[288]{0:T(512)S(1)} %get-tuple-element.112, s32[864]{0:T(1024)S(1)} %get-tuple-element.108, ...), kind=kOutput, calls=%fused_computation.22 | convolution fusion | flops 21441024 | bytes 2050048 | tf_op jit(solution)/shard_map/dot_general | solution.py:419
  26.8 2.0 %copy-done.1 = f32[144,48,128]{2,1,0:T(8,128)S(1)} copy-done((f32[144,48,128]{2,1,0:T(8,128)S(1)}, f32[144,48,128]{2,1,0:T(8,128)}, u32[]{:S(2)}) %copy-start.1) | copy-done | bytes 3538968
  28.8 8.9 %advance.5 = (bf16[24,16,128]{2,1,0:T(8,128)(2,1)S(1)}, bf16[24,16,128]{2,1,0:T(8,128)(2,1)S(1)}, bf16[24,16,128]{2,1,0:T(8,128)(2,1)S(1)}, bf16[24,16,128]{2,1,0:T(8,128)(2,1)S(1)}) custom-call(s32[2]{0:T(128)S(1)} %pad_add_fusion.2.table, s32[1]{0:T(128)} %get-tuple-element.117.steps, f32[144,48,128]{2,1,0:T(8,128)S(1)} %copy-done.1, ...), custom_call_target="tpu_custom_call" | custom-call | flops 737280000 | bytes 983040 | tf_op jit(solution)/shard_map/advance/pallas_call | solution.py:138
  37.9 3.0 %collective-permute-start.3 = (bf16[24,16,128]{2,1,0:T(8,128)(2,1)S(1)}, bf16[24,16,128]{2,1,0:T(8,128)(2,1)S(1)}, u32[]{:S(2)}, u32[]{:S(2)}) collective-permute-start(bf16[24,16,128]{2,1,0:T(8,128)(2,1)S(1)} %get-tuple-element.32), channel_id=1, source_target_pairs={{0,2},{2,0},{4,6},{6,4},{8,10},{10,8},{12,14},{14,12},{1,3},{3,1},... | collective-permute-start | bytes 294920 | tf_op jit(solution)/shard_map/ppermute | solution.py:387
  40.9 3.1 %collective-permute-done.3 = bf16[24,16,128]{2,1,0:T(8,128)(2,1)S(1)} collective-permute-done((bf16[24,16,128]{2,1,0:T(8,128)(2,1)S(1)}, bf16[24,16,128]{2,1,0:T(8,128)(2,1)S(1)}, u32[]{:S(2)}, u32[]{:S(2)}) %collective-permute-start.3) | collective-permute-done | bytes 98336 | tf_op jit(solution)/shard_map/ppermute | solution.py:387
  44.1 2.0 %collective-permute-done.4 = bf16[24,16,128]{2,1,0:T(8,128)(2,1)S(1)} collective-permute-done((bf16[24,16,128]{2,1,0:T(8,128)(2,1)S(1)}, bf16[24,16,128]{2,1,0:T(8,128)(2,1)S(1)}, u32[]{:S(2)}, u32[]{:S(2)}) %collective-permute-start.4) | collective-permute-done | bytes 98336 | tf_op jit(solution)/shard_map/ppermute | solution.py:388
  46.0 1.3 collective-permute-start.6
  47.3 4.6 %collective-permute-start.5 = (bf16[24,64,128]{2,1,0:T(8,128)(2,1)S(1)}, bf16[24,64,128]{2,1,0:T(8,128)(2,1)S(1)}, u32[]{:S(2)}, u32[]{:S(2)}) collective-permute-start(bf16[24,64,128]{2,1,0:T(8,128)(2,1)S(1)} %constant_dynamic-update-slice_fusion.refs_0_), channel_id=1, source_target_pairs={{0,4},{2,6},{4,8},{6,10},{8,12},{10,14},{1,5},{3,7},{5,9},{7,11},{... | collective-permute-start | bytes 1179656 | tf_op jit(solution)/shard_map/ppermute | solution.py:400
  52.0 8.9 %advance.8 = (bf16[24,16,128]{2,1,0:T(8,128)(2,1)S(1)}, bf16[24,16,128]{2,1,0:T(8,128)(2,1)S(1)}, bf16[24,16,128]{2,1,0:T(8,128)(2,1)S(1)}, bf16[24,16,128]{2,1,0:T(8,128)(2,1)S(1)}) custom-call(s32[2]{0:T(128)S(1)} %get-tuple-element.131.table, s32[1]{0:T(128)} %get-tuple-element.114.steps, f32[144,48,128]{2,1,0:T(8,128)S(1)} %copy-done.1, ...), custom_call_target="tpu_custom_call" | custom-call | flops 737280000 | bytes 983040 | tf_op jit(solution)/shard_map/advance/pallas_call | solution.py:138
  61.0 1.0 collective-permute-start.19
  62.9 9.0 %advance.7 = (bf16[24,16,128]{2,1,0:T(8,128)(2,1)S(1)}, bf16[24,16,128]{2,1,0:T(8,128)(2,1)S(1)}, bf16[24,16,128]{2,1,0:T(8,128)(2,1)S(1)}, bf16[24,16,128]{2,1,0:T(8,128)(2,1)S(1)}) custom-call(s32[2]{0:T(128)S(1)} %get-tuple-element.130.table, s32[1]{0:T(128)} %get-tuple-element.115.steps, f32[144,48,128]{2,1,0:T(8,128)S(1)} %copy-done.1, ...), custom_call_target="tpu_custom_call" | custom-call | flops 737280000 | bytes 983040 | tf_op jit(solution)/shard_map/advance/pallas_call | solution.py:138
  72.0 9.7 %advance.9 = (bf16[24,16,128]{2,1,0:T(8,128)(2,1)S(1)}, bf16[24,16,128]{2,1,0:T(8,128)(2,1)}, bf16[24,16,128]{2,1,0:T(8,128)(2,1)S(1)}, bf16[24,16,128]{2,1,0:T(8,128)(2,1)}) custom-call(s32[2]{0:T(128)S(1)} %get-tuple-element.132.table, s32[1]{0:T(128)} %get-tuple-element.113.steps, f32[144,48,128]{2,1,0:T(8,128)S(1)} %copy-done.1, ...), custom_call_target="tpu_custom_call" | custom-call | flops 737280000 | bytes 983040 | tf_op jit(solution)/shard_map/advance/pallas_call | solution.py:138
  81.8 8.9 %advance.6 = (bf16[24,16,128]{2,1,0:T(8,128)(2,1)S(1)}, bf16[24,16,128]{2,1,0:T(8,128)(2,1)S(1)}, bf16[24,16,128]{2,1,0:T(8,128)(2,1)S(1)}, bf16[24,16,128]{2,1,0:T(8,128)(2,1)S(1)}) custom-call(s32[2]{0:T(128)S(1)} %get-tuple-element.129.table, s32[1]{0:T(128)} %get-tuple-element.116.steps, f32[144,48,128]{2,1,0:T(8,128)S(1)} %copy-done.1, ...), custom_call_target="tpu_custom_call" | custom-call | flops 737280000 | bytes 983040 | tf_op jit(solution)/shard_map/advance/pallas_call | solution.py:138
  91.1 1.0 collective-permute-start.14
  92.3 1.3 collective-permute-done.8
  93.6 1.1 collective-permute-start.9
  94.7 3.8 %collective-permute-done.9 = bf16[24,16,128]{2,1,0:T(8,128)(2,1)S(1)} collective-permute-done((bf16[24,16,128]{2,1,0:T(8,128)(2,1)S(1)}, bf16[24,16,128]{2,1,0:T(8,128)(2,1)S(1)}, u32[]{:S(2)}, u32[]{:S(2)}) %collective-permute-start.9) | collective-permute-done | bytes 98336 | tf_op jit(solution)/shard_map/ppermute | solution.py:387
  98.4 4.7 %collective-permute-done.10 = bf16[24,16,128]{2,1,0:T(8,128)(2,1)S(1)} collective-permute-done((bf16[24,16,128]{2,1,0:T(8,128)(2,1)S(1)}, bf16[24,16,128]{2,1,0:T(8,128)(2,1)S(1)}, u32[]{:S(2)}, u32[]{:S(2)}) %collective-permute-start.10) | collective-permute-done | bytes 98336 | tf_op jit(solution)/shard_map/ppermute | solution.py:388
  103.1 1.0 collective-permute-start.23
  104.1 1.3 collective-permute-start.12
  105.4 2.3 %collective-permute-done.23 = bf16[24,16,128]{2,1,0:T(8,128)(2,1)S(1)} collective-permute-done((bf16[24,16,128]{2,1,0:T(8,128)(2,1)S(1)}, bf16[24,16,128]{2,1,0:T(8,128)(2,1)S(1)}, u32[]{:S(2)}, u32[]{:S(2)}) %collective-permute-start.23) | collective-permute-done | bytes 98336 | tf_op jit(solution)/shard_map/ppermute | solution.py:391
  107.8 1.3 collective-permute-start.25
  109.1 3.3 %collective-permute-done.15 = bf16[24,16,128]{2,1,0:T(8,128)(2,1)S(1)} collective-permute-done((bf16[24,16,128]{2,1,0:T(8,128)(2,1)S(1)}, bf16[24,16,128]{2,1,0:T(8,128)(2,1)S(1)}, u32[]{:S(2)}, u32[]{:S(2)}) %collective-permute-start.15) | collective-permute-done | bytes 98336 | tf_op jit(solution)/shard_map/ppermute | solution.py:388
  112.4 3.6 %collective-permute-start.24 = (bf16[24,32,128]{2,1,0:T(8,128)(2,1)S(1)}, bf16[24,32,128]{2,1,0:T(8,128)(2,1)S(1)}, u32[]{:S(2)}, u32[]{:S(2)}) collective-permute-start(bf16[24,32,128]{2,1,0:T(8,128)(2,1)S(1)} %constant_dynamic-update-slice_fusion.16.refs_12_), channel_id=1, source_target_pairs={{0,4},{2,6},{4,8},{6,10},{8,12},{10,14},{1,5},{3,7},{5,9},{7,11},{... | collective-permute-start | bytes 589832 | tf_op jit(solution)/shard_map/ppermute | solution.py:400
  116.0 3.1 %collective-permute-start.11 = (bf16[24,64,128]{2,1,0:T(8,128)(2,1)S(1)}, bf16[24,64,128]{2,1,0:T(8,128)(2,1)}, u32[]{:S(2)}, u32[]{:S(2)}) collective-permute-start(bf16[24,64,128]{2,1,0:T(8,128)(2,1)S(1)} %constant_dynamic-update-slice_fusion.4.refs_3_), channel_id=1, source_target_pairs={{0,4},{2,6},{4,8},{6,10},{8,12},{10,14},{1,5},{3,7},{5,9},{7,11},{... | collective-permute-start | bytes 1179656 | tf_op jit(solution)/shard_map/ppermute | solution.py:400
  119.1 1.3 collective-permute-start.17
  121.5 4.9 %collective-permute-start.16 = (bf16[24,64,128]{2,1,0:T(8,128)(2,1)S(1)}, bf16[24,64,128]{2,1,0:T(8,128)(2,1)}, u32[]{:S(2)}, u32[]{:S(2)}) collective-permute-start(bf16[24,64,128]{2,1,0:T(8,128)(2,1)S(1)} %constant_dynamic-update-slice_fusion.8.refs_6_), channel_id=1, source_target_pairs={{0,4},{2,6},{4,8},{6,10},{8,12},{10,14},{1,5},{3,7},{5,9},{7,11},{... | collective-permute-start | bytes 1179656 | tf_op jit(solution)/shard_map/ppermute | solution.py:400
  127.1 1.3 collective-permute-start.22
  128.4 5.3 %collective-permute-start.21 = (bf16[24,64,128]{2,1,0:T(8,128)(2,1)S(1)}, bf16[24,64,128]{2,1,0:T(8,128)(2,1)}, u32[]{:S(2)}, u32[]{:S(2)}) collective-permute-start(bf16[24,64,128]{2,1,0:T(8,128)(2,1)S(1)} %constant_dynamic-update-slice_fusion.12.refs_9_), channel_id=1, source_target_pairs={{0,4},{2,6},{4,8},{6,10},{8,12},{10,14},{1,5},{3,7},{5,9},{7,11},{... | collective-permute-start | bytes 1179656 | tf_op jit(solution)/shard_map/ppermute | solution.py:400
  134.1 2.3 %fusion.4.matrix = bf16[288,864]{1,0:T(8,128)(2,1)} fusion(bf16[288,864]{1,0:T(8,128)(2,1)} %fusion.3, s32[288]{0:T(512)S(1)} %get-tuple-element.112, s32[864]{0:T(1024)S(1)} %get-tuple-element.108, s32[864]{0:T(1024)S(1)} %get-tuple-element.107, s32[288]{0:T(512)S(1)} %get-tuple-element.111, bf16[5,36,36]{2,1,0:T(8,128)(2,1)S(1)} %copy-done.13), kind=kOutput, calls=%fused_computation.23 | convolution fusion | flops 20445696 | bytes 1017856 | tf_op jit(solution)/shard_map/dot_general | solution.py:419
  136.4 1.7 collective-permute-done.16.refs_7_
  138.1 1.7 collective-permute-done.22.refs_11_
  139.8 5.6 %collective-permute-done.21.refs_10_ = bf16[24,64,128]{2,1,0:T(8,128)(2,1)} collective-permute-done((bf16[24,64,128]{2,1,0:T(8,128)(2,1)S(1)}, bf16[24,64,128]{2,1,0:T(8,128)(2,1)}, u32[]{:S(2)}, u32[]{:S(2)}) %collective-permute-start.21) | collective-permute-done | bytes 393248 | tf_op jit(solution)/shard_map/ppermute | solution.py:400
  146.4 0.9 copy-done.5
  147.3 3.6 %sources.5 = (bf16[8,144,128]{2,1,0:T(8,128)(2,1)S(1)}, bf16[8,144,128]{2,1,0:T(8,128)(2,1)S(1)}) custom-call(bf16[288,864]{1,0:T(8,128)(2,1)} %fusion.4.matrix, f32[2,288,128]{2,1,0:T(8,128)S(1)} %pad_maximum_fusion.scales, f32[2,24,1,128]{3,2,1,0:T(1,128)S(1)} %bitcast.108, bf16[24,64,128]{2,1,0:T(8,128)(2,1)S(1)} %constant_dynamic-update-slice_fusion.refs_0_, ...), custom_call_target="tpu_custom_call" | custom-call | flops 4076863488 | bytes 2359296 | tf_op jit(solution)/shard_map/sources/pallas_call | solution.py:211
  151.6 3.6 %sources.4 = (bf16[8,144,128]{2,1,0:T(8,128)(2,1)S(1)}, bf16[8,144,128]{2,1,0:T(8,128)(2,1)S(1)}) custom-call(bf16[288,864]{1,0:T(8,128)(2,1)} %fusion.4.matrix, f32[2,288,128]{2,1,0:T(8,128)S(1)} %pad_maximum_fusion.scales, f32[2,24,1,128]{3,2,1,0:T(1,128)S(1)} %bitcast.109, bf16[24,64,128]{2,1,0:T(8,128)(2,1)S(1)} %constant_dynamic-update-slice_fusion.refs_0_, ...), custom_call_target="tpu_custom_call" | custom-call | flops 4076863488 | bytes 2359296 | tf_op jit(solution)/shard_map/sources/pallas_call | solution.py:211
  155.1 1.6 collective-permute-start.27
  156.7 3.6 %sources.3 = (bf16[8,144,128]{2,1,0:T(8,128)(2,1)S(1)}, bf16[8,144,128]{2,1,0:T(8,128)(2,1)S(1)}) custom-call(bf16[288,864]{1,0:T(8,128)(2,1)} %fusion.4.matrix, f32[2,288,128]{2,1,0:T(8,128)S(1)} %pad_maximum_fusion.scales, f32[2,24,1,128]{3,2,1,0:T(1,128)S(1)} %bitcast.110, bf16[24,64,128]{2,1,0:T(8,128)(2,1)S(1)} %constant_dynamic-update-slice_fusion.refs_0_, ...), custom_call_target="tpu_custom_call" | custom-call | flops 4076863488 | bytes 2359296 | tf_op jit(solution)/shard_map/sources/pallas_call | solution.py:211
  161.0 6.3 %collective-permute-done.27.refs_4_ = bf16[8,144,128]{2,1,0:T(8,128)(2,1)S(1)} collective-permute-done((bf16[8,144,128]{2,1,0:T(8,128)(2,1)S(1)}, bf16[8,144,128]{2,1,0:T(8,128)(2,1)S(1)}, u32[]{:S(2)}, u32[]{:S(2)}) %collective-permute-start.27) | collective-permute-done | bytes 294944 | tf_op jit(solution)/shard_map/ppermute | solution.py:431
  167.3 4.3 %collective-permute-done.26.refs_3_ = bf16[8,144,128]{2,1,0:T(8,128)(2,1)S(1)} collective-permute-done((bf16[8,144,128]{2,1,0:T(8,128)(2,1)S(1)}, bf16[8,144,128]{2,1,0:T(8,128)(2,1)S(1)}, u32[]{:S(2)}, u32[]{:S(2)}) %collective-permute-start.26) | collective-permute-done | bytes 294944 | tf_op jit(solution)/shard_map/ppermute | solution.py:431
  171.6 4.9 %finish.1 = f32[144,48,128]{2,1,0:T(8,128)} custom-call(s32[10]{0:T(128)S(1)} %pad_add_fusion.1.table, bf16[8,144,128]{2,1,0:T(8,128)(2,1)S(1)} %get-tuple-element.48.refs_0_, bf16[8,144,128]{2,1,0:T(8,128)(2,1)S(1)} %get-tuple-element.49.refs_1_, bf16[8,144,128]{2,1,0:T(8,128)(2,1)S(1)} %get-tuple-element.50.refs_2_, ...), custom_call_target="tpu_custom_call" | custom-call | tf_op jit(solution)/shard_map/finish/pallas_call | solution.py:247
  (172 shorter events, 20.0 us)
Async XLA Ops:
  0.0 22.7 %copy-start = (f32[2,48,128]{2,1,0:T(8,128)S(1)}, f32[2,48,128]{2,1,0:T(8,128)}, u32[]{:S(2)}) copy-start(f32[2,48,128]{2,1,0:T(8,128)} %param.15) | copy-start | bytes 147460
  0.0 7.7 %copy-start.12 = (s32[5]{0:T(128)S(1)}, s32[5]{0:T(128)}, u32[]{:S(2)}) copy-start(s32[5]{0:T(128)} %constant.197.clone) | copy-start | bytes 64
  0.0 8.6 %copy-start.10 = (s32[9,1]{0,1:T(1,128)S(1)}, s32[9,1]{0,1:T(1,128)}, u32[]{:S(2)}) copy-start(s32[9,1]{0,1:T(1,128)} %constant.204) | copy-start | bytes 112
  0.0 8.6 %copy-start.11 = (s32[9,1]{0,1:T(1,128)S(1)}, s32[9,1]{0,1:T(1,128)}, u32[]{:S(2)}) copy-start(s32[9,1]{0,1:T(1,128)} %constant.203) | copy-start | bytes 112
  0.0 7.7 %copy-start.9 = (s32[1152]{0:T(1024)S(1)}, s32[1152]{0:T(1024)}, u32[]{:S(2)}) copy-start(s32[1152]{0:T(1024)} %param.16) | copy-start | bytes 13828
  0.0 12.4 %copy-start.7 = (s32[32]{0:T(128)S(1)}, s32[32]{0:T(128)}, u32[]{:S(2)}) copy-start(s32[32]{0:T(128)} %param.17) | copy-start | bytes 388
  1.5 24.5 %collective-permute-start.1 = (f32[2,48,128]{2,1,0:T(8,128)S(1)}, f32[2,48,128]{2,1,0:T(8,128)S(1)}, u32[]{:S(2)}, u32[]{:S(2)}) collective-permute-start(f32[2,48,128]{2,1,0:T(8,128)S(1)} %pad_maximum_fusion.2), channel_id=1, source_target_pairs={{0,1},{1,0},{2,3},{3,2},{4,5},{5,4},{6,7},{7,6},{8,9},{9,8},{10,11... | collective-permute-start | bytes 147464 | tf_op jit(solution)/shard_map/ppermute | solution.py:345
  3.3 23.5 %collective-permute-start = (bf16[16,48,128]{2,1,0:T(8,128)(2,1)S(1)}, bf16[16,48,128]{2,1,0:T(8,128)(2,1)S(1)}, u32[]{:S(2)}, u32[]{:S(2)}) collective-permute-start(bf16[16,48,128]{2,1,0:T(8,128)(2,1)S(1)} %get-tuple-element.59), channel_id=1, source_target_pairs={{0,1},{1,0},{2,3},{3,2},{4,5},{5,4},{6,7},{7,6},{8,9},{9,8},{10,11... | collective-permute-start | bytes 589832 | tf_op jit(solution)/shard_map/ppermute | solution.py:342
  4.7 11.5 %copy-start.13 = (bf16[5,36,36]{2,1,0:T(8,128)(2,1)S(1)}, bf16[5,36,36]{2,1,0:T(8,128)(2,1)}, u32[]{:S(2)}) copy-start(bf16[5,36,36]{2,1,0:T(8,128)(2,1)} %param.18) | copy-start | bytes 38884
  7.2 44.7 %collective-permute-start.7 = (bf16[64,48,128]{2,1,0:T(8,128)(2,1)}, bf16[64,48,128]{2,1,0:T(8,128)(2,1)S(1)}, u32[]{:S(2)}, u32[]{:S(2)}) collective-permute-start(bf16[64,48,128]{2,1,0:T(8,128)(2,1)} %fusion), channel_id=1, source_target_pairs={{0,1},{1,0},{2,3},{3,2},{4,5},{5,4},{6,7},{7,6},{8,9},{9,8},{10,11... | collective-permute-start | bytes 2359304 | tf_op jit(solution)/shard_map/ppermute | solution.py:342
  13.6 12.4 %copy-start.8 = (f32[48,128]{1,0:T(8,128)S(1)}, f32[48,128]{1,0:T(8,128)}, u32[]{:S(2)}) copy-start(f32[48,128]{1,0:T(8,128)} %param.13) | copy-start | bytes 73732
  26.8 2.0 %copy-start.1 = (f32[144,48,128]{2,1,0:T(8,128)S(1)}, f32[144,48,128]{2,1,0:T(8,128)}, u32[]{:S(2)}) copy-start(f32[144,48,128]{2,1,0:T(8,128)} %mine.9) | copy-start | bytes 10616836
  37.8 3.1 %collective-permute-start.2 = (bf16[24,16,128]{2,1,0:T(8,128)(2,1)S(1)}, bf16[24,16,128]{2,1,0:T(8,128)(2,1)S(1)}, u32[]{:S(2)}, u32[]{:S(2)}) collective-permute-start(bf16[24,16,128]{2,1,0:T(8,128)(2,1)S(1)} %get-tuple-element.31), channel_id=1, source_target_pairs={{0,1},{1,0},{2,3},{3,2},{4,5},{5,4},{6,7},{7,6},{8,9},{9,8},{10,11... | collective-permute-start | bytes 294920 | tf_op jit(solution)/shard_map/ppermute | solution.py:386
  37.9 6.1 %collective-permute-start.3 = (bf16[24,16,128]{2,1,0:T(8,128)(2,1)S(1)}, bf16[24,16,128]{2,1,0:T(8,128)(2,1)S(1)}, u32[]{:S(2)}, u32[]{:S(2)}) collective-permute-start(bf16[24,16,128]{2,1,0:T(8,128)(2,1)S(1)} %get-tuple-element.32), channel_id=1, source_target_pairs={{0,2},{2,0},{4,6},{6,4},{8,10},{10,8},{12,14},{14,12},{1,3},{3,1},... | collective-permute-start | bytes 294920 | tf_op jit(solution)/shard_map/ppermute | solution.py:387
  40.9 5.1 %collective-permute-start.4 = (bf16[24,16,128]{2,1,0:T(8,128)(2,1)S(1)}, bf16[24,16,128]{2,1,0:T(8,128)(2,1)S(1)}, u32[]{:S(2)}, u32[]{:S(2)}) collective-permute-start(bf16[24,16,128]{2,1,0:T(8,128)(2,1)S(1)} %get-tuple-element.33), channel_id=1, source_target_pairs={{0,3},{1,2},{2,1},{3,0},{4,7},{5,6},{6,5},{7,4},{8,11},{9,10},{10,... | collective-permute-start | bytes 294920 | tf_op jit(solution)/shard_map/ppermute | solution.py:388
  46.0 70.0 %collective-permute-start.6 = (bf16[24,64,128]{2,1,0:T(8,128)(2,1)S(1)}, bf16[24,64,128]{2,1,0:T(8,128)(2,1)S(1)}, u32[]{:S(2)}, u32[]{:S(2)}) collective-permute-start(bf16[24,64,128]{2,1,0:T(8,128)(2,1)S(1)} %constant_dynamic-update-slice_fusion.refs_0_), channel_id=1, source_target_pairs={{4,0},{6,2},{8,4},{10,6},{12,8},{14,10},{5,1},{7,3},{9,5},{11,7},{... | collective-permute-start | bytes 1179656 | tf_op jit(solution)/shard_map/ppermute | solution.py:400
  47.3 71.8 %collective-permute-start.5 = (bf16[24,64,128]{2,1,0:T(8,128)(2,1)S(1)}, bf16[24,64,128]{2,1,0:T(8,128)(2,1)S(1)}, u32[]{:S(2)}, u32[]{:S(2)}) collective-permute-start(bf16[24,64,128]{2,1,0:T(8,128)(2,1)S(1)} %constant_dynamic-update-slice_fusion.refs_0_), channel_id=1, source_target_pairs={{0,4},{2,6},{4,8},{6,10},{8,12},{10,14},{1,5},{3,7},{5,9},{7,11},{... | collective-permute-start | bytes 1179656 | tf_op jit(solution)/shard_map/ppermute | solution.py:400
  60.9 29.8 %collective-permute-start.18 = (bf16[24,16,128]{2,1,0:T(8,128)(2,1)S(1)}, bf16[24,16,128]{2,1,0:T(8,128)(2,1)S(1)}, u32[]{:S(2)}, u32[]{:S(2)}) collective-permute-start(bf16[24,16,128]{2,1,0:T(8,128)(2,1)S(1)} %get-tuple-element.43), channel_id=1, source_target_pairs={{0,1},{1,0},{2,3},{3,2},{4,5},{5,4},{6,7},{7,6},{8,9},{9,8},{10,11... | collective-permute-start | bytes 294920 | tf_op jit(solution)/shard_map/ppermute | solution.py:386
  61.0 30.2 %collective-permute-start.19 = (bf16[24,16,128]{2,1,0:T(8,128)(2,1)S(1)}, bf16[24,16,128]{2,1,0:T(8,128)(2,1)S(1)}, u32[]{:S(2)}, u32[]{:S(2)}) collective-permute-start(bf16[24,16,128]{2,1,0:T(8,128)(2,1)S(1)} %get-tuple-element.44), channel_id=1, source_target_pairs={{0,2},{2,0},{4,6},{6,4},{8,10},{10,8},{12,14},{14,12},{1,3},{3,1},... | collective-permute-start | bytes 294920 | tf_op jit(solution)/shard_map/ppermute | solution.py:387
  62.0 30.2 %collective-permute-start.20 = (bf16[24,16,128]{2,1,0:T(8,128)(2,1)S(1)}, bf16[24,16,128]{2,1,0:T(8,128)(2,1)S(1)}, u32[]{:S(2)}, u32[]{:S(2)}) collective-permute-start(bf16[24,16,128]{2,1,0:T(8,128)(2,1)S(1)} %get-tuple-element.45), channel_id=1, source_target_pairs={{0,3},{1,2},{2,1},{3,0},{4,7},{5,6},{6,5},{7,4},{8,11},{9,10},{10,... | collective-permute-start | bytes 294920 | tf_op jit(solution)/shard_map/ppermute | solution.py:388
  90.7 13.4 %collective-permute-start.13 = (bf16[24,16,128]{2,1,0:T(8,128)(2,1)S(1)}, bf16[24,16,128]{2,1,0:T(8,128)(2,1)S(1)}, u32[]{:S(2)}, u32[]{:S(2)}) collective-permute-start(bf16[24,16,128]{2,1,0:T(8,128)(2,1)S(1)} %get-tuple-element.39), channel_id=1, source_target_pairs={{0,1},{1,0},{2,3},{3,2},{4,5},{5,4},{6,7},{7,6},{8,9},{9,8},{10,11... | collective-permute-start | bytes 294920 | tf_op jit(solution)/shard_map/ppermute | solution.py:386
  91.1 16.6 %collective-permute-start.14 = (bf16[24,16,128]{2,1,0:T(8,128)(2,1)S(1)}, bf16[24,16,128]{2,1,0:T(8,128)(2,1)S(1)}, u32[]{:S(2)}, u32[]{:S(2)}) collective-permute-start(bf16[24,16,128]{2,1,0:T(8,128)(2,1)S(1)} %get-tuple-element.40), channel_id=1, source_target_pairs={{0,2},{2,0},{4,6},{6,4},{8,10},{10,8},{12,14},{14,12},{1,3},{3,1},... | collective-permute-start | bytes 294920 | tf_op jit(solution)/shard_map/ppermute | solution.py:387
  92.2 1.4 collective-permute-start.8
  93.6 4.9 %collective-permute-start.9 = (bf16[24,16,128]{2,1,0:T(8,128)(2,1)S(1)}, bf16[24,16,128]{2,1,0:T(8,128)(2,1)S(1)}, u32[]{:S(2)}, u32[]{:S(2)}) collective-permute-start(bf16[24,16,128]{2,1,0:T(8,128)(2,1)S(1)} %get-tuple-element.36), channel_id=1, source_target_pairs={{0,2},{2,0},{4,6},{6,4},{8,10},{10,8},{12,14},{14,12},{1,3},{3,1},... | collective-permute-start | bytes 294920 | tf_op jit(solution)/shard_map/ppermute | solution.py:387
  98.4 4.7 %collective-permute-start.10 = (bf16[24,16,128]{2,1,0:T(8,128)(2,1)S(1)}, bf16[24,16,128]{2,1,0:T(8,128)(2,1)S(1)}, u32[]{:S(2)}, u32[]{:S(2)}) collective-permute-start(bf16[24,16,128]{2,1,0:T(8,128)(2,1)S(1)} %get-tuple-element.37), channel_id=1, source_target_pairs={{0,3},{1,2},{2,1},{3,0},{4,7},{5,6},{6,5},{7,4},{8,11},{9,10},{10,... | collective-permute-start | bytes 294920 | tf_op jit(solution)/shard_map/ppermute | solution.py:388
  103.1 4.6 %collective-permute-start.23 = (bf16[24,16,128]{2,1,0:T(8,128)(2,1)S(1)}, bf16[24,16,128]{2,1,0:T(8,128)(2,1)S(1)}, u32[]{:S(2)}, u32[]{:S(2)}) collective-permute-start(bf16[24,16,128]{2,1,0:T(8,128)(2,1)S(1)} %get-tuple-element.47), channel_id=1, source_target_pairs={{0,2},{2,0},{4,6},{6,4},{8,10},{10,8},{12,14},{14,12},{1,3},{3,1},... | collective-permute-start | bytes 294920 | tf_op jit(solution)/shard_map/ppermute | solution.py:391
  104.1 24.3 %collective-permute-start.12 = (bf16[24,64,128]{2,1,0:T(8,128)(2,1)S(1)}, bf16[24,64,128]{2,1,0:T(8,128)(2,1)S(1)}, u32[]{:S(2)}, u32[]{:S(2)}) collective-permute-start(bf16[24,64,128]{2,1,0:T(8,128)(2,1)S(1)} %constant_dynamic-update-slice_fusion.4.refs_3_), channel_id=1, source_target_pairs={{4,0},{6,2},{8,4},{10,6},{12,8},{14,10},{5,1},{7,3},{9,5},{11,7},{... | collective-permute-start | bytes 1179656 | tf_op jit(solution)/shard_map/ppermute | solution.py:400
  107.8 4.6 %collective-permute-start.15 = (bf16[24,16,128]{2,1,0:T(8,128)(2,1)S(1)}, bf16[24,16,128]{2,1,0:T(8,128)(2,1)S(1)}, u32[]{:S(2)}, u32[]{:S(2)}) collective-permute-start(bf16[24,16,128]{2,1,0:T(8,128)(2,1)S(1)} %get-tuple-element.41), channel_id=1, source_target_pairs={{0,3},{1,2},{2,1},{3,0},{4,7},{5,6},{6,5},{7,4},{8,11},{9,10},{10,... | collective-permute-start | bytes 294920 | tf_op jit(solution)/shard_map/ppermute | solution.py:388
  107.8 13.1 %collective-permute-start.25 = (bf16[24,32,128]{2,1,0:T(8,128)(2,1)S(1)}, bf16[24,32,128]{2,1,0:T(8,128)(2,1)S(1)}, u32[]{:S(2)}, u32[]{:S(2)}) collective-permute-start(bf16[24,32,128]{2,1,0:T(8,128)(2,1)S(1)} %constant_dynamic-update-slice_fusion.16.refs_12_), channel_id=1, source_target_pairs={{4,0},{6,2},{8,4},{10,6},{12,8},{14,10},{5,1},{7,3},{9,5},{11,7},{... | collective-permute-start | bytes 589832 | tf_op jit(solution)/shard_map/ppermute | solution.py:400
  112.4 14.0 %collective-permute-start.24 = (bf16[24,32,128]{2,1,0:T(8,128)(2,1)S(1)}, bf16[24,32,128]{2,1,0:T(8,128)(2,1)S(1)}, u32[]{:S(2)}, u32[]{:S(2)}) collective-permute-start(bf16[24,32,128]{2,1,0:T(8,128)(2,1)S(1)} %constant_dynamic-update-slice_fusion.16.refs_12_), channel_id=1, source_target_pairs={{0,4},{2,6},{4,8},{6,10},{8,12},{10,14},{1,5},{3,7},{5,9},{7,11},{... | collective-permute-start | bytes 589832 | tf_op jit(solution)/shard_map/ppermute | solution.py:400
  116.0 20.4 %collective-permute-start.11 = (bf16[24,64,128]{2,1,0:T(8,128)(2,1)S(1)}, bf16[24,64,128]{2,1,0:T(8,128)(2,1)}, u32[]{:S(2)}, u32[]{:S(2)}) collective-permute-start(bf16[24,64,128]{2,1,0:T(8,128)(2,1)S(1)} %constant_dynamic-update-slice_fusion.4.refs_3_), channel_id=1, source_target_pairs={{0,4},{2,6},{4,8},{6,10},{8,12},{10,14},{1,5},{3,7},{5,9},{7,11},{... | collective-permute-start | bytes 1179656 | tf_op jit(solution)/shard_map/ppermute | solution.py:400
  119.1 17.3 %collective-permute-start.17 = (bf16[24,64,128]{2,1,0:T(8,128)(2,1)S(1)}, bf16[24,64,128]{2,1,0:T(8,128)(2,1)}, u32[]{:S(2)}, u32[]{:S(2)}) collective-permute-start(bf16[24,64,128]{2,1,0:T(8,128)(2,1)S(1)} %constant_dynamic-update-slice_fusion.8.refs_6_), channel_id=1, source_target_pairs={{4,0},{6,2},{8,4},{10,6},{12,8},{14,10},{5,1},{7,3},{9,5},{11,7},{... | collective-permute-start | bytes 1179656 | tf_op jit(solution)/shard_map/ppermute | solution.py:400
  120.9 0.7 copy-start.2
  121.5 16.6 %collective-permute-start.16 = (bf16[24,64,128]{2,1,0:T(8,128)(2,1)S(1)}, bf16[24,64,128]{2,1,0:T(8,128)(2,1)}, u32[]{:S(2)}, u32[]{:S(2)}) collective-permute-start(bf16[24,64,128]{2,1,0:T(8,128)(2,1)S(1)} %constant_dynamic-update-slice_fusion.8.refs_6_), channel_id=1, source_target_pairs={{0,4},{2,6},{4,8},{6,10},{8,12},{10,14},{1,5},{3,7},{5,9},{7,11},{... | collective-permute-start | bytes 1179656 | tf_op jit(solution)/shard_map/ppermute | solution.py:400
  126.4 0.7 copy-start.4
  127.1 12.7 %collective-permute-start.22 = (bf16[24,64,128]{2,1,0:T(8,128)(2,1)S(1)}, bf16[24,64,128]{2,1,0:T(8,128)(2,1)}, u32[]{:S(2)}, u32[]{:S(2)}) collective-permute-start(bf16[24,64,128]{2,1,0:T(8,128)(2,1)S(1)} %constant_dynamic-update-slice_fusion.12.refs_9_), channel_id=1, source_target_pairs={{4,0},{6,2},{8,4},{10,6},{12,8},{14,10},{5,1},{7,3},{9,5},{11,7},{... | collective-permute-start | bytes 1179656 | tf_op jit(solution)/shard_map/ppermute | solution.py:400
  128.4 17.1 %collective-permute-start.21 = (bf16[24,64,128]{2,1,0:T(8,128)(2,1)S(1)}, bf16[24,64,128]{2,1,0:T(8,128)(2,1)}, u32[]{:S(2)}, u32[]{:S(2)}) collective-permute-start(bf16[24,64,128]{2,1,0:T(8,128)(2,1)S(1)} %constant_dynamic-update-slice_fusion.12.refs_9_), channel_id=1, source_target_pairs={{0,4},{2,6},{4,8},{6,10},{8,12},{10,14},{1,5},{3,7},{5,9},{7,11},{... | collective-permute-start | bytes 1179656 | tf_op jit(solution)/shard_map/ppermute | solution.py:400
  145.4 0.9 copy-start.3
  146.4 0.9 copy-start.5
  147.3 4.3 %copy-start.6 = (bf16[24,32,128]{2,1,0:T(8,128)(2,1)S(1)}, bf16[24,32,128]{2,1,0:T(8,128)(2,1)}, u32[]{:S(2)}) copy-start(bf16[24,32,128]{2,1,0:T(8,128)(2,1)} %copy-done.4) | copy-start | bytes 589828
  150.9 10.0 %collective-permute-start.28 = (bf16[8,144,128]{2,1,0:T(8,128)(2,1)S(1)}, bf16[8,144,128]{2,1,0:T(8,128)(2,1)S(1)}, u32[]{:S(2)}, u32[]{:S(2)}) collective-permute-start(bf16[8,144,128]{2,1,0:T(8,128)(2,1)S(1)} %get-tuple-element.53), channel_id=1, source_target_pairs={{0,2},{2,0},{4,6},{6,4},{8,10},{10,8},{12,14},{14,12},{1,3},{3,1},... | collective-permute-start | bytes 884744 | tf_op jit(solution)/shard_map/ppermute | solution.py:431
  155.1 12.1 %collective-permute-start.27 = (bf16[8,144,128]{2,1,0:T(8,128)(2,1)S(1)}, bf16[8,144,128]{2,1,0:T(8,128)(2,1)S(1)}, u32[]{:S(2)}, u32[]{:S(2)}) collective-permute-start(bf16[8,144,128]{2,1,0:T(8,128)(2,1)S(1)} %get-tuple-element.52), channel_id=1, source_target_pairs={{0,2},{2,0},{4,6},{6,4},{8,10},{10,8},{12,14},{14,12},{1,3},{3,1},... | collective-permute-start | bytes 884744 | tf_op jit(solution)/shard_map/ppermute | solution.py:431
  160.3 11.3 %collective-permute-start.26 = (bf16[8,144,128]{2,1,0:T(8,128)(2,1)S(1)}, bf16[8,144,128]{2,1,0:T(8,128)(2,1)S(1)}, u32[]{:S(2)}, u32[]{:S(2)}) collective-permute-start(bf16[8,144,128]{2,1,0:T(8,128)(2,1)S(1)} %get-tuple-element.51), channel_id=1, source_target_pairs={{0,2},{2,0},{4,6},{6,4},{8,10},{10,8},{12,14},{14,12},{1,3},{3,1},... | collective-permute-start | bytes 884744 | tf_op jit(solution)/shard_map/ppermute | solution.py:431

commit v4 on v3

--- a/solution.py
+++ b/solution.py
@@ -13,6 +13,7 @@
 ROUND = 16
 UNROLL = 16
 UNROLL_C = 4
+WORK = 400
 CHUNKS = 3
 REACH = 8
 NOWHERE = -100000
@@ -156,8 +157,8 @@
         out_shape=[shape] * 4,
         compiler_params=pltpu.CompilerParams(vmem_limit_bytes=VMEM),
         cost_estimate=pl.CostEstimate(
-            flops=60000 * ROUND * lat * half // 8,
-            bytes_accessed=10 * ROUND * lat * half,
+            flops=100 * ROUND * lat * half,
+            bytes_accessed=WORK * ROUND * lat * half,
             transcendentals=0,
         ),
         name="advance",
@@ -313,9 +314,19 @@
     for distance in range(1, reach + 1):
         offsets += [-distance, distance]
 
+
+    def picked(values, which):
+        return jnp.concatenate([values[:, block : block + 1] for block in which], axis=1)
+
+    arranged = jnp.where(
+        lon_place == 0,
+        picked(spread, [pair[0] for pair in order]),
+        picked(spread, [pair[1] for pair in order]),
+    )
+
     def held_by(offset, who):
         index = (group + offset + reach) * 2 + (member if who == 0 else 1 - member)
-        return jnp.take(lax.dynamic_index_in_dim(spread, index, 0, keepdims=False), held_order, axis=0)
+        return lax.dynamic_index_in_dim(arranged, index, 0, keepdims=False)
 
     held_of = {(offset, who): held_by(offset, who) for offset in offsets for who in range(2)}
     near = []
@@ -352,7 +363,11 @@
     fields = [value[:, None] for value in (depth, ocean, face_x, face_left, face_y)]
 
     own_comps = lax.dynamic_index_in_dim(comps, comp_place, 0, keepdims=False)
-    held = jnp.take(own_comps, held_blocks, axis=0)
+    held = jnp.where(
+        lon_place == 0,
+        picked(own_comps[None], block_of[0])[0],
+        picked(own_comps[None], block_of[1])[0],
+    )
     real = held >= 0
     held = jnp.where(real, held, 0)
     held_freq = held // NDIR
@@ -369,8 +384,14 @@
 
     part_rows = lat // 2
     inputs, homes = [], []
+    routes = 1 + 2 * reach
     for turn in range(handled_blocks):
         table = jnp.stack([held_blocks[turn], member]).astype(jnp.int32)
+        if turn >= 2:
+            first = (turn - 2) * routes
+            low = max(first - routes, 0)
+            tied = lax.optimization_barrier((table, inputs[low : first + 1]))
+            table, inputs[low : first + 1] = tied
         keep, over_lon, over_pair, over_both = advance(
             table,
             most[turn : turn + 1],
@@ -400,6 +421,7 @@
                 inputs.append(lax.ppermute(block, "comp", route))
                 homes.append(False)
 
+    near, home, inputs[-routes] = lax.optimization_barrier((near, home, inputs[-routes]))
     home_safe = jnp.where(home >= 0, home, 0)
     home_heading = heading_of(home_safe % NDIR)
     home_scale = jnp.sqrt(frequency_of(home_safe // NDIR) / 0.2)

time: 178 us -> 176 us (0.989)
  local copies, waits for them, and re-layouts: 16.8 us -> 13.9 us
  starting transfers between devices: 40.3 us -> 43.1 us
  waiting for transfers between devices: 40.5 us -> 37.9 us
  matrix products: 7.09 us -> 8.99 us
    ppermute x10, waiting for transfers between devices: 9.49 us -> 0.82 us  [on_device(): inputs.append(lax.ppermute(block, 'comp', route))]
    gather x7 -> x0, local copies, waits for them, and re-layouts: 3.89 us -> none  [the longest x6 3.34 us: held_by(): jnp.take(lax.dynamic_index_in_dim(spread, index, 0, keepdims=False), held...]
    ppermute x4, waiting for transfers between devices: 6.89 us -> 10.5 us  [on_device(): lax.ppermute(over_pair, 'comp', pairs)]
    ppermute x10, starting transfers between devices: 27.9 us -> 30.8 us  [on_device(): inputs.append(lax.ppermute(block, 'comp', route))]
    reshape x0 -> x27, local copies, waits for them, and re-layouts: none -> 2.13 us  [the longest x25 1.97 us: on_device(): near.append(held_of[offset, who][start:start + size].reshape(-1))]
    concatenate x31 -> x1, local copies, waits for them, and re-layouts: 2.06 us -> 0.09 us  [on_device(): near = jnp.concatenate(near)]
    dot_general x5, matrix products: 7.09 us -> 8.99 us  [on_device(): term = jnp.dot(rows, near_dir.T, preferred_element_type=jnp.bfloat16)]
    unnamed x41 -> x47, local copies, waits for them, and re-layouts: 5.4 us -> 5.82 us
  transfers between devices with their start and end apart: 29 -> 29, of which waited for: 13 -> 12; matrix products, arithmetic and copies ran while one was open for 15% -> 14% of each run, Pallas kernels for 30% -> 30%
where the time goes in v4:
time: 176 us; the launch traced here: 175 us
  Pallas kernels  61 us (35%)
  starting transfers between devices  43.1 us (24%)
  waiting for transfers between devices  37.9 us (22%)
  local copies, waits for them, and re-layouts  13.9 us (8%)
  other arithmetic  9.59 us (5%)
  matrix products  8.99 us (5%)
    pallas_call x5, Pallas kernels, advance(): pl.pallas_call(advect_kernel, grid_spec=pltpu.PrefetchScalarGridSpec(num_...  45.5 us
    ppermute x10, starting transfers between devices, on_device(): inputs.append(lax.ppermute(block, 'comp', route))  30.8 us
    ppermute x4, waiting for transfers between devices, on_device(): lax.ppermute(over_both, ('comp', 'lon'), both)  11.3 us
    pallas_call x3, Pallas kernels, sources(): pl.pallas_call(functools.partial(source_kernel, spans), grid=(rows // 2,)...  10.6 us
    ppermute x4, waiting for transfers between devices, on_device(): lax.ppermute(over_pair, 'comp', pairs)  10.5 us
    ppermute x3, waiting for transfers between devices, on_device(): values[1].append(lax.ppermute(sent_back, 'comp', pairs))  9.06 us
    dot_general x5, matrix products, on_device(): term = jnp.dot(rows, near_dir.T, preferred_element_type=jnp.bfloat16)  8.99 us
    ppermute x4, starting transfers between devices, on_device(): lax.ppermute(over_pair, 'comp', pairs)  6.29 us
  transfers between devices with their start and end apart: 29, of which 12 were waited for; matrix products, arithmetic and copies ran while one was open for 14% of the time, Pallas kernels for 30%

profile of v4, /device:TPU:0, one launch (start us, length us, event | category | flops | bytes accessed | tf_op | source)
XLA Modules:
  0.0 175.1 jit_solution(2112925806171841324)
XLA Ops:
  2.0 1.3 fusion.73
  3.4 1.3 slice.361
  4.8 2.5 %fusion = bf16[64,48,128]{2,1,0:T(8,128)(2,1)} fusion(bf16[16,48,128]{2,1,0:T(8,128)(2,1)S(1)} %get-tuple-element.87, bf16[48,48,128]{2,1,0:T(8,128)(2,1)S(1)} %slice.361, f32[144,48,128]{2,1,0:T(8,128)} %mine.9, pred[]{:T(512)S(6)} %eq.74), kind=kLoop, calls=%fused_computation.7 | loop fusion | flops 786432 | bytes 2359297 | tf_op jit(solution)/shard_map/convert_element_type | solution.py:353
  8.0 1.2 gather_fusion
  18.3 2.0 %copy-done.1 = f32[144,48,128]{2,1,0:T(8,128)S(1)} copy-done((f32[144,48,128]{2,1,0:T(8,128)S(1)}, f32[144,48,128]{2,1,0:T(8,128)}, u32[]{:S(2)}) %copy-start.1) | copy-done | bytes 3538968
  20.3 9.0 %advance.5 = (bf16[24,16,128]{2,1,0:T(8,128)(2,1)S(1)}, bf16[24,16,128]{2,1,0:T(8,128)(2,1)S(1)}, bf16[24,16,128]{2,1,0:T(8,128)(2,1)S(1)}, bf16[24,16,128]{2,1,0:T(8,128)(2,1)S(1)}) custom-call(s32[2]{0:T(128)S(1)} %pad_add_fusion.5.table, s32[1]{0:T(128)} %get-tuple-element.156.steps, f32[144,48,128]{2,1,0:T(8,128)S(1)} %copy-done.1, ...), custom_call_target="tpu_custom_call" | custom-call | flops 9830400 | bytes 39321600 | tf_op jit(solution)/shard_map/advance/pallas_call | solution.py:139
  29.4 3.0 %collective-permute-start.3 = (bf16[24,16,128]{2,1,0:T(8,128)(2,1)S(1)}, bf16[24,16,128]{2,1,0:T(8,128)(2,1)S(1)}, u32[]{:S(2)}, u32[]{:S(2)}) collective-permute-start(bf16[24,16,128]{2,1,0:T(8,128)(2,1)S(1)} %get-tuple-element.46), channel_id=1, source_target_pairs={{0,2},{2,0},{4,6},{6,4},{8,10},{10,8},{12,14},{14,12},{1,3},{3,1},... | collective-permute-start | bytes 294920 | tf_op jit(solution)/shard_map/ppermute | solution.py:408
  32.4 3.1 %collective-permute-done.3 = bf16[24,16,128]{2,1,0:T(8,128)(2,1)S(1)} collective-permute-done((bf16[24,16,128]{2,1,0:T(8,128)(2,1)S(1)}, bf16[24,16,128]{2,1,0:T(8,128)(2,1)S(1)}, u32[]{:S(2)}, u32[]{:S(2)}) %collective-permute-start.3) | collective-permute-done | bytes 98336 | tf_op jit(solution)/shard_map/ppermute | solution.py:408
  35.6 2.0 %collective-permute-done.4 = bf16[24,16,128]{2,1,0:T(8,128)(2,1)S(1)} collective-permute-done((bf16[24,16,128]{2,1,0:T(8,128)(2,1)S(1)}, bf16[24,16,128]{2,1,0:T(8,128)(2,1)S(1)}, u32[]{:S(2)}, u32[]{:S(2)}) %collective-permute-start.4) | collective-permute-done | bytes 98336 | tf_op jit(solution)/shard_map/ppermute | solution.py:409
  37.6 1.3 collective-permute-start.6
  38.9 4.6 %collective-permute-start.5 = (bf16[24,64,128]{2,1,0:T(8,128)(2,1)S(1)}, bf16[24,64,128]{2,1,0:T(8,128)(2,1)S(1)}, u32[]{:S(2)}, u32[]{:S(2)}) collective-permute-start(bf16[24,64,128]{2,1,0:T(8,128)(2,1)S(1)} %constant_dynamic-update-slice_fusion.refs_0_), channel_id=1, source_target_pairs={{0,4},{2,6},{4,8},{6,10},{8,12},{10,14},{1,5},{3,7},{5,9},{7,11},{... | collective-permute-start | bytes 1179656 | tf_op jit(solution)/shard_map/ppermute | solution.py:421
  43.5 9.0 %advance.7 = (bf16[24,16,128]{2,1,0:T(8,128)(2,1)S(1)}, bf16[24,16,128]{2,1,0:T(8,128)(2,1)S(1)}, bf16[24,16,128]{2,1,0:T(8,128)(2,1)S(1)}, bf16[24,16,128]{2,1,0:T(8,128)(2,1)S(1)}) custom-call(s32[2]{0:T(128)S(1)} %pad_add_fusion.4.table, s32[1]{0:T(128)} %get-tuple-element.154.steps, f32[144,48,128]{2,1,0:T(8,128)S(1)} %copy-done.1, ...), custom_call_target="tpu_custom_call" | custom-call | flops 9830400 | bytes 39321600 | tf_op jit(solution)/shard_map/advance/pallas_call | solution.py:139
  52.6 1.0 collective-permute-start.14
  53.7 8.9 %advance.6 = (bf16[24,16,128]{2,1,0:T(8,128)(2,1)S(1)}, bf16[24,16,128]{2,1,0:T(8,128)(2,1)S(1)}, bf16[24,16,128]{2,1,0:T(8,128)(2,1)S(1)}, bf16[24,16,128]{2,1,0:T(8,128)(2,1)S(1)}) custom-call(s32[2]{0:T(128)S(1)} %pad_add_fusion.6.table, s32[1]{0:T(128)} %get-tuple-element.155.steps, f32[144,48,128]{2,1,0:T(8,128)S(1)} %copy-done.1, ...), custom_call_target="tpu_custom_call" | custom-call | flops 9830400 | bytes 39321600 | tf_op jit(solution)/shard_map/advance/pallas_call | solution.py:139
  62.7 1.2 collective-permute-done.8
  63.9 1.1 collective-permute-start.9
  65.0 3.8 %collective-permute-done.9 = bf16[24,16,128]{2,1,0:T(8,128)(2,1)S(1)} collective-permute-done((bf16[24,16,128]{2,1,0:T(8,128)(2,1)S(1)}, bf16[24,16,128]{2,1,0:T(8,128)(2,1)S(1)}, u32[]{:S(2)}, u32[]{:S(2)}) %collective-permute-start.9) | collective-permute-done | bytes 98336 | tf_op jit(solution)/shard_map/ppermute | solution.py:408
  68.8 4.7 %collective-permute-done.10 = bf16[24,16,128]{2,1,0:T(8,128)(2,1)S(1)} collective-permute-done((bf16[24,16,128]{2,1,0:T(8,128)(2,1)S(1)}, bf16[24,16,128]{2,1,0:T(8,128)(2,1)S(1)}, u32[]{:S(2)}, u32[]{:S(2)}) %collective-permute-start.10) | collective-permute-done | bytes 98336 | tf_op jit(solution)/shard_map/ppermute | solution.py:409
  73.8 1.3 collective-permute-start.12
  75.2 4.6 %collective-permute-start.11 = (bf16[24,64,128]{2,1,0:T(8,128)(2,1)S(1)}, bf16[24,64,128]{2,1,0:T(8,128)(2,1)S(1)}, u32[]{:S(2)}, u32[]{:S(2)}) collective-permute-start(bf16[24,64,128]{2,1,0:T(8,128)(2,1)S(1)} %constant_dynamic-update-slice_fusion.4.refs_3_), channel_id=1, source_target_pairs={{0,4},{2,6},{4,8},{6,10},{8,12},{10,14},{1,5},{3,7},{5,9},{7,11},{... | collective-permute-start | bytes 1179656 | tf_op jit(solution)/shard_map/ppermute | solution.py:421
  79.8 1.3 collective-permute-start.18
  81.1 5.3 %collective-permute-start.17 = (bf16[24,64,128]{2,1,0:T(8,128)(2,1)S(1)}, bf16[24,64,128]{2,1,0:T(8,128)(2,1)}, u32[]{:S(2)}, u32[]{:S(2)}) collective-permute-start(bf16[24,64,128]{2,1,0:T(8,128)(2,1)S(1)} %constant_dynamic-update-slice_fusion.8.refs_6_), channel_id=1, source_target_pairs={{0,4},{2,6},{4,8},{6,10},{8,12},{10,14},{1,5},{3,7},{5,9},{7,11},{... | collective-permute-start | bytes 1179656 | tf_op jit(solution)/shard_map/ppermute | solution.py:421
  86.5 9.0 %advance.9 = (bf16[24,16,128]{2,1,0:T(8,128)(2,1)S(1)}, bf16[24,16,128]{2,1,0:T(8,128)(2,1)S(1)}, bf16[24,16,128]{2,1,0:T(8,128)(2,1)S(1)}, bf16[24,16,128]{2,1,0:T(8,128)(2,1)S(1)}) custom-call(s32[2]{0:T(128)S(1)} %pad_add_fusion.3.table, s32[1]{0:T(128)} %get-tuple-element.152.steps, f32[144,48,128]{2,1,0:T(8,128)S(1)} %copy-done.1, ...), custom_call_target="tpu_custom_call" | custom-call | flops 9830400 | bytes 39321600 | tf_op jit(solution)/shard_map/advance/pallas_call | solution.py:139
  95.6 1.3 collective-permute-done.19
  96.9 1.2 collective-permute-start.20
  98.1 3.6 %collective-permute-done.20 = bf16[24,16,128]{2,1,0:T(8,128)(2,1)S(1)} collective-permute-done((bf16[24,16,128]{2,1,0:T(8,128)(2,1)S(1)}, bf16[24,16,128]{2,1,0:T(8,128)(2,1)S(1)}, u32[]{:S(2)}, u32[]{:S(2)}) %collective-permute-start.20) | collective-permute-done | bytes 98336 | tf_op jit(solution)/shard_map/ppermute | solution.py:408
  101.9 4.7 %collective-permute-done.21 = bf16[24,16,128]{2,1,0:T(8,128)(2,1)S(1)} collective-permute-done((bf16[24,16,128]{2,1,0:T(8,128)(2,1)S(1)}, bf16[24,16,128]{2,1,0:T(8,128)(2,1)S(1)}, u32[]{:S(2)}, u32[]{:S(2)}) %collective-permute-start.21) | collective-permute-done | bytes 98336 | tf_op jit(solution)/shard_map/ppermute | solution.py:409
  106.6 1.3 collective-permute-start.23
  107.9 5.3 %collective-permute-start.22 = (bf16[24,64,128]{2,1,0:T(8,128)(2,1)S(1)}, bf16[24,64,128]{2,1,0:T(8,128)(2,1)}, u32[]{:S(2)}, u32[]{:S(2)}) collective-permute-start(bf16[24,64,128]{2,1,0:T(8,128)(2,1)S(1)} %constant_dynamic-update-slice_fusion.14.refs_9_), channel_id=1, source_target_pairs={{0,4},{2,6},{4,8},{6,10},{8,12},{10,14},{1,5},{3,7},{5,9},{7,11},{... | collective-permute-start | bytes 1179656 | tf_op jit(solution)/shard_map/ppermute | solution.py:421
  113.3 9.6 %advance.8 = (bf16[24,16,128]{2,1,0:T(8,128)(2,1)S(1)}, bf16[24,16,128]{2,1,0:T(8,128)(2,1)}, bf16[24,16,128]{2,1,0:T(8,128)(2,1)S(1)}, bf16[24,16,128]{2,1,0:T(8,128)(2,1)}) custom-call(s32[2]{0:T(128)S(1)} %pad_add_fusion.2.table, s32[1]{0:T(128)} %get-tuple-element.153.steps, f32[144,48,128]{2,1,0:T(8,128)S(1)} %copy-done.1, ...), custom_call_target="tpu_custom_call" | custom-call | flops 9830400 | bytes 39321600 | tf_op jit(solution)/shard_map/advance/pallas_call | solution.py:139
  123.9 3.7 %collective-permute-done.16 = bf16[24,16,128]{2,1,0:T(8,128)(2,1)S(1)} collective-permute-done((bf16[24,16,128]{2,1,0:T(8,128)(2,1)S(1)}, bf16[24,16,128]{2,1,0:T(8,128)(2,1)S(1)}, u32[]{:S(2)}, u32[]{:S(2)}) %collective-permute-start.16) | collective-permute-done | bytes 98336 | tf_op jit(solution)/shard_map/ppermute | solution.py:412
  127.6 1.3 collective-permute-start.25
  129.0 1.3 convolution_select_fusion.1
  130.2 1.3 convolution_select_fusion.2
  131.5 1.3 convolution_select_fusion.3
  132.8 2.8 %fusion.3 = bf16[288,864]{1,0:T(8,128)(2,1)} fusion(bf16[288,864]{1,0:T(8,128)(2,1)} %convolution_select_fusion.1, bf16[288,864]{1,0:T(8,128)(2,1)} %convolution_select_fusion.2, bf16[288,864]{1,0:T(8,128)(2,1)} %convolution_select_fusion.3, s32[288]{0:T(512)S(1)} %get-tuple-element.151, s32[864]{0:T(1024)S(1)} %get-tuple-element.145, ...), kind=kOutput, calls=%fused_computation.15 | convolution fusion | flops 21441024 | bytes 2013184 | tf_op jit(solution)/shard_map/dot_general | solution.py:441
  135.9 4.6 %collective-permute-start.24 = (bf16[24,32,128]{2,1,0:T(8,128)(2,1)S(1)}, bf16[24,32,128]{2,1,0:T(8,128)(2,1)S(1)}, u32[]{:S(2)}, u32[]{:S(2)}) collective-permute-start(bf16[24,32,128]{2,1,0:T(8,128)(2,1)S(1)} %constant_dynamic-update-slice_fusion.12.refs_12_), channel_id=1, source_target_pairs={{0,4},{2,6},{4,8},{6,10},{8,12},{10,14},{1,5},{3,7},{5,9},{7,11},{... | collective-permute-start | bytes 589832 | tf_op jit(solution)/shard_map/ppermute | solution.py:421
  140.5 2.3 %fusion.4.matrix = bf16[288,864]{1,0:T(8,128)(2,1)} fusion(bf16[288,864]{1,0:T(8,128)(2,1)} %fusion.3, s32[288]{0:T(512)S(1)} %get-tuple-element.151, s32[864]{0:T(1024)S(1)} %get-tuple-element.145, s32[864]{0:T(1024)S(1)} %get-tuple-element.144, s32[288]{0:T(512)S(1)} %get-tuple-element.150, bf16[5,36,36]{2,1,0:T(8,128)(2,1)S(1)} %copy-done.15), kind=kOutput, calls=%fused_computation.16 | convolution fusion | flops 20445696 | bytes 1017856 | tf_op jit(solution)/shard_map/dot_general | solution.py:441
  144.3 1.0 copy-done.3
  147.2 3.5 %sources.5 = (bf16[8,144,128]{2,1,0:T(8,128)(2,1)S(1)}, bf16[8,144,128]{2,1,0:T(8,128)(2,1)S(1)}) custom-call(bf16[288,864]{1,0:T(8,128)(2,1)} %fusion.4.matrix, f32[2,288,128]{2,1,0:T(8,128)S(1)} %pad_maximum_fusion.scales, f32[2,24,1,128]{3,2,1,0:T(1,128)S(1)} %bitcast.77, bf16[24,64,128]{2,1,0:T(8,128)(2,1)S(1)} %constant_dynamic-update-slice_fusion.refs_0_, ...), custom_call_target="tpu_custom_call" | custom-call | flops 4076863488 | bytes 2359296 | tf_op jit(solution)/shard_map/sources/pallas_call | solution.py:212
  150.8 1.0 collective-permute-start.28
  151.8 3.5 %sources.4 = (bf16[8,144,128]{2,1,0:T(8,128)(2,1)S(1)}, bf16[8,144,128]{2,1,0:T(8,128)(2,1)S(1)}) custom-call(bf16[288,864]{1,0:T(8,128)(2,1)} %fusion.4.matrix, f32[2,288,128]{2,1,0:T(8,128)S(1)} %pad_maximum_fusion.scales, f32[2,24,1,128]{3,2,1,0:T(1,128)S(1)} %bitcast.78, bf16[24,64,128]{2,1,0:T(8,128)(2,1)S(1)} %constant_dynamic-update-slice_fusion.refs_0_, ...), custom_call_target="tpu_custom_call" | custom-call | flops 4076863488 | bytes 2359296 | tf_op jit(solution)/shard_map/sources/pallas_call | solution.py:212
  155.4 1.2 collective-permute-start.27
  156.5 3.5 %sources.3 = (bf16[8,144,128]{2,1,0:T(8,128)(2,1)S(1)}, bf16[8,144,128]{2,1,0:T(8,128)(2,1)S(1)}) custom-call(bf16[288,864]{1,0:T(8,128)(2,1)} %fusion.4.matrix, f32[2,288,128]{2,1,0:T(8,128)S(1)} %pad_maximum_fusion.scales, f32[2,24,1,128]{3,2,1,0:T(1,128)S(1)} %bitcast.79, bf16[24,64,128]{2,1,0:T(8,128)(2,1)S(1)} %constant_dynamic-update-slice_fusion.refs_0_, ...), custom_call_target="tpu_custom_call" | custom-call | flops 4076863488 | bytes 2359296 | tf_op jit(solution)/shard_map/sources/pallas_call | solution.py:212
  160.1 1.0 collective-permute-start.26
  161.2 5.7 %collective-permute-done.27.refs_4_ = bf16[8,144,128]{2,1,0:T(8,128)(2,1)S(1)} collective-permute-done((bf16[8,144,128]{2,1,0:T(8,128)(2,1)S(1)}, bf16[8,144,128]{2,1,0:T(8,128)(2,1)S(1)}, u32[]{:S(2)}, u32[]{:S(2)}) %collective-permute-start.27) | collective-permute-done | bytes 294944 | tf_op jit(solution)/shard_map/ppermute | solution.py:453
  166.9 3.3 %collective-permute-done.26.refs_3_ = bf16[8,144,128]{2,1,0:T(8,128)(2,1)S(1)} collective-permute-done((bf16[8,144,128]{2,1,0:T(8,128)(2,1)S(1)}, bf16[8,144,128]{2,1,0:T(8,128)(2,1)S(1)}, u32[]{:S(2)}, u32[]{:S(2)}) %collective-permute-start.26) | collective-permute-done | bytes 294944 | tf_op jit(solution)/shard_map/ppermute | solution.py:453
  170.2 4.9 %finish.1 = f32[144,48,128]{2,1,0:T(8,128)} custom-call(s32[10]{0:T(128)S(1)} %pad_add_fusion.1.table, bf16[8,144,128]{2,1,0:T(8,128)(2,1)S(1)} %get-tuple-element.77.refs_0_, bf16[8,144,128]{2,1,0:T(8,128)(2,1)S(1)} %get-tuple-element.78.refs_1_, bf16[8,144,128]{2,1,0:T(8,128)(2,1)S(1)} %get-tuple-element.79.refs_2_, ...), custom_call_target="tpu_custom_call" | custom-call | tf_op jit(solution)/shard_map/finish/pallas_call | solution.py:248
  (169 shorter events, 17.8 us)
Async XLA Ops:
  0.0 14.5 %copy-start = (f32[2,48,128]{2,1,0:T(8,128)S(1)}, f32[2,48,128]{2,1,0:T(8,128)}, u32[]{:S(2)}) copy-start(f32[2,48,128]{2,1,0:T(8,128)} %param.13) | copy-start | bytes 147460
  0.0 7.7 %copy-start.12 = (s32[1152]{0:T(1024)S(1)}, s32[1152]{0:T(1024)}, u32[]{:S(2)}) copy-start(s32[1152]{0:T(1024)} %param.14) | copy-start | bytes 13828
  0.0 8.0 %copy-start.10 = (s32[32]{0:T(128)S(1)}, s32[32]{0:T(128)}, u32[]{:S(2)}) copy-start(s32[32]{0:T(128)} %param.15) | copy-start | bytes 388
  1.5 15.9 %collective-permute-start.1 = (f32[2,48,128]{2,1,0:T(8,128)S(1)}, f32[2,48,128]{2,1,0:T(8,128)S(1)}, u32[]{:S(2)}, u32[]{:S(2)}) collective-permute-start(f32[2,48,128]{2,1,0:T(8,128)S(1)} %pad_maximum_fusion.2), channel_id=1, source_target_pairs={{0,1},{1,0},{2,3},{3,2},{4,5},{5,4},{6,7},{7,6},{8,9},{9,8},{10,11... | collective-permute-start | bytes 147464 | tf_op jit(solution)/shard_map/ppermute | solution.py:356
  3.3 14.9 %collective-permute-start = (bf16[16,48,128]{2,1,0:T(8,128)(2,1)S(1)}, bf16[16,48,128]{2,1,0:T(8,128)(2,1)S(1)}, u32[]{:S(2)}, u32[]{:S(2)}) collective-permute-start(bf16[16,48,128]{2,1,0:T(8,128)(2,1)S(1)} %get-tuple-element.88), channel_id=1, source_target_pairs={{0,1},{1,0},{2,3},{3,2},{4,5},{5,4},{6,7},{7,6},{8,9},{9,8},{10,11... | collective-permute-start | bytes 589832 | tf_op jit(solution)/shard_map/ppermute | solution.py:353
  4.7 4.8 %copy-start.16 = (s32[5]{0:T(128)S(1)}, s32[5]{0:T(128)}, u32[]{:S(2)}) copy-start(s32[5]{0:T(128)} %constant.174.clone) | copy-start | bytes 64
  4.8 12.7 %copy-start.11 = (f32[48,128]{1,0:T(8,128)S(1)}, f32[48,128]{1,0:T(8,128)}, u32[]{:S(2)}) copy-start(f32[48,128]{1,0:T(8,128)} %param.11) | copy-start | bytes 73732
  7.2 36.2 %collective-permute-start.7 = (bf16[64,48,128]{2,1,0:T(8,128)(2,1)}, bf16[64,48,128]{2,1,0:T(8,128)(2,1)S(1)}, u32[]{:S(2)}, u32[]{:S(2)}) collective-permute-start(bf16[64,48,128]{2,1,0:T(8,128)(2,1)} %fusion), channel_id=1, source_target_pairs={{0,1},{1,0},{2,3},{3,2},{4,5},{5,4},{6,7},{7,6},{8,9},{9,8},{10,11... | collective-permute-start | bytes 2359304 | tf_op jit(solution)/shard_map/ppermute | solution.py:353
  18.3 2.0 %copy-start.1 = (f32[144,48,128]{2,1,0:T(8,128)S(1)}, f32[144,48,128]{2,1,0:T(8,128)}, u32[]{:S(2)}) copy-start(f32[144,48,128]{2,1,0:T(8,128)} %mine.9) | copy-start | bytes 10616836
  29.3 3.1 %collective-permute-start.2 = (bf16[24,16,128]{2,1,0:T(8,128)(2,1)S(1)}, bf16[24,16,128]{2,1,0:T(8,128)(2,1)S(1)}, u32[]{:S(2)}, u32[]{:S(2)}) collective-permute-start(bf16[24,16,128]{2,1,0:T(8,128)(2,1)S(1)} %get-tuple-element.45), channel_id=1, source_target_pairs={{0,1},{1,0},{2,3},{3,2},{4,5},{5,4},{6,7},{7,6},{8,9},{9,8},{10,11... | collective-permute-start | bytes 294920 | tf_op jit(solution)/shard_map/ppermute | solution.py:407
  29.4 6.1 %collective-permute-start.3 = (bf16[24,16,128]{2,1,0:T(8,128)(2,1)S(1)}, bf16[24,16,128]{2,1,0:T(8,128)(2,1)S(1)}, u32[]{:S(2)}, u32[]{:S(2)}) collective-permute-start(bf16[24,16,128]{2,1,0:T(8,128)(2,1)S(1)} %get-tuple-element.46), channel_id=1, source_target_pairs={{0,2},{2,0},{4,6},{6,4},{8,10},{10,8},{12,14},{14,12},{1,3},{3,1},... | collective-permute-start | bytes 294920 | tf_op jit(solution)/shard_map/ppermute | solution.py:408
  32.4 5.1 %collective-permute-start.4 = (bf16[24,16,128]{2,1,0:T(8,128)(2,1)S(1)}, bf16[24,16,128]{2,1,0:T(8,128)(2,1)S(1)}, u32[]{:S(2)}, u32[]{:S(2)}) collective-permute-start(bf16[24,16,128]{2,1,0:T(8,128)(2,1)S(1)} %get-tuple-element.47), channel_id=1, source_target_pairs={{0,3},{1,2},{2,1},{3,0},{4,7},{5,6},{6,5},{7,4},{8,11},{9,10},{10,... | collective-permute-start | bytes 294920 | tf_op jit(solution)/shard_map/ppermute | solution.py:409
  37.6 43.5 %collective-permute-start.6 = (bf16[24,64,128]{2,1,0:T(8,128)(2,1)S(1)}, bf16[24,64,128]{2,1,0:T(8,128)(2,1)S(1)}, u32[]{:S(2)}, u32[]{:S(2)}) collective-permute-start(bf16[24,64,128]{2,1,0:T(8,128)(2,1)S(1)} %constant_dynamic-update-slice_fusion.refs_0_), channel_id=1, source_target_pairs={{4,0},{6,2},{8,4},{10,6},{12,8},{14,10},{5,1},{7,3},{9,5},{11,7},{... | collective-permute-start | bytes 1179656 | tf_op jit(solution)/shard_map/ppermute | solution.py:421
  38.9 47.6 %collective-permute-start.5 = (bf16[24,64,128]{2,1,0:T(8,128)(2,1)S(1)}, bf16[24,64,128]{2,1,0:T(8,128)(2,1)S(1)}, u32[]{:S(2)}, u32[]{:S(2)}) collective-permute-start(bf16[24,64,128]{2,1,0:T(8,128)(2,1)S(1)} %constant_dynamic-update-slice_fusion.refs_0_), channel_id=1, source_target_pairs={{0,4},{2,6},{4,8},{6,10},{8,12},{10,14},{1,5},{3,7},{5,9},{7,11},{... | collective-permute-start | bytes 1179656 | tf_op jit(solution)/shard_map/ppermute | solution.py:421
  52.5 21.3 %collective-permute-start.13 = (bf16[24,16,128]{2,1,0:T(8,128)(2,1)S(1)}, bf16[24,16,128]{2,1,0:T(8,128)(2,1)S(1)}, u32[]{:S(2)}, u32[]{:S(2)}) collective-permute-start(bf16[24,16,128]{2,1,0:T(8,128)(2,1)S(1)} %get-tuple-element.56), channel_id=1, source_target_pairs={{0,1},{1,0},{2,3},{3,2},{4,5},{5,4},{6,7},{7,6},{8,9},{9,8},{10,11... | collective-permute-start | bytes 294920 | tf_op jit(solution)/shard_map/ppermute | solution.py:407
  52.6 22.6 %collective-permute-start.14 = (bf16[24,16,128]{2,1,0:T(8,128)(2,1)S(1)}, bf16[24,16,128]{2,1,0:T(8,128)(2,1)S(1)}, u32[]{:S(2)}, u32[]{:S(2)}) collective-permute-start(bf16[24,16,128]{2,1,0:T(8,128)(2,1)S(1)} %get-tuple-element.57), channel_id=1, source_target_pairs={{0,2},{2,0},{4,6},{6,4},{8,10},{10,8},{12,14},{14,12},{1,3},{3,1},... | collective-permute-start | bytes 294920 | tf_op jit(solution)/shard_map/ppermute | solution.py:408
  62.6 1.4 collective-permute-start.8
  63.9 4.9 %collective-permute-start.9 = (bf16[24,16,128]{2,1,0:T(8,128)(2,1)S(1)}, bf16[24,16,128]{2,1,0:T(8,128)(2,1)S(1)}, u32[]{:S(2)}, u32[]{:S(2)}) collective-permute-start(bf16[24,16,128]{2,1,0:T(8,128)(2,1)S(1)} %get-tuple-element.51), channel_id=1, source_target_pairs={{0,2},{2,0},{4,6},{6,4},{8,10},{10,8},{12,14},{14,12},{1,3},{3,1},... | collective-permute-start | bytes 294920 | tf_op jit(solution)/shard_map/ppermute | solution.py:408
  68.8 4.7 %collective-permute-start.10 = (bf16[24,16,128]{2,1,0:T(8,128)(2,1)S(1)}, bf16[24,16,128]{2,1,0:T(8,128)(2,1)S(1)}, u32[]{:S(2)}, u32[]{:S(2)}) collective-permute-start(bf16[24,16,128]{2,1,0:T(8,128)(2,1)S(1)} %get-tuple-element.52), channel_id=1, source_target_pairs={{0,3},{1,2},{2,1},{3,0},{4,7},{5,6},{6,5},{7,4},{8,11},{9,10},{10,... | collective-permute-start | bytes 294920 | tf_op jit(solution)/shard_map/ppermute | solution.py:409
  73.5 6.2 %collective-permute-start.15 = (bf16[24,16,128]{2,1,0:T(8,128)(2,1)S(1)}, bf16[24,16,128]{2,1,0:T(8,128)(2,1)S(1)}, u32[]{:S(2)}, u32[]{:S(2)}) collective-permute-start(bf16[24,16,128]{2,1,0:T(8,128)(2,1)S(1)} %get-tuple-element.58), channel_id=1, source_target_pairs={{0,3},{1,2},{2,1},{3,0},{4,7},{5,6},{6,5},{7,4},{8,11},{9,10},{10,... | collective-permute-start | bytes 294920 | tf_op jit(solution)/shard_map/ppermute | solution.py:409
  73.8 34.1 %collective-permute-start.12 = (bf16[24,64,128]{2,1,0:T(8,128)(2,1)S(1)}, bf16[24,64,128]{2,1,0:T(8,128)(2,1)S(1)}, u32[]{:S(2)}, u32[]{:S(2)}) collective-permute-start(bf16[24,64,128]{2,1,0:T(8,128)(2,1)S(1)} %constant_dynamic-update-slice_fusion.4.refs_3_), channel_id=1, source_target_pairs={{4,0},{6,2},{8,4},{10,6},{12,8},{14,10},{5,1},{7,3},{9,5},{11,7},{... | collective-permute-start | bytes 1179656 | tf_op jit(solution)/shard_map/ppermute | solution.py:421
  75.2 38.1 %collective-permute-start.11 = (bf16[24,64,128]{2,1,0:T(8,128)(2,1)S(1)}, bf16[24,64,128]{2,1,0:T(8,128)(2,1)S(1)}, u32[]{:S(2)}, u32[]{:S(2)}) collective-permute-start(bf16[24,64,128]{2,1,0:T(8,128)(2,1)S(1)} %constant_dynamic-update-slice_fusion.4.refs_3_), channel_id=1, source_target_pairs={{0,4},{2,6},{4,8},{6,10},{8,12},{10,14},{1,5},{3,7},{5,9},{7,11},{... | collective-permute-start | bytes 1179656 | tf_op jit(solution)/shard_map/ppermute | solution.py:421
  79.8 56.1 %collective-permute-start.18 = (bf16[24,64,128]{2,1,0:T(8,128)(2,1)S(1)}, bf16[24,64,128]{2,1,0:T(8,128)(2,1)}, u32[]{:S(2)}, u32[]{:S(2)}) collective-permute-start(bf16[24,64,128]{2,1,0:T(8,128)(2,1)S(1)} %constant_dynamic-update-slice_fusion.8.refs_6_), channel_id=1, source_target_pairs={{4,0},{6,2},{8,4},{10,6},{12,8},{14,10},{5,1},{7,3},{9,5},{11,7},{... | collective-permute-start | bytes 1179656 | tf_op jit(solution)/shard_map/ppermute | solution.py:421
  81.1 61.7 %collective-permute-start.17 = (bf16[24,64,128]{2,1,0:T(8,128)(2,1)S(1)}, bf16[24,64,128]{2,1,0:T(8,128)(2,1)}, u32[]{:S(2)}, u32[]{:S(2)}) collective-permute-start(bf16[24,64,128]{2,1,0:T(8,128)(2,1)S(1)} %constant_dynamic-update-slice_fusion.8.refs_6_), channel_id=1, source_target_pairs={{0,4},{2,6},{4,8},{6,10},{8,12},{10,14},{1,5},{3,7},{5,9},{7,11},{... | collective-permute-start | bytes 1179656 | tf_op jit(solution)/shard_map/ppermute | solution.py:421
  95.5 33.5 %copy-start.15 = (bf16[5,36,36]{2,1,0:T(8,128)(2,1)S(1)}, bf16[5,36,36]{2,1,0:T(8,128)(2,1)}, u32[]{:S(2)}) copy-start(bf16[5,36,36]{2,1,0:T(8,128)(2,1)} %param.16) | copy-start | bytes 38884
  95.5 1.4 collective-permute-start.19
  96.9 4.9 %collective-permute-start.20 = (bf16[24,16,128]{2,1,0:T(8,128)(2,1)S(1)}, bf16[24,16,128]{2,1,0:T(8,128)(2,1)S(1)}, u32[]{:S(2)}, u32[]{:S(2)}) collective-permute-start(bf16[24,16,128]{2,1,0:T(8,128)(2,1)S(1)} %get-tuple-element.74), channel_id=1, source_target_pairs={{0,2},{2,0},{4,6},{6,4},{8,10},{10,8},{12,14},{14,12},{1,3},{3,1},... | collective-permute-start | bytes 294920 | tf_op jit(solution)/shard_map/ppermute | solution.py:408
  101.7 4.9 %collective-permute-start.21 = (bf16[24,16,128]{2,1,0:T(8,128)(2,1)S(1)}, bf16[24,16,128]{2,1,0:T(8,128)(2,1)S(1)}, u32[]{:S(2)}, u32[]{:S(2)}) collective-permute-start(bf16[24,16,128]{2,1,0:T(8,128)(2,1)S(1)} %get-tuple-element.75), channel_id=1, source_target_pairs={{0,3},{1,2},{2,1},{3,0},{4,7},{5,6},{6,5},{7,4},{8,11},{9,10},{10,... | collective-permute-start | bytes 294920 | tf_op jit(solution)/shard_map/ppermute | solution.py:409
  106.6 36.2 %collective-permute-start.23 = (bf16[24,64,128]{2,1,0:T(8,128)(2,1)S(1)}, bf16[24,64,128]{2,1,0:T(8,128)(2,1)}, u32[]{:S(2)}, u32[]{:S(2)}) collective-permute-start(bf16[24,64,128]{2,1,0:T(8,128)(2,1)S(1)} %constant_dynamic-update-slice_fusion.14.refs_9_), channel_id=1, source_target_pairs={{4,0},{6,2},{8,4},{10,6},{12,8},{14,10},{5,1},{7,3},{9,5},{11,7},{... | collective-permute-start | bytes 1179656 | tf_op jit(solution)/shard_map/ppermute | solution.py:421
  107.9 19.7 %copy-start.2 = (bf16[24,64,128]{2,1,0:T(8,128)(2,1)}, bf16[24,64,128]{2,1,0:T(8,128)(2,1)S(1)}, u32[]{:S(2)}) copy-start(bf16[24,64,128]{2,1,0:T(8,128)(2,1)S(1)} %collective-permute-done.12.refs_5_) | copy-start | bytes 1179652
  107.9 34.9 %collective-permute-start.22 = (bf16[24,64,128]{2,1,0:T(8,128)(2,1)S(1)}, bf16[24,64,128]{2,1,0:T(8,128)(2,1)}, u32[]{:S(2)}, u32[]{:S(2)}) collective-permute-start(bf16[24,64,128]{2,1,0:T(8,128)(2,1)S(1)} %constant_dynamic-update-slice_fusion.14.refs_9_), channel_id=1, source_target_pairs={{0,4},{2,6},{4,8},{6,10},{8,12},{10,14},{1,5},{3,7},{5,9},{7,11},{... | collective-permute-start | bytes 1179656 | tf_op jit(solution)/shard_map/ppermute | solution.py:421
  113.2 15.7 %copy-start.4 = (bf16[24,64,128]{2,1,0:T(8,128)(2,1)}, bf16[24,64,128]{2,1,0:T(8,128)(2,1)S(1)}, u32[]{:S(2)}) copy-start(bf16[24,64,128]{2,1,0:T(8,128)(2,1)S(1)} %collective-permute-done.11.refs_4_) | copy-start | bytes 1179652
  122.9 4.6 %collective-permute-start.16 = (bf16[24,16,128]{2,1,0:T(8,128)(2,1)S(1)}, bf16[24,16,128]{2,1,0:T(8,128)(2,1)S(1)}, u32[]{:S(2)}, u32[]{:S(2)}) collective-permute-start(bf16[24,16,128]{2,1,0:T(8,128)(2,1)S(1)} %get-tuple-element.61), channel_id=1, source_target_pairs={{0,2},{2,0},{4,6},{6,4},{8,10},{10,8},{12,14},{14,12},{1,3},{3,1},... | collective-permute-start | bytes 294920 | tf_op jit(solution)/shard_map/ppermute | solution.py:412
  127.6 15.2 %collective-permute-start.25 = (bf16[24,32,128]{2,1,0:T(8,128)(2,1)S(1)}, bf16[24,32,128]{2,1,0:T(8,128)(2,1)S(1)}, u32[]{:S(2)}, u32[]{:S(2)}) collective-permute-start(bf16[24,32,128]{2,1,0:T(8,128)(2,1)S(1)} %constant_dynamic-update-slice_fusion.12.refs_12_), channel_id=1, source_target_pairs={{4,0},{6,2},{8,4},{10,6},{12,8},{14,10},{5,1},{7,3},{9,5},{11,7},{... | collective-permute-start | bytes 589832 | tf_op jit(solution)/shard_map/ppermute | solution.py:421
  135.9 7.7 %collective-permute-start.24 = (bf16[24,32,128]{2,1,0:T(8,128)(2,1)S(1)}, bf16[24,32,128]{2,1,0:T(8,128)(2,1)S(1)}, u32[]{:S(2)}, u32[]{:S(2)}) collective-permute-start(bf16[24,32,128]{2,1,0:T(8,128)(2,1)S(1)} %constant_dynamic-update-slice_fusion.12.refs_12_), channel_id=1, source_target_pairs={{0,4},{2,6},{4,8},{6,10},{8,12},{10,14},{1,5},{3,7},{5,9},{7,11},{... | collective-permute-start | bytes 589832 | tf_op jit(solution)/shard_map/ppermute | solution.py:421
  143.6 0.7 copy-start.7
  144.3 1.0 copy-start.3
  145.3 1.0 copy-start.5
  146.3 0.9 copy-start.8
  150.8 5.7 %copy-start.6 = (bf16[24,64,128]{2,1,0:T(8,128)(2,1)S(1)}, bf16[24,64,128]{2,1,0:T(8,128)(2,1)}, u32[]{:S(2)}) copy-start(bf16[24,64,128]{2,1,0:T(8,128)(2,1)} %copy-done.4) | copy-start | bytes 1179652
  150.8 5.7 %copy-start.9 = (bf16[24,32,128]{2,1,0:T(8,128)(2,1)S(1)}, bf16[24,32,128]{2,1,0:T(8,128)(2,1)}, u32[]{:S(2)}) copy-start(bf16[24,32,128]{2,1,0:T(8,128)(2,1)} %copy-done.7) | copy-start | bytes 589828
  150.8 10.4 %collective-permute-start.28 = (bf16[8,144,128]{2,1,0:T(8,128)(2,1)S(1)}, bf16[8,144,128]{2,1,0:T(8,128)(2,1)S(1)}, u32[]{:S(2)}, u32[]{:S(2)}) collective-permute-start(bf16[8,144,128]{2,1,0:T(8,128)(2,1)S(1)} %get-tuple-element.82), channel_id=1, source_target_pairs={{0,2},{2,0},{4,6},{6,4},{8,10},{10,8},{12,14},{14,12},{1,3},{3,1},... | collective-permute-start | bytes 884744 | tf_op jit(solution)/shard_map/ppermute | solution.py:453
  155.3 5.7 %copy-start.13 = (s32[9,1]{0,1:T(1,128)S(1)}, s32[9,1]{0,1:T(1,128)}, u32[]{:S(2)}) copy-start(s32[9,1]{0,1:T(1,128)} %constant.181) | copy-start | bytes 112
  155.4 5.7 %copy-start.14 = (s32[9,1]{0,1:T(1,128)S(1)}, s32[9,1]{0,1:T(1,128)}, u32[]{:S(2)}) copy-start(s32[9,1]{0,1:T(1,128)} %constant.180) | copy-start | bytes 112
  155.4 11.5 %collective-permute-start.27 = (bf16[8,144,128]{2,1,0:T(8,128)(2,1)S(1)}, bf16[8,144,128]{2,1,0:T(8,128)(2,1)S(1)}, u32[]{:S(2)}, u32[]{:S(2)}) collective-permute-start(bf16[8,144,128]{2,1,0:T(8,128)(2,1)S(1)} %get-tuple-element.81), channel_id=1, source_target_pairs={{0,2},{2,0},{4,6},{6,4},{8,10},{10,8},{12,14},{14,12},{1,3},{3,1},... | collective-permute-start | bytes 884744 | tf_op jit(solution)/shard_map/ppermute | solution.py:453
  160.1 10.2 %collective-permute-start.26 = (bf16[8,144,128]{2,1,0:T(8,128)(2,1)S(1)}, bf16[8,144,128]{2,1,0:T(8,128)(2,1)S(1)}, u32[]{:S(2)}, u32[]{:S(2)}) collective-permute-start(bf16[8,144,128]{2,1,0:T(8,128)(2,1)S(1)} %get-tuple-element.80), channel_id=1, source_target_pairs={{0,2},{2,0},{4,6},{6,4},{8,10},{10,8},{12,14},{14,12},{1,3},{3,1},... | collective-permute-start | bytes 884744 | tf_op jit(solution)/shard_map/ppermute | solution.py:453
